TPU v7x, 32 devices: a whole 2x2x4 slice. The times are simulated.
32 devices in a mesh: dp: 8 (over y, x, core), head: 4 (over z).
Axes of the slice: x: 2, y: 2, z: 4, core: 2. Of those that a mesh axis runs over, the one named last changes fastest.
Arguments:
- hidden_in: bfloat16 [12288, 768], P('dp'), may hold values from -6 to 6
- seq_lengths: int32 [24], P('dp'), may hold values from 64 to 512, as said below
- layer_map: int32 [2], replicated, may hold values from 0 to 3, as said below
- teacher_states: bfloat16 [4, 12288, 768], P(None, 'dp', 'head'), may hold values from -6 to 6
- out_cotangent: bfloat16 [12288, 768], P('dp'), may hold values from -6 to 6
- query_weight: bfloat16 [2, 768, 768], P(None, None, 'head'), may hold values from -0.21875 to 0.21875
- key_weight: bfloat16 [2, 768, 768], P(None, None, 'head'), may hold values from -0.21875 to 0.21875
- value_weight: bfloat16 [2, 768, 768], P(None, None, 'head'), may hold values from -0.21875 to 0.21875
- query_value_bias: float32 [2, 2, 768], P(None, None, 'head'), may hold values from -0.3 to 0.3
- output_weight: bfloat16 [2, 768, 768], P(None, 'head'), may hold values from -2.5 to 2.5
- branch_bias: float32 [2, 2, 768], replicated, may hold values from -0.15 to 0.15
- norm_gain: float32 [2, 2, 768], replicated, may hold values from 0.5 to 1.5
- norm_shift: float32 [2, 2, 768], replicated, may hold values from -0.15 to 0.15
- inner_weight: bfloat16 [2, 768, 3072], P(None, None, 'head'), may hold values from -0.21875 to 0.21875
- inner_bias: float32 [2, 3072], P(None, 'head'), may hold values from -3 to 3
- outer_weight: bfloat16 [2, 3072, 768], P(None, 'head'), may hold values from -0.21875 to 0.21875
- head_alpha: float32 [2, 12], P(None, 'head'), may hold values from -3 to 3
- head_noise: float32 [2, 12], P(None, 'head'), may hold values from -1.5 to 1.5
- unit_alpha: float32 [2, 3072], P(None, 'head'), may hold values from -3 to 3
- unit_noise: float32 [2, 3072], P(None, 'head'), may hold values from -1.5 to 1.5
- map_weight: bfloat16 [768, 768], P(None, 'head'), may hold values from -0.21875 to 0.21875
Outputs:
- block_out: bfloat16 [12288, 768], P('dp')
- grad_hidden: float32 [12288, 768], P('dp')
- distill_loss: float32 [], replicated
- grad_query: float32 [2, 768, 768], P(None, 'dp', 'head')
- grad_key: float32 [2, 768, 768], P(None, 'dp', 'head')
- grad_value: float32 [2, 768, 768], P(None, 'dp', 'head')
- grad_query_value_bias: float32 [2, 2, 768], P(None, None, ('head', 'dp'))
- grad_output: float32 [2, 768, 768], P(None, 'head', 'dp')
- grad_branch_bias: float32 [2, 2, 768], P(None, None, 'dp')
- grad_norm_gain: float32 [2, 2, 768], P(None, None, 'dp')
- grad_norm_shift: float32 [2, 2, 768], P(None, None, 'dp')
- grad_inner: float32 [2, 768, 3072], P(None, 'dp', 'head')
- grad_inner_bias: float32 [2, 3072], P(None, ('head', 'dp'))
- grad_outer: float32 [2, 3072, 768], P(None, 'head', 'dp')
- grad_head_alpha: float32 [2, 12], P(None, 'head')
- grad_unit_alpha: float32 [2, 3072], P(None, ('head', 'dp'))
- grad_map: float32 [768, 768], P('dp', 'head')
Inputs may be any that keep to these rules, and one draw needn't show every extreme that they name: Each sequence uses its first seq_lengths slots; some sequence uses all 512, some only 64. `layer_map`: the last student layer matches teacher layer 3; the entries differ.
All inputs are finite; a program needn't handle non-finite values.
Results may differ from a plain program's by a relative error of at most 0.03.
Values may be sent and summed in bfloat16 or wider, within the bound.
A program may use at most 256 MiB of HBM per device.

v0:
```python
from functools import partial

import jax
import jax.numpy as jnp
from jax import lax
from jax.sharding import PartitionSpec as P

BETA = 2.0 / 3.0
EPS = 1e-05


def layer_norm(before, gain, shift):
    center = before - jnp.mean(before, -1, keepdims=True)
    spread = jnp.mean(center * center, -1, keepdims=True)
    return center * lax.rsqrt(spread + EPS) * gain + shift


def gate_open(noise, alpha):
    return jnp.clip(jax.nn.sigmoid((noise + alpha) / BETA) * 1.2 - 0.1, 0.0, 1.0)


def unit_piece(noise, unit_in, alpha):
    return jax.nn.gelu(unit_in) * gate_open(noise, alpha)


def matmul(left, right):
    return jnp.dot(left, right, preferred_element_type=jnp.float32)


def inner_rows(left, right):
    return lax.dot_general(
        left, right, (((0,), (0,)), ((), ())), preferred_element_type=jnp.float32
    )


def times_t(left, right):
    return lax.dot_general(
        left, right, (((1,), (1,)), ((), ())), preferred_element_type=jnp.float32
    )


def attention_scores(query_four, key_four, usable):
    scores = (
        jnp.einsum("sqhd,skhd->shqk", query_four, key_four, preferred_element_type=jnp.float32)
        * 0.125
    )
    return jnp.where(usable[:, None, None, :], scores, -1e30)


def add_norm(branch_part, resid, bias, gain, shift):
    total = lax.psum(branch_part.astype(jnp.bfloat16), "head").astype(jnp.float32)
    before = resid + total + bias
    return (before, layer_norm(before, gain, shift))


def head_total(grad_part):
    return lax.psum(grad_part.astype(jnp.bfloat16), "head").astype(jnp.float32)


def on_device(
    hidden_in,
    seq_lengths,
    layer_map,
    teacher_states,
    out_cotangent,
    query_weight,
    key_weight,
    value_weight,
    query_value_bias,
    output_weight,
    branch_bias,
    norm_gain,
    norm_shift,
    inner_weight,
    inner_bias,
    outer_weight,
    head_alpha,
    head_noise,
    unit_alpha,
    unit_noise,
    map_weight,
):
    tokens_dev = hidden_in.shape[0]
    model_width = hidden_in.shape[1]
    seqs_dev = seq_lengths.shape[0]
    seq_len = tokens_dev // seqs_dev
    width = query_weight.shape[2]
    heads_dev = head_alpha.shape[1]
    head_size = width // heads_dev
    layers = query_weight.shape[0]
    shape_four = (seqs_dev, seq_len, heads_dev, head_size)
    usable = jnp.arange(seq_len)[None, :] < seq_lengths[:, None]
    row_ok = usable.reshape(tokens_dev, 1).astype(jnp.float32)
    count_local = jnp.sum(seq_lengths).astype(jnp.float32)
    count_all = lax.psum(count_local, "dp")
    current = hidden_in.astype(jnp.float32)
    rounded = hidden_in
    records = []
    outputs_low = []
    misses = []
    error_local = jnp.zeros((), jnp.float32)
    for layer in range(layers):
        query_rows = (matmul(rounded, query_weight[layer]) + query_value_bias[layer, 0]).astype(
            jnp.bfloat16
        )
        key_rows = matmul(rounded, key_weight[layer]).astype(jnp.bfloat16)
        value_rows = (matmul(rounded, value_weight[layer]) + query_value_bias[layer, 1]).astype(
            jnp.bfloat16
        )
        scores = attention_scores(
            query_rows.reshape(shape_four), key_rows.reshape(shape_four), usable
        )
        largest = jnp.max(scores, -1, keepdims=True)
        powers = jnp.exp(scores - largest)
        totals = jnp.sum(powers, -1, keepdims=True)
        log_total = largest + jnp.log(totals)
        chances_low = (powers / totals).astype(jnp.bfloat16)
        context = jnp.einsum(
            "shqk,skhd->sqhd",
            chances_low,
            value_rows.reshape(shape_four),
            preferred_element_type=jnp.float32,
        ).reshape(tokens_dev, heads_dev, head_size)
        opened_head = gate_open(head_noise[layer], head_alpha[layer])
        gated = (
            (context * opened_head[None, :, None]).reshape(tokens_dev, width).astype(jnp.bfloat16)
        )
        before_one, middle = add_norm(
            matmul(gated, output_weight[layer]),
            current,
            branch_bias[layer, 0],
            norm_gain[layer, 0],
            norm_shift[layer, 0],
        )
        middle_low = middle.astype(jnp.bfloat16)
        unit_in = matmul(middle_low, inner_weight[layer]) + inner_bias[layer]
        active = unit_piece(unit_noise[layer], unit_in, unit_alpha[layer]).astype(jnp.bfloat16)
        before_two, current = add_norm(
            matmul(active, outer_weight[layer]),
            middle,
            branch_bias[layer, 1],
            norm_gain[layer, 1],
            norm_shift[layer, 1],
        )
        records.append(
            (
                rounded,
                query_rows,
                key_rows,
                value_rows,
                log_total,
                context,
                opened_head,
                gated,
                before_one,
                middle_low,
                unit_in,
                active,
                before_two,
            )
        )
        rounded = current.astype(jnp.bfloat16)
        target = jnp.take(teacher_states, layer_map[layer], axis=0).astype(jnp.float32)
        miss = (matmul(rounded, map_weight) - target) * row_ok
        error_local = error_local + jnp.sum(miss * miss)
        outputs_low.append(rounded)
        misses.append(miss)
    error_all = lax.psum(error_local, ("dp", "head"))
    distill_loss = error_all / (count_all * model_width * layers)
    factor = tokens_dev * lax.axis_size("dp") / count_all
    grad_map = jnp.zeros((model_width, width), jnp.float32)
    spread_back = []
    for layer in range(layers):
        grad_mapped = (factor * misses[layer]).astype(jnp.bfloat16)
        grad_map = grad_map + inner_rows(outputs_low[layer], grad_mapped)
        spread_back.append(times_t(grad_mapped, map_weight))
    grad_out = out_cotangent.astype(jnp.float32) + head_total(spread_back[layers - 1])
    layer_results = [None] * layers
    head_results = [None] * layers
    for layer in reversed(range(layers)):
        (
            rounded_in,
            query_rows,
            key_rows,
            value_rows,
            log_total,
            context,
            opened_head,
            gated,
            before_one,
            middle_low,
            unit_in,
            active,
            before_two,
        ) = records[layer]
        norm_out, norm_back = jax.vjp(
            layer_norm, before_two, norm_gain[layer, 1], norm_shift[layer, 1]
        )
        grad_before_two, grad_gain_two, grad_shift_two = norm_back(grad_out)
        grad_feed = grad_before_two.astype(jnp.bfloat16)
        grad_outer = inner_rows(active, grad_feed)
        grad_active = times_t(grad_feed, outer_weight[layer])
        unit_out, unit_back = jax.vjp(
            partial(unit_piece, unit_noise[layer]), unit_in, unit_alpha[layer]
        )
        grad_unit, grad_unit_alpha = unit_back(grad_active)
        grad_unit_low = grad_unit.astype(jnp.bfloat16)
        grad_inner = inner_rows(middle_low, grad_unit_low)
        grad_inner_bias = jnp.sum(grad_unit_low.astype(jnp.float32), 0)
        grad_middle = grad_before_two + head_total(times_t(grad_unit_low, inner_weight[layer]))
        first_out, first_back = jax.vjp(
            layer_norm, before_one, norm_gain[layer, 0], norm_shift[layer, 0]
        )
        grad_before_one, grad_gain_one, grad_shift_one = first_back(grad_middle)
        grad_attn = grad_before_one.astype(jnp.bfloat16)
        grad_output = inner_rows(gated, grad_attn)
        grad_gated = times_t(grad_attn, output_weight[layer]).reshape(
            tokens_dev, heads_dev, head_size
        )
        open_out, open_back = jax.vjp(partial(gate_open, head_noise[layer]), head_alpha[layer])
        (grad_head_alpha,) = open_back(jnp.sum(grad_gated * context, axis=(0, 2)))
        grad_context = (
            (grad_gated * opened_head[None, :, None]).astype(jnp.bfloat16).reshape(shape_four)
        )
        query_four = query_rows.reshape(shape_four)
        key_four = key_rows.reshape(shape_four)
        value_four = value_rows.reshape(shape_four)
        scores = attention_scores(query_four, key_four, usable)
        chances = jnp.exp(scores - log_total)
        grad_chances = jnp.einsum(
            "sqhd,skhd->shqk", grad_context, value_four, preferred_element_type=jnp.float32
        )
        grad_scores = (
            chances * (grad_chances - jnp.sum(chances * grad_chances, -1, keepdims=True))
        ).astype(jnp.bfloat16)
        grad_query_rows = (
            (
                jnp.einsum(
                    "shqk,skhd->sqhd", grad_scores, key_four, preferred_element_type=jnp.float32
                )
                * 0.125
            )
            .astype(jnp.bfloat16)
            .reshape(tokens_dev, width)
        )
        grad_key_rows = (
            (
                jnp.einsum(
                    "shqk,sqhd->skhd", grad_scores, query_four, preferred_element_type=jnp.float32
                )
                * 0.125
            )
            .astype(jnp.bfloat16)
            .reshape(tokens_dev, width)
        )
        grad_value_rows = (
            jnp.einsum(
                "shqk,sqhd->skhd",
                chances.astype(jnp.bfloat16),
                grad_context,
                preferred_element_type=jnp.float32,
            )
            .astype(jnp.bfloat16)
            .reshape(tokens_dev, width)
        )
        input_part = (
            times_t(grad_query_rows, query_weight[layer])
            + times_t(grad_key_rows, key_weight[layer])
            + times_t(grad_value_rows, value_weight[layer])
        )
        if layer > 0:
            input_part = input_part + spread_back[layer - 1]
        grad_out = grad_before_one + head_total(input_part)
        grad_query = inner_rows(rounded_in, grad_query_rows)
        grad_key = inner_rows(rounded_in, grad_key_rows)
        grad_value = inner_rows(rounded_in, grad_value_rows)
        grad_qv_bias = jnp.stack(
            [
                jnp.sum(grad_query_rows.astype(jnp.float32), 0),
                jnp.sum(grad_value_rows.astype(jnp.float32), 0),
            ]
        )
        grad_branch_bias = jnp.stack([jnp.sum(grad_before_one, 0), jnp.sum(grad_before_two, 0)])
        grad_norm_gain = jnp.stack([grad_gain_one, grad_gain_two])
        grad_norm_shift = jnp.stack([grad_shift_one, grad_shift_two])
        layer_results[layer] = (
            lax.psum_scatter(
                grad_query.astype(jnp.bfloat16), "dp", scatter_dimension=0, tiled=True
            ).astype(jnp.float32),
            lax.psum_scatter(
                grad_key.astype(jnp.bfloat16), "dp", scatter_dimension=0, tiled=True
            ).astype(jnp.float32),
            lax.psum_scatter(
                grad_value.astype(jnp.bfloat16), "dp", scatter_dimension=0, tiled=True
            ).astype(jnp.float32),
            lax.psum_scatter(
                grad_qv_bias.astype(jnp.bfloat16), "dp", scatter_dimension=1, tiled=True
            ).astype(jnp.float32),
            lax.psum_scatter(
                grad_output.astype(jnp.bfloat16), "dp", scatter_dimension=1, tiled=True
            ).astype(jnp.float32),
            lax.psum_scatter(
                grad_branch_bias.astype(jnp.bfloat16), "dp", scatter_dimension=1, tiled=True
            ).astype(jnp.float32),
            lax.psum_scatter(
                grad_norm_gain.astype(jnp.bfloat16), "dp", scatter_dimension=1, tiled=True
            ).astype(jnp.float32),
            lax.psum_scatter(
                grad_norm_shift.astype(jnp.bfloat16), "dp", scatter_dimension=1, tiled=True
            ).astype(jnp.float32),
            lax.psum_scatter(
                grad_inner.astype(jnp.bfloat16), "dp", scatter_dimension=0, tiled=True
            ).astype(jnp.float32),
            lax.psum_scatter(
                grad_inner_bias.astype(jnp.bfloat16), "dp", scatter_dimension=0, tiled=True
            ).astype(jnp.float32),
            lax.psum_scatter(
                grad_outer.astype(jnp.bfloat16), "dp", scatter_dimension=1, tiled=True
            ).astype(jnp.float32),
            lax.psum_scatter(
                grad_unit_alpha.astype(jnp.bfloat16), "dp", scatter_dimension=0, tiled=True
            ).astype(jnp.float32),
        )
        head_results[layer] = grad_head_alpha
    head_summed = lax.psum(jnp.stack(head_results), "dp")
    map_summed = lax.psum_scatter(
        grad_map.astype(jnp.bfloat16), "dp", scatter_dimension=0, tiled=True
    ).astype(jnp.float32)
    stacked = [
        jnp.stack([layer_results[layer][member] for layer in range(layers)]) for member in range(12)
    ]
    return (
        current.astype(jnp.bfloat16),
        grad_out,
        distill_loss,
        stacked[0],
        stacked[1],
        stacked[2],
        stacked[3],
        stacked[4],
        stacked[5],
        stacked[6],
        stacked[7],
        stacked[8],
        stacked[9],
        stacked[10],
        head_summed,
        stacked[11],
        map_summed,
    )


def solution(mesh):
    in_specs = (
        P("dp", None),
        P("dp"),
        P(),
        P(None, "dp", "head"),
        P("dp", None),
        P(None, None, "head"),
        P(None, None, "head"),
        P(None, None, "head"),
        P(None, None, "head"),
        P(None, "head", None),
        P(),
        P(),
        P(),
        P(None, None, "head"),
        P(None, "head"),
        P(None, "head", None),
        P(None, "head"),
        P(None, "head"),
        P(None, "head"),
        P(None, "head"),
        P(None, "head"),
    )
    out_specs = (
        P("dp", None),
        P("dp", None),
        P(),
        P(None, "dp", "head"),
        P(None, "dp", "head"),
        P(None, "dp", "head"),
        P(None, None, ("head", "dp")),
        P(None, "head", "dp"),
        P(None, None, "dp"),
        P(None, None, "dp"),
        P(None, None, "dp"),
        P(None, "dp", "head"),
        P(None, ("head", "dp")),
        P(None, "head", "dp"),
        P(None, "head"),
        P(None, ("head", "dp")),
        P("dp", "head"),
    )
    return jax.shard_map(
        on_device, mesh=mesh, in_specs=in_specs, out_specs=out_specs, check_vma=False
    )
```

profile of v0, /device:TPU:0, one launch (start us, length us, event | category | flops | bytes accessed | tf_op | source)
XLA Modules:
  0.0 1782.1 jit_solution(3074413963925384887)
XLA Ops:
  42.5 95.1 %all-reduce.17.cloned.1.call-done = bf16[1536,768]{1,0:T(8,128)(2,1)} async-done(((bf16[1536,768]{1,0:T(8,128)(2,1)}), bf16[1536,768]{1,0:T(8,128)(2,1)}) %all-reduce.17.cloned.1.call-update) | async-done | bytes 2359312 | tf_op jit(solution)/shard_map/psum | solution.py:51
  146.7 4.4 convolution_convert_fusion.5
  151.4 94.6 %all-reduce.19.cloned.1.call-done = bf16[1536,768]{1,0:T(8,128)(2,1)} async-done(((bf16[1536,768]{1,0:T(8,128)(2,1)}), bf16[1536,768]{1,0:T(8,128)(2,1)}) %all-reduce.19.cloned.1.call-update) | async-done | bytes 2359312 | tf_op jit(solution)/shard_map/psum | solution.py:51
  276.5 93.9 %all-reduce.21.cloned.1.call-done = bf16[1536,768]{1,0:T(8,128)(2,1)} async-done(((bf16[1536,768]{1,0:T(8,128)(2,1)}), bf16[1536,768]{1,0:T(8,128)(2,1)}) %all-reduce.21.cloned.1.call-update) | async-done | bytes 2359312 | tf_op jit(solution)/shard_map/psum | solution.py:51
  382.2 4.4 convolution_convert_fusion.3
  388.0 14.5 psum.88
  405.7 75.7 %all-reduce.23.cloned.1.call-done = bf16[1536,768]{1,0:T(8,128)(2,1)} async-done(((bf16[1536,768]{1,0:T(8,128)(2,1)}), bf16[1536,768]{1,0:T(8,128)(2,1)}) %all-reduce.23.cloned.1.call-update) | async-done | bytes 2359312 | tf_op jit(solution)/shard_map/psum | solution.py:51
  494.5 94.3 %all-reduce.25.cloned.1.call-done = bf16[1536,768]{1,0:T(8,128)(2,1)} async-done(((bf16[1536,768]{1,0:T(8,128)(2,1)}), bf16[1536,768]{1,0:T(8,128)(2,1)}) %all-reduce.25.cloned.1.call-update) | async-done | bytes 2359312 | tf_op jit(solution)/shard_map/psum | solution.py:57
  588.9 5.1 multiply_reduce_fusion.4
  615.3 4.7 multiply_reduce_fusion.19
  620.0 86.2 %all-reduce.27.cloned.1.call-done = bf16[1536,768]{1,0:T(8,128)(2,1)} async-done(((bf16[1536,768]{1,0:T(8,128)(2,1)}), bf16[1536,768]{1,0:T(8,128)(2,1)}) %all-reduce.27.cloned.1.call-update) | async-done | bytes 2359312 | tf_op jit(solution)/shard_map/psum | solution.py:57
  706.2 6.5 multiply_reduce_fusion.5
  712.8 5.2 fusion.202
  742.5 94.8 %all-reduce.29.cloned.1.call-done = bf16[1536,768]{1,0:T(8,128)(2,1)} async-done(((bf16[1536,768]{1,0:T(8,128)(2,1)}), bf16[1536,768]{1,0:T(8,128)(2,1)}) %all-reduce.29.cloned.1.call-update) | async-done | bytes 2359312 | tf_op jit(solution)/shard_map/psum | solution.py:57
  837.3 6.9 multiply_reduce_fusion.6
  844.3 5.2 fusion.201
  853.5 4.3 fusion.196
  887.9 7.8 convolution_convert_fusion.9
  895.8 7.9 convolution_convert_fusion.10
  904.2 4.7 convolution_convert_fusion.11
  920.2 37.3 %all-reduce.31.cloned.1.call-done = bf16[1536,768]{1,0:T(8,128)(2,1)} async-done(((bf16[1536,768]{1,0:T(8,128)(2,1)}), bf16[1536,768]{1,0:T(8,128)(2,1)}) %all-reduce.31.cloned.1.call-update) | async-done | bytes 2359312 | tf_op jit(solution)/shard_map/psum | solution.py:57
  957.5 7.2 multiply_reduce_fusion.7
  964.8 6.6 fusion.200
  972.9 4.5 multiply_reduce_fusion.17
  978.4 7.1 fusion.212
  985.5 6.2 multiply_reduce_fusion
  994.7 7.7 multiply_convert_fusion
  1035.7 6.0 add_convert_fusion
  1045.6 39.4 %psum.94 = f32[]{:T(128)} all-reduce(f32[]{:T(128)S(6)} %add.493), channel_id=1, replica_groups=mesh['dp'=8,'head'=4] {'dp','head'}, use_global_device_ids=true, to_apply=%region_35.38 | all-reduce | flops 1 | bytes 8 | tf_op jit(solution)/shard_map/psum | solution.py:168
  1089.0 15.7 reduce-scatter.74.cloned.1.call-done
  1105.6 36.0 %reduce-scatter.70.cloned.1.call-done = bf16[96,192]{1,0:T(8,128)(2,1)} async-done(((bf16[768,192]{1,0:T(8,128)(2,1)}), bf16[96,192]{1,0:T(8,128)(2,1)}) %reduce-scatter.70.cloned.1.call-update) | async-done | bytes 36880
  1142.5 35.8 %reduce-scatter.66.cloned.1.call-done = bf16[96,192]{1,0:T(8,128)(2,1)} async-done(((bf16[768,192]{1,0:T(8,128)(2,1)}), bf16[96,192]{1,0:T(8,128)(2,1)}) %reduce-scatter.66.cloned.1.call-update) | async-done | bytes 36880
  1179.2 35.8 %reduce-scatter.62.cloned.1.call-done = bf16[96,192]{1,0:T(8,128)(2,1)} async-done(((bf16[768,192]{1,0:T(8,128)(2,1)}), bf16[96,192]{1,0:T(8,128)(2,1)}) %reduce-scatter.62.cloned.1.call-update) | async-done | bytes 36880
  1216.0 36.1 %reduce-scatter.78.cloned.1.call-done = bf16[96,2]{1,0:T(8,128)(2,1)} async-done(((bf16[768,2]{1,0:T(8,128)(2,1)}), bf16[96,2]{1,0:T(8,128)(2,1)}) %reduce-scatter.78.cloned.1.call-update) | async-done | bytes 400
  1252.9 39.4 %reduce-scatter.56.cloned.1.call-done = bf16[768,96]{0,1:T(8,128)(2,1)} async-done(((bf16[768,768]{0,1:T(8,128)(2,1)}), bf16[768,96]{0,1:T(8,128)(2,1)}) %reduce-scatter.56.cloned.1.call-update) | async-done | bytes 147472 | tf_op jit(solution)/shard_map/reduce_scatter | solution.py:317
  1292.3 39.9 %reduce-scatter.54.cloned.1.call-done = bf16[768,96]{0,1:T(8,128)(2,1)} async-done(((bf16[768,768]{0,1:T(8,128)(2,1)}), bf16[768,96]{0,1:T(8,128)(2,1)}) %reduce-scatter.54.cloned.1.call-update) | async-done | bytes 147472 | tf_op jit(solution)/shard_map/reduce_scatter | solution.py:317
  1334.1 38.5 %reduce-scatter.52.cloned.1.call-done = bf16[96,768]{1,0:T(8,128)(2,1)} async-done(((bf16[768,768]{1,0:T(8,128)(2,1)}), bf16[96,768]{1,0:T(8,128)(2,1)}) %reduce-scatter.52.cloned.1.call-update) | async-done | bytes 147472 | tf_op jit(solution)/shard_map/reduce_scatter | solution.py:311
  1372.6 39.9 %reduce-scatter.50.cloned.1.call-done = bf16[96,768]{1,0:T(8,128)(2,1)} async-done(((bf16[768,768]{1,0:T(8,128)(2,1)}), bf16[96,768]{1,0:T(8,128)(2,1)}) %reduce-scatter.50.cloned.1.call-update) | async-done | bytes 147472 | tf_op jit(solution)/shard_map/reduce_scatter | solution.py:311
  1414.3 13.1 psum.95
  1427.7 22.3 %all-reduce.6 = (bf16[2,192]{1,0:T(2,128)(2,1)S(1)}, bf16[2,192]{1,0:T(2,128)(2,1)S(1)}, bf16[768]{0:T(1024)(128)(2,1)S(1)}, bf16[768]{0:T(1024)(128)(2,1)S(1)},...) all-reduce(bf16[2,192]{1,0:T(2,128)(2,1)S(1)} %pad_maximum_fusion.7, ...), channel_id=9, replica_groups=mesh['dp'=8,'head'=4] {'dp'}, use_global_device_ids=true, to_apply=%region_47.50.clone | all-reduce | flops 3840 | bytes 15360
  1452.8 33.7 %reduce-scatter.80.cloned.1.call-done = bf16[96,2]{1,0:T(8,128)(2,1)} async-done(((bf16[768,2]{1,0:T(8,128)(2,1)}), bf16[96,2]{1,0:T(8,128)(2,1)}) %reduce-scatter.80.cloned.1.call-update) | async-done | bytes 400
  1487.9 35.8 %reduce-scatter.72.cloned.1.call-done = bf16[96,192]{1,0:T(8,128)(2,1)} async-done(((bf16[768,192]{1,0:T(8,128)(2,1)}), bf16[96,192]{1,0:T(8,128)(2,1)}) %reduce-scatter.72.cloned.1.call-update) | async-done | bytes 36880
  1524.6 36.2 %reduce-scatter.68.cloned.1.call-done = bf16[96,192]{1,0:T(8,128)(2,1)} async-done(((bf16[768,192]{1,0:T(8,128)(2,1)}), bf16[96,192]{1,0:T(8,128)(2,1)}) %reduce-scatter.68.cloned.1.call-update) | async-done | bytes 36880
  1561.6 36.3 %reduce-scatter.64.cloned.1.call-done = bf16[96,192]{1,0:T(8,128)(2,1)} async-done(((bf16[768,192]{1,0:T(8,128)(2,1)}), bf16[96,192]{1,0:T(8,128)(2,1)}) %reduce-scatter.64.cloned.1.call-update) | async-done | bytes 36880
  1598.8 36.1 %reduce-scatter.60.cloned.1.call-done = bf16[96,192]{1,0:T(8,128)(2,1)} async-done(((bf16[768,192]{1,0:T(8,128)(2,1)}), bf16[96,192]{1,0:T(8,128)(2,1)}) %reduce-scatter.60.cloned.1.call-update) | async-done | bytes 36880
  1636.7 96.3 %all-reduce.33.cloned.1.call-done = bf16[1536,768]{1,0:T(8,128)(2,1)} async-done(((bf16[1536,768]{1,0:T(8,128)(2,1)}), bf16[1536,768]{1,0:T(8,128)(2,1)}) %all-reduce.33.cloned.1.call-update) | async-done | bytes 2359312 | tf_op jit(solution)/shard_map/psum | solution.py:57
  1733.0 6.0 add_reduce_fusion
  1742.3 30.3 %reduce-scatter.76.cloned.1.call-done = bf16[96,2]{1,0:T(8,128)(2,1)} async-done(((bf16[768,2]{1,0:T(8,128)(2,1)}), bf16[96,2]{1,0:T(8,128)(2,1)}) %reduce-scatter.76.cloned.1.call-update) | async-done | bytes 400
  (570 shorter events, 253.5 us)
Async XLA Ops:
  7.2 480.5 %copy-start = (bf16[768,192]{0,1:T(8,128)(2,1)S(1)}, bf16[768,192]{0,1:T(8,128)(2,1)}, u32[]{:S(2)}) copy-start(bf16[768,192]{0,1:T(8,128)(2,1)} %param.49) | copy-start | bytes 884740
  7.2 130.4 %all-reduce.17.cloned.1.call-start = ((), (), s32[]{:S(2)}) async-start(), calls=%async_computation.19 | async-start | bytes 4718592 | tf_op jit(solution)/shard_map/psum | solution.py:51
  25.4 242.2 %copy-start.85 = (f32[3]{0:T(128)}, f32[3]{0:T(128)S(1)}, u32[]{:S(2)}) copy-start(f32[3]{0:T(128)S(1)} %get-tuple-element.179) | copy-start | bytes 40
  39.1 206.8 %all-reduce.19.cloned.1.call-start = ((), (), s32[]{:S(2)}) async-start(), calls=%async_computation.20 | async-start | bytes 4718592 | tf_op jit(solution)/shard_map/psum | solution.py:51
  40.5 104.0 %copy-start.120 = (f32[768]{0:T(1024)}, f32[768]{0:T(1024)S(1)}, u32[]{:S(2)}) copy-start(f32[768]{0:T(1024)S(1)} %get-tuple-element.130) | copy-start | bytes 9220
  41.2 103.4 %copy-start.89 = (f32[768]{0:T(1024)}, f32[768]{0:T(1024)S(1)}, u32[]{:S(2)}) copy-start(f32[768]{0:T(1024)S(1)} %get-tuple-element.128) | copy-start | bytes 9220
  41.8 204.2 %copy-start.65 = (f32[768]{0:T(1024)}, f32[768]{0:T(1024)S(1)}, u32[]{:S(2)}) copy-start(f32[768]{0:T(1024)S(1)} %get-tuple-element.125) | copy-start | bytes 9220
  41.8 204.1 %copy-start.79 = (f32[768]{0:T(1024)}, f32[768]{0:T(1024)S(1)}, u32[]{:S(2)}) copy-start(f32[768]{0:T(1024)S(1)} %get-tuple-element.117) | copy-start | bytes 9220
  42.5 203.5 %copy-start.87 = (f32[768]{0:T(1024)}, f32[768]{0:T(1024)S(1)}, u32[]{:S(2)}) copy-start(f32[768]{0:T(1024)S(1)} %get-tuple-element.121) | copy-start | bytes 9220
  140.2 105.7 %copy-start.63 = (f32[1536]{0:T(1024)}, f32[1536]{0:T(1024)S(1)}, u32[]{:S(2)}) copy-start(f32[1536]{0:T(1024)S(1)} %broadcast_multiply_fusion.3) | copy-start | bytes 18436
  141.6 104.4 %copy-start.67 = (f32[1536]{0:T(1024)}, f32[1536]{0:T(1024)S(1)}, u32[]{:S(2)}) copy-start(f32[1536]{0:T(1024)S(1)} %fusion.146) | copy-start | bytes 18436
  151.1 219.3 %all-reduce.21.cloned.1.call-start = ((), (), s32[]{:S(2)}) async-start(), calls=%async_computation.21 | async-start | bytes 4718592 | tf_op jit(solution)/shard_map/psum | solution.py:51
  275.6 205.9 %all-reduce.23.cloned.1.call-start = ((), (), s32[]{:S(2)}) async-start(), calls=%async_computation.22 | async-start | bytes 4718592 | tf_op jit(solution)/shard_map/psum | solution.py:51
  276.5 103.4 %copy-start.122 = (f32[768]{0:T(1024)}, f32[768]{0:T(1024)S(1)}, u32[]{:S(2)}) copy-start(f32[768]{0:T(1024)S(1)} %get-tuple-element.132) | copy-start | bytes 9220
  386.6 202.2 %all-reduce.25.cloned.1.call-start = ((), (), s32[]{:S(2)}) async-start(), calls=%async_computation.23 | async-start | bytes 4718592 | tf_op jit(solution)/shard_map/psum | solution.py:57
  494.0 212.2 %all-reduce.27.cloned.1.call-start = ((), (), s32[]{:S(2)}) async-start(), calls=%async_computation.24 | async-start | bytes 4718592 | tf_op jit(solution)/shard_map/psum | solution.py:57
  611.4 225.9 %all-reduce.29.cloned.1.call-start = ((), (), s32[]{:S(2)}) async-start(), calls=%async_computation.25 | async-start | bytes 4718592 | tf_op jit(solution)/shard_map/psum | solution.py:57
  742.4 215.1 %all-reduce.31.cloned.1.call-start = ((), (), s32[]{:S(2)}) async-start(), calls=%async_computation.26 | async-start | bytes 4718592 | tf_op jit(solution)/shard_map/psum | solution.py:57
  862.7 223.0 %reduce-scatter.58.cloned.1.call-start = ((), (), s32[]{:S(2)}) async-start(), calls=%async_computation.32 | async-start | bytes 442368 | tf_op jit(solution)/shard_map/reduce_scatter | solution.py:326
  868.4 218.9 %reduce-scatter.86.cloned.1.call-start = ((), (), s32[]{:S(2)}) async-start(), calls=%async_computation.46 | async-start | bytes 221184
  871.6 216.5 %reduce-scatter.82.cloned.1.call-start = ((), (), s32[]{:S(2)}) async-start(), calls=%async_computation.44 | async-start | bytes 221184
  872.6 232.1 %reduce-scatter.74.cloned.1.call-start = ((), (), s32[]{:S(2)}) async-start(), calls=%async_computation.40 | async-start | bytes 442368
  876.7 264.8 %reduce-scatter.70.cloned.1.call-start = ((), (), s32[]{:S(2)}) async-start(), calls=%async_computation.38 | async-start | bytes 442368
  880.1 298.2 %reduce-scatter.66.cloned.1.call-start = ((), (), s32[]{:S(2)}) async-start(), calls=%async_computation.36 | async-start | bytes 442368
  883.4 331.7 %reduce-scatter.62.cloned.1.call-start = ((), (), s32[]{:S(2)}) async-start(), calls=%async_computation.34 | async-start | bytes 442368
  886.8 365.3 %reduce-scatter.78.cloned.1.call-start = ((), (), s32[]{:S(2)}) async-start(), calls=%async_computation.42 | async-start | bytes 221184
  887.8 404.5 %reduce-scatter.56.cloned.1.call-start = ((), (), s32[]{:S(2)}) async-start(), calls=%async_computation.31 | async-start | bytes 1327104 | tf_op jit(solution)/shard_map/reduce_scatter | solution.py:317
  895.7 436.5 %reduce-scatter.54.cloned.1.call-start = ((), (), s32[]{:S(2)}) async-start(), calls=%async_computation.30 | async-start | bytes 1327104 | tf_op jit(solution)/shard_map/reduce_scatter | solution.py:317
  903.7 468.9 %reduce-scatter.52.cloned.1.call-start = ((), (), s32[]{:S(2)}) async-start(), calls=%async_computation.29 | async-start | bytes 1327104 | tf_op jit(solution)/shard_map/reduce_scatter | solution.py:311
  909.0 503.5 %reduce-scatter.50.cloned.1.call-start = ((), (), s32[]{:S(2)}) async-start(), calls=%async_computation.28 | async-start | bytes 1327104 | tf_op jit(solution)/shard_map/reduce_scatter | solution.py:311
  920.1 531.8 %reduce-scatter.84.cloned.1.call-start = ((), (), s32[]{:S(2)}) async-start(), calls=%async_computation.45 | async-start | bytes 221184
  991.7 494.7 %reduce-scatter.80.cloned.1.call-start = ((), (), s32[]{:S(2)}) async-start(), calls=%async_computation.43 | async-start | bytes 221184
  994.6 529.1 %reduce-scatter.72.cloned.1.call-start = ((), (), s32[]{:S(2)}) async-start(), calls=%async_computation.39 | async-start | bytes 442368
  1009.4 551.4 %reduce-scatter.68.cloned.1.call-start = ((), (), s32[]{:S(2)}) async-start(), calls=%async_computation.37 | async-start | bytes 442368
  1020.5 577.4 %reduce-scatter.64.cloned.1.call-start = ((), (), s32[]{:S(2)}) async-start(), calls=%async_computation.35 | async-start | bytes 442368
  1028.7 606.2 %reduce-scatter.60.cloned.1.call-start = ((), (), s32[]{:S(2)}) async-start(), calls=%async_computation.33 | async-start | bytes 442368
  1035.6 298.4 %copy-start.124 = (f32[3]{0:T(128)S(1)}, f32[3]{0:T(128)}, u32[]{:S(2)}) copy-start(f32[3]{0:T(128)} %get-tuple-element.165) | copy-start | bytes 40
  1035.6 298.4 %copy-start.125 = (f32[3]{0:T(128)S(1)}, f32[3]{0:T(128)}, u32[]{:S(2)}) copy-start(f32[3]{0:T(128)} %get-tuple-element.163) | copy-start | bytes 40
  1035.6 298.4 %copy-start.127 = (f32[1,3]{1,0:T(1,128)S(1)}, f32[1,3]{1,0:T(1,128)}, u32[]{:S(2)}) copy-start(f32[1,3]{1,0:T(1,128)} %get-tuple-element.158) | copy-start | bytes 40
  1035.6 298.4 %copy-start.128 = (f32[1,3]{1,0:T(1,128)S(1)}, f32[1,3]{1,0:T(1,128)}, u32[]{:S(2)}) copy-start(f32[1,3]{1,0:T(1,128)} %get-tuple-element.180) | copy-start | bytes 40
  1035.6 697.3 %all-reduce.33.cloned.1.call-start = ((), (), s32[]{:S(2)}) async-start(), calls=%async_computation.27 | async-start | bytes 4718592 | tf_op jit(solution)/shard_map/psum | solution.py:57
  1041.7 385.7 %copy-start.109 = (bf16[768]{0:T(1024)(128)(2,1)S(1)}, bf16[768]{0:T(1024)(128)(2,1)}, u32[]{:S(2)}) copy-start(bf16[768]{0:T(1024)(128)(2,1)} %get-tuple-element.111) | copy-start | bytes 4612
  1041.7 385.7 %copy-start.130 = (bf16[3,64]{1,0:T(4,128)(2,1)S(1)}, bf16[3,64]{1,0:T(4,128)(2,1)}, u32[]{:S(2)}) copy-start(bf16[3,64]{1,0:T(4,128)(2,1)} %get-tuple-element.209) | copy-start | bytes 1156
  1041.7 385.9 %copy-start.104 = (bf16[768]{0:T(1024)(128)(2,1)S(1)}, bf16[768]{0:T(1024)(128)(2,1)}, u32[]{:S(2)}) copy-start(bf16[768]{0:T(1024)(128)(2,1)} %get-tuple-element.173) | copy-start | bytes 4612
  1041.7 385.9 %copy-start.105 = (bf16[768]{0:T(1024)(128)(2,1)S(1)}, bf16[768]{0:T(1024)(128)(2,1)}, u32[]{:S(2)}) copy-start(bf16[768]{0:T(1024)(128)(2,1)} %get-tuple-element.171) | copy-start | bytes 4612
  1041.7 385.9 %copy-start.107 = (bf16[768]{0:T(1024)(128)(2,1)S(1)}, bf16[768]{0:T(1024)(128)(2,1)}, u32[]{:S(2)}) copy-start(bf16[768]{0:T(1024)(128)(2,1)} %get-tuple-element.141) | copy-start | bytes 4612
  1041.7 385.9 %copy-start.108 = (bf16[768]{0:T(1024)(128)(2,1)S(1)}, bf16[768]{0:T(1024)(128)(2,1)}, u32[]{:S(2)}) copy-start(bf16[768]{0:T(1024)(128)(2,1)} %get-tuple-element.139) | copy-start | bytes 4612
  1041.8 730.8 %reduce-scatter.76.cloned.1.call-start = ((), (), s32[]{:S(2)}) async-start(), calls=%async_computation.41 | async-start | bytes 221184
  (135 other events, 1182.4 us)
Sparse Core Ops, SparseCore 0:
  39.2 98.3 all-reduce.16
  151.2 94.6 all-reduce.18
  275.7 94.6 all-reduce.20
  386.7 94.6 all-reduce.22
  494.2 94.6 all-reduce.24
  611.5 94.6 all-reduce.26
  742.6 94.6 all-reduce.28
  862.8 94.6 all-reduce.30
  960.6 32.8 reduce-scatter.57
  996.9 33.4 reduce-scatter.85
  1034.3 33.5 reduce-scatter.81
  1070.8 33.8 reduce-scatter.73
  1107.8 33.7 reduce-scatter.69
  1144.5 33.7 reduce-scatter.65
  1181.2 33.7 reduce-scatter.61
  1218.5 33.4 reduce-scatter.77
  1255.5 36.7 reduce-scatter.55
  1295.4 36.7 reduce-scatter.53
  1335.8 36.7 reduce-scatter.51
  1375.7 36.7 reduce-scatter.49
  1415.8 33.4 reduce-scatter.83
  1452.9 33.4 reduce-scatter.79
  1489.8 33.8 reduce-scatter.71
  1526.9 33.8 reduce-scatter.67
  1564.1 33.8 reduce-scatter.63
  1601.1 33.8 reduce-scatter.59
  1637.3 95.6 all-reduce.32
  1740.0 32.5 reduce-scatter.75
where the time goes:
time: 1790 us; the launch traced here: 1780 us
  waiting for transfers between devices  1290 us (72%)
  matrix products  174 us (10%)
  other arithmetic  115 us (6%)
  blocking collectives  89.4 us (5%)
  local copies, waits for them, and re-layouts  78.6 us (4%)
  between operations  26.9 us (2%)
    psum x5, waiting for transfers between devices, head_total(): return lax.psum(grad_part.astype(jnp.bfloat16), 'head').astype(jnp.float32)  409 us
    unnamed x42, waiting for transfers between devices  368 us
    psum x4, waiting for transfers between devices, add_norm(): lax.psum(branch_part.astype(jnp.bfloat16), 'head').astype(jnp.float32)  359 us
    reduce_scatter x2, waiting for transfers between devices, on_device(): lax.psum_scatter(grad_outer.astype(jnp.bfloat16), 'dp', scatter_dimension...  79.3 us
    reduce_scatter x2, waiting for transfers between devices, on_device(): lax.psum_scatter(grad_inner.astype(jnp.bfloat16), 'dp', scatter_dimension...  78.4 us
    unnamed x349, local copies, waits for them, and re-layouts  51 us
    dot_general x14, matrix products, inner_rows(): lax.dot_general(left, right, (((0,), (0,)), ((), ())), preferred_element_...  49.7 us
    dot_general x14, matrix products, matmul(): return jnp.dot(left, right, preferred_element_type=jnp.float32)  41.2 us
  transfers between devices with their start and end apart: 28, of which 24 were waited for; matrix products, arithmetic and copies ran while one was open for 10% of the time, Pallas kernels for 0%

commit v1 on v0

v1 whole, which is shorter than its diff:
```python
from functools import partial

import jax
import jax.numpy as jnp
from jax import lax
from jax.experimental import pallas as pl
from jax.experimental.pallas import tpu as pltpu
from jax.sharding import PartitionSpec as P

BETA = 2.0 / 3.0
EPS = 1e-05
LOW = jnp.bfloat16
F32 = jnp.float32
GELU_C = 0.7978845608028654
GELU_K = 0.044715
VMEM_LIMIT = 56 * 1024 * 1024


def gate_open(noise, alpha):
    return jnp.clip(jax.nn.sigmoid((noise + alpha) / BETA) * 1.2 - 0.1, 0.0, 1.0)


def product(left, right, dims):
    return lax.dot_general(left, right, ((dims[:1], dims[1:]), ((), ())), preferred_element_type=F32)


def nn(left, right):
    return product(left, right, (1, 0))


def nt(left, right):
    return product(left, right, (1, 1))


def tn(left, right):
    return product(left, right, (0, 0))


def full(array):
    shape = array.shape
    return pl.BlockSpec(shape, lambda r, info: (0,) * len(shape))


def by_group(shape):
    return pl.BlockSpec((1,) + shape[1:], lambda r, info: (r,) + (0,) * (len(shape) - 1))


def run(body, groups, info, inputs, outputs, scratch, flops, name):
    specs = {
        "full": full,
        "group": lambda a: by_group(a.shape),
        "any": lambda a: pl.BlockSpec(memory_space=pl.ANY),
    }
    out_shape = [jax.ShapeDtypeStruct(shape, dtype) for shape, dtype, _ in outputs]
    moved = sum(a.size * a.dtype.itemsize for a, _ in inputs)
    return pl.pallas_call(
        body,
        name=name,
        grid_spec=pltpu.PrefetchScalarGridSpec(
            num_scalar_prefetch=1,
            grid=(groups,),
            in_specs=[specs[kind](a) for a, kind in inputs],
            out_specs=[specs[kind](o) for o, (_, _, kind) in zip(out_shape, outputs)],
            scratch_shapes=scratch,
        ),
        out_shape=out_shape,
        compiler_params=pltpu.CompilerParams(vmem_limit_bytes=VMEM_LIMIT),
        cost_estimate=pl.CostEstimate(flops=int(flops), bytes_accessed=int(moved), transcendentals=0),
    )(info, *[a for a, _ in inputs])


class Stream:
    def __init__(self, own, parts, col, width, buf, sems):
        self.own, self.parts, self.col, self.width, self.buf, self.sems = own, parts, col, width, buf, sems

    def first(self):
        return [
            pltpu.make_async_copy(
                self.own.at[:, pl.ds(self.col, self.width)], self.buf.at[0], self.sems.at[0, 0]
            )
        ]

    def later(self, index, slot):
        copies, row = [], 0
        for number, part in enumerate(self.parts):
            rows = part.shape[1]
            copies.append(
                pltpu.make_async_copy(
                    part.at[index - 1, :, pl.ds(self.col, self.width)],
                    self.buf.at[slot, pl.ds(row, rows), :],
                    self.sems.at[slot, number],
                )
            )
            row += rows
        return copies


def turn(streams, r, groups):
    slot = lax.rem(r, 2)

    @pl.when(r == 0)
    def _():
        for stream in streams:
            for copy in stream.first():
                copy.start()
        for stream in streams:
            for copy in stream.later(1, 1):
                copy.start()
        for stream in streams:
            for copy in stream.first():
                copy.wait()

    @pl.when((r > 0) & (r < groups - 1))
    def _():
        for stream in streams:
            for copy in stream.later(r + 1, 1 - slot):
                copy.start()

    @pl.when(r > 0)
    def _():
        for stream in streams:
            for copy in stream.later(r, slot):
                copy.wait()

    return slot


class Gathered:
    def __init__(self, own, parts, col=0, width=None):
        self.own, self.parts, self.col = own, parts, col
        self.width = own.shape[1] if width is None else width

    def columns(self, col, width):
        return Gathered(self.own, self.parts, col, width)

    def operands(self):
        return [(self.own, "any")] + [(part, "any") for part in self.parts]

    def scratch(self):
        return [
            pltpu.VMEM((2, self.own.shape[0], self.width), LOW),
            pltpu.SemaphoreType.DMA((2, len(self.parts))),
        ]

    def stream(self, refs, buf, sems):
        return Stream(refs[0], refs[1:], self.col, self.width, buf, sems)


def norm_forward(before, gain, shift):
    center = before - jnp.mean(before, -1, keepdims=True)
    spread = jnp.mean(center * center, -1, keepdims=True)
    return center * lax.rsqrt(spread + EPS) * gain + shift


def norm_backward(before, gain, grad):
    center = before - jnp.mean(before, -1, keepdims=True)
    rate = lax.rsqrt(jnp.mean(center * center, -1, keepdims=True) + EPS)
    hat = center * rate
    grad_hat = grad * gain
    mean_one = jnp.mean(grad_hat, -1, keepdims=True)
    mean_two = jnp.mean(grad_hat * hat, -1, keepdims=True)
    grad_before = rate * (grad_hat - mean_one - hat * mean_two)
    return (
        grad_before,
        jnp.sum(grad * hat, 0, keepdims=True),
        jnp.sum(grad, 0, keepdims=True),
        jnp.sum(grad_before, 0, keepdims=True),
    )


BIAS_ONE, BIAS_TWO, GAIN_ONE, GAIN_TWO, SHIFT_ONE, SHIFT_TWO = range(6)
OWN, PAIR, MID, MID_ROW, LOC, LENGTH = 0, 1, 2, 3, 4, 8


def attention_forward(size, layer, first, left, right, info, *refs):
    seq_len, block, heads, head_size = size
    refs = list(refs)
    xwin, small, vec = refs[:3]
    refs = refs[3:]
    resid = None if first else refs.pop(0)
    left_refs = [refs.pop(0) for _ in left.operands()]
    right_refs = [refs.pop(0) for _ in right.operands()]
    kv_out, q_out, ctx_out, lse_out, gated_out, before_out, h_out, hb_out = refs[:8]
    left_buf, left_sems, right_buf, right_sems, total = refs[8:]
    r, groups = pl.program_id(0), pl.num_programs(0)
    slot = turn(
        [left.stream(left_refs, left_buf, left_sems), right.stream(right_refs, right_buf, right_sems)], r, groups
    )
    width = heads * head_size
    rows = total.shape[0]
    row = small[0, 4 * layer + 2 : 4 * layer + 3, :]
    kv = nn(xwin[...], left_buf[slot]) + row[:, 2 * width :]
    kv_out[0] = kv.astype(LOW)
    own = pl.multiple_of(info[OWN], block)
    query = (nn(xwin[pl.ds(own, rows), :], right_buf[slot, :, :width]) + row[:, :width]).astype(LOW)
    q_out[0] = query
    scaled = query * jnp.asarray(0.125, LOW)
    for piece in range(rows // block):
        here = slice(piece * block, (piece + 1) * block)
        loc = info[LOC + piece]
        length = info[LENGTH + loc]
        keys = pl.ds(pl.multiple_of(loc * seq_len, seq_len), seq_len)
        usable = lax.broadcasted_iota(jnp.int32, (block, seq_len), 1) < length
        for head in range(heads):
            lanes = slice(head * head_size, (head + 1) * head_size)
            scores = nt(scaled[here, lanes], kv_out[0, keys, lanes])
            scores = jnp.where(usable, scores, -1e30)
            largest = jnp.max(scores, -1, keepdims=True)
            powers = jnp.exp(scores - largest)
            sums = jnp.sum(powers, -1, keepdims=True)
            value = kv_out[0, keys, width + head * head_size : width + (head + 1) * head_size]
            context = nn(powers.astype(LOW), value) / sums
            ctx_out[0, here, lanes] = context
            lse_out[0, here, head : head + 1] = largest + jnp.log(sums)
    gated = (ctx_out[0] * row[:, width : 2 * width]).astype(LOW)
    gated_out[0] = gated
    part = nt(gated, right_buf[slot, :, width:])

    @pl.when(r == 0)
    def _():
        total[...] = part

    @pl.when(r > 0)
    def _():
        total[...] += part

    @pl.when(r == groups - 1)
    def _():
        base = 6 * layer
        if first:
            current = xwin[pl.ds(own, rows), :].astype(F32)
        else:
            current = resid[...]
        before = current + total[...] + vec[base + BIAS_ONE : base + BIAS_ONE + 1, :]
        middle = norm_forward(
            before,
            vec[base + GAIN_ONE : base + GAIN_ONE + 1, :],
            vec[base + SHIFT_ONE : base + SHIFT_ONE + 1, :],
        )
        before_out[...] = before
        h_out[...] = middle
        hb_out[...] = middle.astype(LOW)


def gelu_parts(unit):
    square = unit * unit
    bent = jnp.tanh(GELU_C * unit * (1.0 + GELU_K * square))
    half = 0.5 * (1.0 + bent)
    slope = half + 0.5 * unit * (1.0 - bent * bent) * (GELU_C * (1.0 + 3.0 * GELU_K * square))
    return unit * half, slope


def feed_forward(layer, left, right, info, *refs):
    refs = list(refs)
    middle, middle_low, small, vec = refs[:4]
    refs = refs[4:]
    left_refs = [refs.pop(0) for _ in left.operands()]
    right_refs = [refs.pop(0) for _ in right.operands()]
    unit_out, before_out, x_out, xb_out = refs[:4]
    left_buf, left_sems, right_buf, right_sems, total = refs[4:]
    r, groups = pl.program_id(0), pl.num_programs(0)
    slot = turn(
        [left.stream(left_refs, left_buf, left_sems), right.stream(right_refs, right_buf, right_sems)], r, groups
    )
    unit = nn(middle_low[...], left_buf[slot]) + small[0, 4 * layer + 1 : 4 * layer + 2, :]
    unit_out[0] = unit.astype(LOW)
    bent = jnp.tanh(GELU_C * unit * (1.0 + GELU_K * (unit * unit)))
    active = (0.5 * unit * (1.0 + bent) * small[0, 4 * layer : 4 * layer + 1, :]).astype(LOW)
    part = nt(active, right_buf[slot])

    @pl.when(r == 0)
    def _():
        total[...] = part

    @pl.when(r > 0)
    def _():
        total[...] += part

    @pl.when(r == groups - 1)
    def _():
        base = 6 * layer
        before = middle[...] + total[...] + vec[base + BIAS_TWO : base + BIAS_TWO + 1, :]
        current = norm_forward(
            before,
            vec[base + GAIN_TWO : base + GAIN_TWO + 1, :],
            vec[base + SHIFT_TWO : base + SHIFT_TWO + 1, :],
        )
        before_out[...] = before
        x_out[...] = current
        xb_out[...] = current.astype(LOW)


def match_teacher(layers, weight, info, *refs):
    refs = list(refs)
    states = [refs.pop(0) for _ in range(layers)]
    target, row_ok, factor = refs[:3]
    refs = refs[3:]
    weight_refs = [refs.pop(0) for _ in weight.operands()]
    back_out, loss_out, keep_out, send_out = refs[:4]
    buf, sems = refs[4:]
    r, groups = pl.program_id(0), pl.num_programs(0)
    slot = turn([weight.stream(weight_refs, buf, sems)], r, groups)

    @pl.when(r == 0)
    def _():
        loss_out[...] = jnp.zeros_like(loss_out)
        back_out[...] = jnp.zeros_like(back_out)

    total = None
    for layer in range(layers):
        miss = (nn(states[layer][...], buf[slot]) - target[0, layer].astype(F32)) * row_ok[:, :1]
        loss_out[:1, : miss.shape[1]] += jnp.sum(miss * miss, 0, keepdims=True)
        low = (factor[0, 0] * miss).astype(LOW)
        back_out[layer] += nt(low, buf[slot])
        grad = tn(states[layer][...], low)
        total = grad if total is None else total + grad
    half = keep_out.shape[1]
    keep_out[0] = total[:half].astype(LOW)
    send_out[0] = total[half:].astype(LOW)


def feed_backward(layer, last, left, right, info, *refs):
    refs = list(refs)
    before_two, before_one, middle_low, unit_in, small, vec = refs[:6]
    refs = refs[6:]
    if last:
        grad_refs = refs[:2]
        refs = refs[2:]
    else:
        grad_refs = refs[:3]
        refs = refs[3:]
    left_refs = [refs.pop(0) for _ in left.operands()]
    right_refs = [refs.pop(0) for _ in right.operands()]
    inner_keep, inner_send, outer_keep, outer_send, attn_out, grad_out, vec_out, unit_vec = refs[:8]
    left_buf, left_sems, right_buf, right_sems, total, feed = refs[8:]
    r, groups = pl.program_id(0), pl.num_programs(0)
    slot = turn(
        [left.stream(left_refs, left_buf, left_sems), right.stream(right_refs, right_buf, right_sems)], r, groups
    )
    base = 6 * layer

    @pl.when(r == 0)
    def _():
        if last:
            cotangent, back = grad_refs
            grad = cotangent[...].astype(F32) + back[...]
        else:
            mine, pair, mid = grad_refs
            total[...] = mine[...] + pair[...].astype(F32)
            here = pl.ds(pl.multiple_of(info[MID_ROW], mid.shape[0] // 2), mid.shape[0])
            total[here, :] += mid[...].astype(F32)
            grad = total[...]
        grad_before, grad_gain, grad_shift, grad_bias = norm_backward(
            before_two[...], vec[base + GAIN_TWO : base + GAIN_TWO + 1, :], grad
        )
        vec_out[BIAS_TWO : BIAS_TWO + 1, :] = grad_bias
        vec_out[GAIN_TWO : GAIN_TWO + 1, :] = grad_gain
        vec_out[SHIFT_TWO : SHIFT_TWO + 1, :] = grad_shift
        feed[...] = grad_before.astype(LOW)
        total[...] = grad_before

    grad_active = nn(feed[...], right_buf[slot])
    value, slope = gelu_parts(unit_in[0].astype(F32))
    opened = small[0, 4 * layer : 4 * layer + 1, :]
    grad_unit = (grad_active * (slope * opened)).astype(LOW)
    unit_vec[0, 0:1, :] = jnp.sum(grad_unit.astype(F32), 0, keepdims=True)
    unit_vec[0, 1:2, :] = jnp.sum(grad_active * value, 0, keepdims=True)
    active = (value * opened).astype(LOW)
    half = inner_keep.shape[1]
    total[...] += nt(grad_unit, left_buf[slot])
    inner_keep[0] = tn(middle_low[:, :half], grad_unit).astype(LOW)
    inner_send[0] = tn(middle_low[:, half:], grad_unit).astype(LOW)
    outer_keep[0] = tn(feed[:, :half], active).astype(LOW)
    outer_send[0] = tn(feed[:, half:], active).astype(LOW)

    @pl.when(r == groups - 1)
    def _():
        grad_before, grad_gain, grad_shift, grad_bias = norm_backward(
            before_one[...], vec[base + GAIN_ONE : base + GAIN_ONE + 1, :], total[...]
        )
        vec_out[BIAS_ONE : BIAS_ONE + 1, :] = grad_bias
        vec_out[GAIN_ONE : GAIN_ONE + 1, :] = grad_gain
        vec_out[SHIFT_ONE : SHIFT_ONE + 1, :] = grad_shift
        grad_out[...] = grad_before
        attn_out[...] = grad_before.astype(LOW)


def attention_backward(size, layer, extra, left, right, info, *refs):
    seq_len, block, heads, head_size = size
    refs = list(refs)
    attn, grad_before, xwin, query_in, kv, ctx, lse, gated, small = refs[:9]
    refs = refs[9:]
    back = refs.pop(0) if extra else None
    left_refs = [refs.pop(0) for _ in left.operands()]
    right_refs = [refs.pop(0) for _ in right.operands()]
    left_keep, left_send, right_keep, right_send, mine_out, pair_out, mid_out, head_vec = refs[:8]
    left_buf, left_sems, right_buf, right_sems, grad_kv, grad_q, window, mine = refs[8:]
    r, groups = pl.program_id(0), pl.num_programs(0)
    slot = turn(
        [left.stream(left_refs, left_buf, left_sems), right.stream(right_refs, right_buf, right_sems)], r, groups
    )
    width = heads * head_size
    rows = mine.shape[0]
    row = small[0, 4 * layer + 2 : 4 * layer + 3, :]
    opened = row[:, width : 2 * width]
    grad_gated = nn(attn[...], right_buf[slot, :, width:])
    shared = grad_gated * ctx[0]
    grad_ctx = (grad_gated * opened).astype(LOW)
    pulled = shared * opened
    scaled = query_in[0] * jnp.asarray(0.125, LOW)
    grad_kv[...] = jnp.zeros_like(grad_kv)
    for piece in range(rows // block):
        here = slice(piece * block, (piece + 1) * block)
        loc = info[LOC + piece]
        length = info[LENGTH + loc]
        keys = pl.ds(pl.multiple_of(loc * seq_len, seq_len), seq_len)
        usable = lax.broadcasted_iota(jnp.int32, (block, seq_len), 1) < length
        for head in range(heads):
            lanes = slice(head * head_size, (head + 1) * head_size)
            later = slice(width + head * head_size, width + (head + 1) * head_size)
            key = kv[0, keys, lanes]
            scores = nt(scaled[here, lanes], key)
            chances = jnp.where(usable, jnp.exp(scores - lse[0, here, head : head + 1]), 0.0)
            grad_chances = nt(grad_ctx[here, lanes], kv[0, keys, later])
            delta = jnp.sum(pulled[here, lanes], -1, keepdims=True)
            grad_scores = (chances * (grad_chances - delta)).astype(LOW)
            grad_q[here, lanes] = nn(grad_scores, key) * 0.125
            grad_kv[keys, lanes] += tn(grad_scores, scaled[here, lanes])
            grad_kv[keys, later] += tn(chances.astype(LOW), grad_ctx[here, lanes])
    query_low = grad_q[...].astype(LOW)
    kv_low = grad_kv[...].astype(LOW)
    head_vec[0, 0:1, :width] = jnp.sum(query_low.astype(F32), 0, keepdims=True)
    head_vec[0, 0:1, 2 * width :] = jnp.sum(kv_low.astype(F32), 0, keepdims=True)
    head_vec[0, 1:2, :width] = jnp.sum(shared, 0, keepdims=True)
    own = pl.multiple_of(info[OWN], block)

    @pl.when(r == 0)
    def _():
        window[...] = jnp.zeros_like(window)
        if extra:
            mine[...] = grad_before[...] + back[0]
        else:
            mine[...] = grad_before[...]

    window[...] += nt(kv_low, left_buf[slot])
    mine[...] += nt(query_low, right_buf[slot, :, :width])
    half = left_keep.shape[1]
    left_keep[0] = tn(xwin[:, :half], kv_low).astype(LOW)
    left_send[0] = tn(xwin[:, half:], kv_low).astype(LOW)
    here = pl.ds(own, rows)
    right_keep[0, :, :width] = tn(xwin[here, :half], query_low).astype(LOW)
    right_send[0, :, :width] = tn(xwin[here, half:], query_low).astype(LOW)
    right_keep[0, :, width:] = tn(attn[:, :half], gated[0]).astype(LOW)
    right_send[0, :, width:] = tn(attn[:, half:], gated[0]).astype(LOW)

    @pl.when(r == groups - 1)
    def _():
        mine_out[...] = mine[...] + window[here, :]
        pair_out[...] = window[pl.ds(pl.multiple_of(info[PAIR], block), rows), :].astype(LOW)
        mid_out[...] = window[pl.ds(pl.multiple_of(info[MID], block), mid_out.shape[0]), :].astype(LOW)


def place_rows(groups, info, *refs):
    pieces, matrix, out = refs[:groups], refs[groups], refs[groups + 1]
    r = pl.program_id(0)
    for group in range(groups):

        @pl.when(r == group)
        def _(group=group):
            out[...] = nn(pieces[group][...], matrix[...]).astype(out.dtype)


def factor_pair(count):
    side = 1
    for trial in range(1, count + 1):
        if count % trial == 0 and trial * trial <= count:
            side = trial
    return side, count // side


def after(value, *others):
    return lax.optimization_barrier((value,) + others)[0]


def on_device(
    ndp,
    groups,
    hidden_in,
    seq_lengths,
    layer_map,
    teacher_states,
    out_cotangent,
    query_weight,
    key_weight,
    value_weight,
    query_value_bias,
    output_weight,
    branch_bias,
    norm_gain,
    norm_shift,
    inner_weight,
    inner_bias,
    outer_weight,
    head_alpha,
    head_noise,
    unit_alpha,
    unit_noise,
    map_weight,
):
    tokens_dev, model = hidden_in.shape
    seqs_dev = seq_lengths.shape[0]
    seq_len = tokens_dev // seqs_dev
    width = query_weight.shape[2]
    units = inner_weight.shape[2]
    layers, heads = head_alpha.shape
    head_size = width // heads
    rows = tokens_dev // groups
    block = seq_len // groups
    blocks = rows // block
    mid_rows = 2 * block
    feats = model // ndp
    size_y, size_x = factor_pair(ndp // 2)
    chips = size_y * size_x
    half = chips * feats
    size = (seq_len, block, heads, head_size)
    dp = lax.axis_index("dp")
    h = lax.axis_index("head")
    my_c, my_x, my_y = dp % 2, (dp // 2) % size_x, dp // (2 * size_x)

    def relative(index, c, y, x):
        core, ix, iy = index % 2, (index // 2) % size_x, index // (2 * size_x)
        return (((iy + y) % size_y) * size_x + (ix + x) % size_x) * 2 + (core ^ c)

    def pull(value, c=0, y=0, x=0):
        return lax.ppermute(value, "dp", [(relative(i, c, y, x), i) for i in range(ndp)])

    def push(value, c=0, y=0, x=0):
        return lax.ppermute(value, "dp", [(i, relative(i, c, y, x)) for i in range(ndp)])

    def pull_group(value, r):
        return lax.ppermute(value, "head", [((i + r) % groups, i) for i in range(groups)])

    def push_group(value, r):
        return lax.ppermute(value, "head", [(i, (i + r) % groups) for i in range(groups)])

    def sum_plane(value):
        for axis, count in (("c", 2), ("y", size_y), ("x", size_x)):
            step = 1
            while step < count:
                stride = {"c": 1, "x": 2, "y": 2 * size_x}[axis] * step
                value = value + lax.ppermute(value, "dp", [(i, i ^ stride) for i in range(ndp)])
                step *= 2
        return value

    def sum_groups(value):
        step = 1
        while step < groups:
            value = value + lax.ppermute(value, "head", [(i, i ^ step) for i in range(groups)])
            step *= 2
        return value

    position = jnp.arange(ndp)
    pos_c, pos_y, pos_x = position // chips, (position // size_x) % size_y, position % size_x
    order = (((my_y + pos_y) % size_y) * size_x + (my_x + pos_x) % size_x) * 2 + (my_c ^ pos_c)
    place = (my_c ^ (position % 2)) * chips
    place = place + ((position // (2 * size_x) - my_y) % size_y) * size_x
    place = place + ((position // 2) % size_x - my_x) % size_x
    source = (order[:, None] * feats + jnp.arange(feats)[None, :]).reshape(model)
    matrix = (source[:, None] == jnp.arange(model)[None, :]).astype(LOW)

    def reorder(value):
        return product(matrix, value, (1, 0)).astype(LOW)

    def reorder_turned(value):
        return product(matrix, value, (1, 1)).astype(LOW)

    def gather(own, dep, y_first):
        mine = own[:feats]
        if dep is not None:
            mine = after(mine, dep)
        got = [pull_group(mine, r) for r in range(1, groups)]
        token = got[0]
        start = jnp.stack(got)
        found = {(0, 0): start}
        if y_first:
            for y in range(1, size_y):
                found[y, 0] = pull(start, y=y)
            for y in range(size_y):
                for x in range(1, size_x):
                    found[y, x] = pull(found[y, 0], x=x)
        else:
            for x in range(1, size_x):
                found[0, x] = pull(start, x=x)
            for x in range(size_x):
                for y in range(1, size_y):
                    found[y, x] = pull(found[0, x], y=y)
        pieces = [found[y, x] for y in range(size_y) for x in range(size_x)]
        if feats % 16:
            pieces = [jnp.concatenate(pieces, 1)]
        return Gathered(own, pieces + [pull(piece, c=1) for piece in pieces]), token

    def scatter(keep, send, y_first):
        terms = [keep, pull(send, c=1)]
        terms = [term.reshape(groups, size_y, size_x, feats, term.shape[-1]) for term in terms]

        def total(items):
            out = items[0].astype(F32)
            for item in items[1:]:
                out = out + item.astype(F32)
            return out

        for axis, count in (("y", size_y), ("x", size_x)) if y_first else (("x", size_x), ("y", size_y)):
            dim = 1 if axis == "y" else terms[0].ndim - 3

            def part(index):
                return [lax.index_in_dim(term, index, dim, keepdims=False) for term in terms]

            arrived = [push(total(part(i)).astype(LOW), **{axis: i}) for i in range(1, count)]
            terms = part(0) + arrived
        final = [term[0] for term in terms]
        for r in range(1, groups):
            final.append(push_group(total([term[r] for term in terms]).astype(LOW), r))
        return total(final)

    dep = None
    attn_weights, feed_weights = [], []
    for layer in range(layers):
        key_value = reorder(jnp.concatenate([key_weight[layer], value_weight[layer]], 1))
        query_output = jnp.concatenate(
            [reorder(query_weight[layer]), reorder_turned(output_weight[layer])], 1
        )
        inner = reorder(inner_weight[layer])
        outer = reorder_turned(outer_weight[layer])
        if layer == 0:
            left, dep = gather(key_value, dep, False)
            right, _ = gather(query_output, None, True)
            attn_weights.append((left, right))
            left, next_dep = gather(inner, dep, False)
            right, _ = gather(outer, dep, True)
            feed_weights.append((left, right))
            dep = next_dep
        else:
            left, next_dep = gather(jnp.concatenate([key_value, inner], 1), dep, False)
            right, _ = gather(jnp.concatenate([query_output, outer], 1), dep, True)
            attn_weights.append((left.columns(0, 2 * width), right.columns(0, 2 * width)))
            feed_weights.append((left.columns(2 * width, units), right.columns(2 * width, units)))
            dep = next_dep
    map_gathered, dep = gather(reorder(map_weight), dep, False)

    open_unit, unit_back = jax.vjp(partial(gate_open, unit_noise), unit_alpha)
    open_head, head_back = jax.vjp(partial(gate_open, head_noise), head_alpha)
    (unit_slope,) = unit_back(jnp.ones_like(open_unit))
    (head_slope,) = head_back(jnp.ones_like(open_head))
    mixed = jnp.concatenate(
        [
            query_value_bias[:, 0],
            jnp.repeat(open_head, head_size, axis=1),
            jnp.zeros((layers, width), F32),
            query_value_bias[:, 1],
        ],
        1,
    )
    empty = jnp.zeros((layers, units), F32)
    small_own = jnp.stack([open_unit, inner_bias, mixed, empty], 1).reshape(4 * layers, units)
    small = jnp.stack([small_own] + [pull_group(small_own, r) for r in range(1, groups)])
    vec = jnp.concatenate([branch_bias, norm_gain, norm_shift], 1).reshape(6 * layers, ndp, feats)
    vec = jnp.take(vec, order, axis=1).reshape(6 * layers, model)
    vec = jnp.concatenate([vec, jnp.zeros((16 - 6 * layers, model), F32)])

    win = jnp.minimum(h * rows // seq_len, seqs_dev - 2)
    base = win * seq_len
    pair_index = h ^ 1
    piece = jnp.arange(blocks)
    locs = (h * blocks + piece) * block // seq_len - win
    mid_row = jnp.where(h == 1, block, 0)
    lengths = lax.dynamic_slice(seq_lengths, (win,), (2,))
    info = jnp.concatenate(
        [
            jnp.stack([h * rows - base, pair_index * rows - base, jnp.where(h == 1, 2 * rows, 0), mid_row]),
            locs,
            jnp.zeros((LENGTH - LOC - blocks,), jnp.int32),
            lengths,
        ]
    ).astype(jnp.int32)
    spot = (h * rows + jnp.arange(rows)) % seq_len
    own_lengths = jnp.repeat(jnp.take(lengths, locs), block, total_repeat_length=rows)
    row_ok = jnp.broadcast_to((spot < own_lengths).astype(F32)[:, None], (rows, 128))
    count_all = sum_plane(jnp.sum(seq_lengths).astype(F32).reshape(1, 1))
    factor = (tokens_dev * ndp) / count_all

    hidden = product(lax.dynamic_slice(hidden_in, (base, 0), (2 * seq_len, model)), matrix, (1, 1)).astype(LOW)
    cotangent = product(
        lax.dynamic_slice(out_cotangent, (h * rows, 0), (rows, model)), matrix, (1, 1)
    ).astype(LOW)
    chosen = jnp.take(teacher_states, layer_map, axis=0)

    def teacher_rows(r):
        return lax.dynamic_slice(
            chosen, (0, ((h - r) % groups) * rows, 0), (layers, rows, width)
        )

    target = jnp.stack(
        [teacher_rows(0)] + [pull_group(after(teacher_rows(r), dep), r) for r in range(1, groups)]
    )

    xwin, resid = hidden, None
    records = []
    lows = []
    for layer in range(layers):
        left, right = attn_weights[layer]
        inputs = [(xwin, "full"), (small, "group"), (vec, "full")]
        if layer:
            inputs.append((resid, "full"))
        kv, query, ctx, lse, gated, before_one, middle, middle_low = run(
            partial(attention_forward, size, layer, layer == 0, left, right),
            groups,
            info,
            inputs + left.operands() + right.operands(),
            [
                ((groups, 2 * seq_len, 2 * width), LOW, "group"),
                ((groups, rows, width), LOW, "group"),
                ((groups, rows, width), F32, "group"),
                ((groups, rows, 128), F32, "group"),
                ((groups, rows, width), LOW, "group"),
                ((rows, model), F32, "full"),
                ((rows, model), F32, "full"),
                ((rows, model), LOW, "full"),
            ],
            left.scratch() + right.scratch() + [pltpu.VMEM((rows, model), F32)],
            8e9,
            "attention_forward",
        )
        left, right = feed_weights[layer]
        unit_in, before_two, resid, low = run(
            partial(feed_forward, layer, left, right),
            groups,
            info,
            [(middle, "full"), (middle_low, "full"), (small, "group"), (vec, "full")]
            + left.operands()
            + right.operands(),
            [
                ((groups, rows, units), LOW, "group"),
                ((rows, model), F32, "full"),
                ((rows, model), F32, "full"),
                ((rows, model), LOW, "full"),
            ],
            left.scratch() + right.scratch() + [pltpu.VMEM((rows, model), F32)],
            5e9,
            "feed_forward",
        )
        records.append((xwin, kv, query, ctx, lse, gated, before_one, middle_low, unit_in, before_two))
        lows.append(low)
        if layer + 1 < layers:
            pair = lax.ppermute(low, "head", [(i, i ^ 1) for i in range(groups)])
            mid = lax.ppermute(
                lax.dynamic_slice(low, (mid_row, 0), (mid_rows, model)), "head", [(1, 2), (2, 1)]
            )
            odd = h % 2 == 1
            ahead = jnp.where(odd, pair, low)
            behind = jnp.where(odd, low, pair)
            xwin = jnp.where(
                h < 2, jnp.concatenate([ahead, behind, mid]), jnp.concatenate([mid, ahead, behind])
            )
    back, loss, map_keep, map_send = run(
        partial(match_teacher, layers, map_gathered),
        groups,
        info,
        [(low, "full") for low in lows]
        + [(target, "group"), (row_ok, "full"), (factor, "full")]
        + map_gathered.operands(),
        [
            ((layers, rows, model), F32, "full"),
            ((8, 256), F32, "full"),
            ((groups, half, width), LOW, "group"),
            ((groups, half, width), LOW, "group"),
        ],
        map_gathered.scratch(),
        4e9,
        "match_teacher",
    )
    info_place = jnp.stack([h]).astype(jnp.int32)

    def place_all(value, dtype):
        pieces = [value] + [pull_group(value, r) for r in range(1, groups)]
        return pl.pallas_call(
            partial(place_rows, groups),
            name="place_rows",
            grid_spec=pltpu.PrefetchScalarGridSpec(
                num_scalar_prefetch=1,
                grid=(groups,),
                in_specs=[full(piece) for piece in pieces] + [full(matrix)],
                out_specs=pl.BlockSpec((rows, model), lambda r, info: (lax.rem(info[0] + r, groups), 0)),
            ),
            out_shape=jax.ShapeDtypeStruct((tokens_dev, model), dtype),
            compiler_params=pltpu.CompilerParams(vmem_limit_bytes=VMEM_LIMIT),
            cost_estimate=pl.CostEstimate(
                flops=2 * tokens_dev * model * model, bytes_accessed=8 * tokens_dev * model, transcendentals=0
            ),
        )(info_place, *pieces, matrix)

    block_out = place_all(lows[-1], LOW)

    grads = [(cotangent, "full"), (back[layers - 1], "full")]
    results = [None] * layers
    for layer in reversed(range(layers)):
        xwin, kv, query, ctx, lse, gated, before_one, middle_low, unit_in, before_two = records[layer]
        left, right = feed_weights[layer]
        inner_keep, inner_send, outer_keep, outer_send, attn, grad_before, vec_out, unit_vec = run(
            partial(feed_backward, layer, layer == layers - 1, left, right),
            groups,
            info,
            [
                (before_two, "full"),
                (before_one, "full"),
                (middle_low, "full"),
                (unit_in, "group"),
                (small, "group"),
                (vec, "full"),
            ]
            + grads
            + left.operands()
            + right.operands(),
            [((groups, half, units), LOW, "group")] * 4
            + [
                ((rows, model), LOW, "full"),
                ((rows, model), F32, "full"),
                ((8, model), F32, "full"),
                ((groups, 8, units), F32, "group"),
            ],
            left.scratch() + right.scratch() + [pltpu.VMEM((rows, model), F32), pltpu.VMEM((rows, model), LOW)],
            10e9,
            "feed_backward",
        )
        grad_inner = scatter(inner_keep, inner_send, False)
        grad_outer = scatter(outer_keep, outer_send, True)
        left, right = attn_weights[layer]
        extra = [(back[layer - 1 : layer], "full")] if layer else []
        left_keep, left_send, right_keep, right_send, mine, to_pair, to_mid, head_vec = run(
            partial(attention_backward, size, layer, bool(layer), left, right),
            groups,
            info,
            [
                (attn, "full"),
                (grad_before, "full"),
                (xwin, "full"),
                (query, "group"),
                (kv, "group"),
                (ctx, "group"),
                (lse, "group"),
                (gated, "group"),
                (small, "group"),
            ]
            + extra
            + left.operands()
            + right.operands(),
            [((groups, half, 2 * width), LOW, "group")] * 4
            + [
                ((rows, model), F32, "full"),
                ((rows, model), LOW, "full"),
                ((mid_rows, model), LOW, "full"),
                ((groups, 8, units), F32, "group"),
            ],
            left.scratch()
            + right.scratch()
            + [
                pltpu.VMEM((2 * seq_len, 2 * width), F32),
                pltpu.VMEM((rows, width), F32),
                pltpu.VMEM((2 * seq_len, model), F32),
                pltpu.VMEM((rows, model), F32),
            ],
            12e9,
            "attention_backward",
        )
        from_pair = lax.ppermute(to_pair, "head", [(i, i ^ 1) for i in range(groups)])
        from_mid = lax.ppermute(to_mid, "head", [(1, 2), (2, 1)])
        grads = [(mine, "full"), (from_pair, "full"), (from_mid, "full")]
        grad_kv = scatter(left_keep, left_send, False)
        grad_qo = scatter(right_keep, right_send, True)
        results[layer] = (grad_inner, grad_outer, grad_kv, grad_qo, vec_out, unit_vec, head_vec)
    grad_map = scatter(map_keep, map_send, False)
    grad_in = mine + from_pair.astype(F32)
    patch = lax.dynamic_slice(grad_in, (mid_row, 0), (mid_rows, model)) + from_mid.astype(F32)
    grad_in = lax.dynamic_update_slice(grad_in, patch, (mid_row, 0)).astype(LOW)
    grad_hidden = place_all(grad_in, F32)

    by_feature = jnp.concatenate([results[layer][4][:6] for layer in range(layers)])
    by_feature = jnp.take(by_feature.reshape(6 * layers, ndp, feats), place, axis=1)
    by_feature = by_feature.reshape(6 * layers, model)
    loss_row = jnp.concatenate([loss[:1], jnp.zeros((1, model - loss.shape[1]), F32)], 1)
    by_feature = sum_groups(jnp.concatenate([by_feature, loss_row]))
    by_unit = jnp.concatenate(
        [jnp.concatenate([results[layer][5][:, :2], results[layer][6][:, :2]], 1) for layer in range(layers)], 1
    )
    summed = by_unit[0]
    for r in range(1, groups):
        summed = summed + push_group(by_unit[r], r)
    everything = sum_plane(jnp.concatenate([by_feature, summed]))
    distill_loss = jnp.sum(everything[6 * layers]) / (count_all[0, 0] * model * layers)
    by_unit = everything[6 * layers + 1 :].reshape(layers, 4, units)
    mine_feats = lax.dynamic_slice(
        everything[: 6 * layers].reshape(layers, 3, 2, model), (0, 0, 0, dp * feats), (layers, 3, 2, feats)
    )
    unit_count = units // ndp
    mine_units = lax.dynamic_slice(by_unit[:, :2], (0, 0, dp * unit_count), (layers, 2, unit_count))
    own_slope = lax.dynamic_slice(unit_slope, (0, dp * unit_count), (layers, unit_count))
    qv_cols = width // ndp
    both = jnp.stack([by_unit[:, 2, :width], by_unit[:, 2, 3 * width : 4 * width]], 1)
    grad_qv_bias = lax.dynamic_slice(both, (0, 0, dp * qv_cols), (layers, 2, qv_cols))
    head_sums = jnp.sum(by_unit[:, 3, :width].reshape(layers, heads, head_size), -1)

    def stacked(member, cols, turned=False):
        arrays = [results[layer][member][:, cols] for layer in range(layers)]
        return jnp.stack([array.T if turned else array for array in arrays])

    front, rear, whole = slice(0, width), slice(width, 2 * width), slice(None)
    return (
        block_out,
        grad_hidden,
        distill_loss,
        stacked(3, front),
        stacked(2, front),
        stacked(2, rear),
        grad_qv_bias,
        stacked(3, rear, True),
        mine_feats[:, 0],
        mine_feats[:, 1],
        mine_feats[:, 2],
        stacked(0, whole),
        mine_units[:, 0],
        stacked(1, whole, True),
        head_sums * head_slope,
        mine_units[:, 1] * own_slope,
        grad_map,
    )


def solution(mesh):
    in_specs = (
        P("dp", None),
        P("dp"),
        P(),
        P(None, "dp", "head"),
        P("dp", None),
        P(None, None, "head"),
        P(None, None, "head"),
        P(None, None, "head"),
        P(None, None, "head"),
        P(None, "head", None),
        P(),
        P(),
        P(),
        P(None, None, "head"),
        P(None, "head"),
        P(None, "head", None),
        P(None, "head"),
        P(None, "head"),
        P(None, "head"),
        P(None, "head"),
        P(None, "head"),
    )
    out_specs = (
        P("dp", None),
        P("dp", None),
        P(),
        P(None, "dp", "head"),
        P(None, "dp", "head"),
        P(None, "dp", "head"),
        P(None, None, ("head", "dp")),
        P(None, "head", "dp"),
        P(None, None, "dp"),
        P(None, None, "dp"),
        P(None, None, "dp"),
        P(None, "dp", "head"),
        P(None, ("head", "dp")),
        P(None, "head", "dp"),
        P(None, "head"),
        P(None, ("head", "dp")),
        P("dp", "head"),
    )
    return jax.shard_map(
        partial(on_device, mesh.shape["dp"], mesh.shape["head"]),
        mesh=mesh,
        in_specs=in_specs,
        out_specs=out_specs,
        check_vma=False,
    )
```

time: 1790 us -> 862 us (0.48)
  waiting for transfers between devices: 1290 us -> 283 us
  Pallas kernels: 0 us -> 217 us
  starting transfers between devices: 3.2 us -> 169 us
  matrix products: 174 us -> 25.1 us
  blocking collectives: 89.4 us -> 0 us
  other arithmetic: 115 us -> 73.5 us
  between operations: 26.9 us -> 6.98 us
    psum x9 -> x0, waiting for transfers between devices: 768 us -> none  [the longest x5 409 us: head_total(): return lax.psum(grad_part.astype(jnp.bfloat16), 'head').astype(jnp.float32)]
    unnamed x42 -> x0, waiting for transfers between devices: 368 us -> none
    ppermute x0 -> x153, waiting for transfers between devices: none -> 283 us  [the longest x33 107 us: pull_group(): lax.ppermute(value, 'head', [((i + r) % groups, i) for i in range(groups)])]
    pallas_call x0 -> x11, Pallas kernels: none -> 217 us  [the longest x9 205 us: run(): pl.pallas_call(body, name=name, grid_spec=pltpu.PrefetchScalarGridSpec(nu...]
    ppermute x0 -> x153, starting transfers between devices: none -> 169 us  [the longest x33 61.4 us: pull_group(): lax.ppermute(value, 'head', [((i + r) % groups, i) for i in range(groups)])]
    reduce_scatter x5 -> x0, waiting for transfers between devices: 158 us -> none  [the longest x2 79.3 us: on_device(): lax.psum_scatter(grad_outer.astype(jnp.bfloat16), 'dp', scatter_dimension...]
    dot_general x54 -> x13, matrix products: 174 us -> 25.1 us  [product(): lax.dot_general(left, right, ((dims[:1], dims[1:]), ((), ())), preferred_...]
    reduce_sum x22 -> x3, other arithmetic: 84.8 us -> 1.33 us  [the longest x1 0.63 us: on_device(): count_all = sum_plane(jnp.sum(seq_lengths).astype(F32).reshape(1, 1))]
  transfers between devices with their start and end apart: 28 -> 153, of which waited for: 24 -> 51; matrix products, arithmetic and copies ran while one was open for 10% -> 19% of each run, Pallas kernels for 0% -> 26%
where the time goes in v1:
time: 862 us; the launch traced here: 849 us
  waiting for transfers between devices  283 us (33%)
  Pallas kernels  217 us (25%)
  starting transfers between devices  169 us (20%)
  local copies, waits for them, and re-layouts  75.1 us (9%)
  other arithmetic  73.5 us (9%)
  matrix products  25.1 us (3%)
    pallas_call x9, Pallas kernels, run(): pl.pallas_call(body, name=name, grid_spec=pltpu.PrefetchScalarGridSpec(nu...  205 us
    ppermute x33, waiting for transfers between devices, pull_group(): lax.ppermute(value, 'head', [((i + r) % groups, i) for i in range(groups)])  107 us
    ppermute x18, waiting for transfers between devices, push(): lax.ppermute(value, 'dp', [(i, relative(i, c, y, x)) for i in range(ndp)])  67.1 us
    ppermute x33, starting transfers between devices, pull_group(): lax.ppermute(value, 'head', [((i + r) % groups, i) for i in range(groups)])  61.4 us
    ppermute x30, waiting for transfers between devices, push_group(): lax.ppermute(value, 'head', [(i, (i + r) % groups) for i in range(groups)])  43.7 us
    ppermute x58, waiting for transfers between devices, pull(): lax.ppermute(value, 'dp', [(relative(i, c, y, x), i) for i in range(ndp)])  41 us
    ppermute x30, starting transfers between devices, push_group(): lax.ppermute(value, 'head', [(i, (i + r) % groups) for i in range(groups)])  40.2 us
    ppermute x58, starting transfers between devices, pull(): lax.ppermute(value, 'dp', [(relative(i, c, y, x), i) for i in range(ndp)])  27.3 us
  transfers between devices with their start and end apart: 153, of which 51 were waited for; matrix products, arithmetic and copies ran while one was open for 19% of the time, Pallas kernels for 26%

profile of v1, /device:TPU:0, one launch (start us, length us, event | category | flops | bytes accessed | tf_op | source)
XLA Modules:
  0.0 849.3 jit_solution(15905335459982034120)
XLA Ops:
  6.5 5.0 collective-permute-start
  22.3 3.7 fusion.17.refs_13_.refs_18_
  73.8 3.9 collective-permute-start.5
  79.3 6.9 collective-permute-done.4
  96.3 3.9 concatenate.62.refs_13_.refs_17_.refs_19_
  113.1 3.3 collective-permute-start.55
  122.8 24.6 %collective-permute-done.56 = bf16[96,1152]{1,0:T(8,128)(2,1)S(1)} collective-permute-done((bf16[96,1152]{1,0:T(8,128)(2,1)S(1)}, bf16[96,1152]{1,0:T(8,128)(2,1)S(1)}, u32[]{:S(2)}, u32[]{:S(2)}) %collective-permute-start.56) | collective-permute-done | bytes 221216 | tf_op jit(solution)/shard_map/ppermute | solution.py:541
  147.5 3.9 collective-permute-done.46
  168.0 4.1 collective-permute-done.77.refs_7_
  173.3 13.3 %collective-permute-done.78.refs_8_ = bf16[3,96,192]{2,1,0:T(8,128)(2,1)S(1)} collective-permute-done((bf16[3,96,192]{2,1,0:T(8,128)(2,1)}, bf16[3,96,192]{2,1,0:T(8,128)(2,1)S(1)}, u32[]{:S(2)}, u32[]{:S(2)}) %collective-permute-start.78) | collective-permute-done | bytes 110624 | tf_op jit(solution)/shard_map/ppermute | solution.py:535
  194.5 3.1 collective-permute-done.79.refs_9_
  201.6 22.5 %collective-permute-done.70 = bf16[2,384,192]{2,1,0:T(8,128)(2,1)S(1)} collective-permute-done((bf16[2,384,192]{2,1,0:T(8,128)(2,1)}, bf16[2,384,192]{2,1,0:T(8,128)(2,1)S(1)}, u32[]{:S(2)}, u32[]{:S(2)}) %collective-permute-start.70) | collective-permute-done | bytes 294944 | tf_op jit(solution)/shard_map/ppermute | solution.py:541
  234.0 6.2 collective-permute-done.59.refs_16_.refs_20_.refs_22_
  242.4 24.7 %attention_forward.2 = (bf16[4,1024,384]{2,1,0:T(8,128)(2,1)}, bf16[4,384,192]{2,1,0:T(8,128)(2,1)}, f32[4,384,192]{2,1,0:T(8,128)}, f32[4,384,128]{2,1,0:T(8,12...) custom-call(s32[10]{0:T(128)} %concatenate.52.info, ...), custom_call_target="tpu_custom_call" | custom-call | flops 8000000000 | bytes 6438912 | tf_op jit(solution)/shard_map/attention_forward/pallas_call | solution.py:56
  268.0 12.8 %feed_forward.2 = (bf16[4,384,768]{2,1,0:T(8,128)(2,1)}, f32[384,768]{1,0:T(8,128)}, f32[384,768]{1,0:T(8,128)}, bf16[384,768]{1,0:T(8,128)(2,1)}) custom-call(s32[10]{0:T(128)} %concatenate.52.info, f32[384,768]{1,0:T(8,128)} %get-tuple-element.97.refs_0_, bf16[384,768]{1,0:T(8,128)(2,1)} %get-tuple-element.98.refs_1_.refs_2_, ...), custom_call_target="tpu_custom_call" | custom-call | flops 5000000000 | bytes 11354112 | tf_op jit(solution)/shard_map/feed_forward/pallas_call | solution.py:56
  288.3 10.2 %collective-permute-done.60.refs_17_.refs_21_.refs_23_ = bf16[3,96,1152]{2,1,0:T(8,128)(2,1)} collective-permute-done((bf16[3,96,1152]{2,1,0:T(8,128)(2,1)}, bf16[3,96,1152]{2,1,0:T(8,128)(2,1)}, u32[]{:S(2)}, u32[]{:S(2)}) %collective-permute-start.60) | collective-permute-done | bytes 663584 | tf_op jit(solution)/shard_map/ppermute | solution.py:535
  305.4 25.1 %attention_forward.3 = (bf16[4,1024,384]{2,1,0:T(8,128)(2,1)}, bf16[4,384,192]{2,1,0:T(8,128)(2,1)}, f32[4,384,192]{2,1,0:T(8,128)}, f32[4,384,128]{2,1,0:T(8,12...) custom-call(s32[10]{0:T(128)} %concatenate.52.info, ...), custom_call_target="tpu_custom_call" | custom-call | flops 8000000000 | bytes 17055744 | tf_op jit(solution)/shard_map/attention_forward/pallas_call | solution.py:56
  330.5 12.7 %feed_forward.3 = (bf16[4,384,768]{2,1,0:T(8,128)(2,1)}, f32[384,768]{1,0:T(8,128)}, f32[384,768]{1,0:T(8,128)}, bf16[384,768]{1,0:T(8,128)(2,1)}) custom-call(s32[10]{0:T(128)} %concatenate.52.info, f32[384,768]{1,0:T(8,128)} %get-tuple-element.105.refs_0_, bf16[384,768]{1,0:T(8,128)(2,1)} %get-tuple-element.106.refs_1_.refs_2_, ...), custom_call_target="tpu_custom_call" | custom-call | flops 5000000000 | bytes 16072704 | tf_op jit(solution)/shard_map/feed_forward/pallas_call | solution.py:56
  345.4 11.0 %match_teacher.1 = (f32[2,384,768]{2,1,0:T(8,128)}, f32[8,256]{1,0:T(8,128)}, bf16[4,384,192]{2,1,0:T(8,128)(2,1)}, bf16[4,384,192]{2,1,0:T(8,128)(2,1)}) custom-call(s32[10]{0:T(128)} %concatenate.52.info, bf16[384,768]{1,0:T(8,128)(2,1)} %get-tuple-element.101.refs_0_, bf16[384,768]{1,0:T(8,128)(2,1)} %get-tuple-element.107.refs_0_.refs_1_, ...), custom_call_target="tpu_custom_call" | custom-call | flops 4000000000 | bytes 3735556 | tf_op jit(solution)/shard_map/match_teacher/pallas_call | solution.py:56
  357.9 3.2 fusion.188
  361.1 21.2 %feed_backward.2 = (bf16[4,384,768]{2,1,0:T(8,128)(2,1)}, bf16[4,384,768]{2,1,0:T(8,128)(2,1)}, bf16[4,384,768]{2,1,0:T(8,128)(2,1)}, bf16[4,384,768]{2,1,0:T(8,...) custom-call(s32[10]{0:T(128)} %concatenate.52.info, ...), custom_call_target="tpu_custom_call" | custom-call | flops 10000000000 | bytes 21381120 | tf_op jit(solution)/shard_map/feed_backward/pallas_call | solution.py:56
  382.4 38.4 %attention_backward.2 = (bf16[4,384,384]{2,1,0:T(8,128)(2,1)}, bf16[4,384,384]{2,1,0:T(8,128)(2,1)}, bf16[4,384,384]{2,1,0:T(8,128)(2,1)}, bf16[4,384,384]{2,1,0...) custom-call(s32[10]{0:T(128)} %concatenate.52.info, ...), custom_call_target="tpu_custom_call" | custom-call | flops 12000000000 | bytes 25067520 | tf_op jit(solution)/shard_map/attention_backward/pallas_call | solution.py:56
  437.2 21.4 %feed_backward.3 = (bf16[4,384,768]{2,1,0:T(8,128)(2,1)}, bf16[4,384,768]{2,1,0:T(8,128)(2,1)}, bf16[4,384,768]{2,1,0:T(8,128)(2,1)}, bf16[4,384,768]{2,1,0:T(8,...) custom-call(s32[10]{0:T(128)} %concatenate.52.info, ...), custom_call_target="tpu_custom_call" | custom-call | flops 10000000000 | bytes 17055744 | tf_op jit(solution)/shard_map/feed_backward/pallas_call | solution.py:56
  462.8 4.0 collective-permute-start.91
  466.8 37.8 %attention_backward.3 = (bf16[4,384,384]{2,1,0:T(8,128)(2,1)}, bf16[4,384,384]{2,1,0:T(8,128)(2,1)}, bf16[4,384,384]{2,1,0:T(8,128)(2,1)}, bf16[4,384,384]{2,1,0...) custom-call(s32[10]{0:T(128)} %concatenate.52.info, ...), custom_call_target="tpu_custom_call" | custom-call | flops 12000000000 | bytes 14450688 | tf_op jit(solution)/shard_map/attention_backward/pallas_call | solution.py:56
  514.0 15.9 %collective-permute-done.92 = f32[13,768]{1,0:T(8,128)S(1)} collective-permute-done((f32[13,768]{1,0:T(8,128)S(1)}, f32[13,768]{1,0:T(8,128)S(1)}, u32[]{:S(2)}, u32[]{:S(2)}) %collective-permute-start.92) | collective-permute-done | bytes 39968 | tf_op jit(solution)/shard_map/ppermute | solution.py:558
  539.5 5.6 place_rows.2
  546.9 3.9 collective-permute-done.98
  558.2 3.5 collective-permute-done.149
  564.9 4.5 collective-permute-done.150
  579.6 19.5 %collective-permute-start.89 = (bf16[384,768]{1,0:T(8,128)(2,1)S(1)}, bf16[384,768]{1,0:T(8,128)(2,1)S(1)}, u32[]{:S(2)}, u32[]{:S(2)}) collective-permute-start(bf16[384,768]{1,0:T(8,128)(2,1)S(1)} %convert_element_type.1177.refs_0_), channel_id=1, source_target_pairs={{2,0},{3,1},{0,2},{1,3},{6,4},{7,5},{4,6},{5,7},{10,8},{11,9},{8,1... | collective-permute-start | bytes 1769480 | tf_op jit(solution)/shard_map/ppermute | solution.py:541
  610.2 39.7 %collective-permute-done.89.refs_2_ = bf16[384,768]{1,0:T(8,128)(2,1)S(1)} collective-permute-done((bf16[384,768]{1,0:T(8,128)(2,1)S(1)}, bf16[384,768]{1,0:T(8,128)(2,1)S(1)}, u32[]{:S(2)}, u32[]{:S(2)}) %collective-permute-start.89) | collective-permute-done | bytes 589856 | tf_op jit(solution)/shard_map/ppermute | solution.py:541
  653.1 6.1 place_rows.3
  660.8 3.6 collective-permute-done.118
  673.8 3.7 collective-permute-start.110
  688.0 3.5 collective-permute-done.122
  700.2 9.1 %collective-permute-done.112 = bf16[4,2,96,384]{3,2,1,0:T(8,128)(2,1)S(1)} collective-permute-done((bf16[4,2,96,384]{3,2,1,0:T(8,128)(2,1)S(1)}, bf16[4,2,96,384]{3,2,1,0:T(8,128)(2,1)S(1)}, u32[]{:S(2)}, u32[]{:S(2)}) %collective-permute-start.112) | collective-permute-done | bytes 589856 | tf_op jit(solution)/shard_map/ppermute | solution.py:538
  711.6 3.6 collective-permute-done.101
  724.2 3.7 collective-permute-start.116
  742.6 15.2 %collective-permute-done.142 = bf16[4,2,96,768]{3,2,1,0:T(8,128)(2,1)} collective-permute-done((bf16[4,2,96,768]{3,2,1,0:T(8,128)(2,1)}, bf16[4,2,96,768]{3,2,1,0:T(8,128)(2,1)}, u32[]{:S(2)}, u32[]{:S(2)}) %collective-permute-start.142) | collective-permute-done | bytes 1179680 | tf_op jit(solution)/shard_map/ppermute | solution.py:538
  764.9 18.1 %collective-permute-done.136 = bf16[4,2,96,768]{3,2,1,0:T(8,128)(2,1)S(1)} collective-permute-done((bf16[4,2,96,768]{3,2,1,0:T(8,128)(2,1)S(1)}, bf16[4,2,96,768]{3,2,1,0:T(8,128)(2,1)S(1)}, u32[]{:S(2)}, u32[]{:S(2)}) %collective-permute-start.136) | collective-permute-done | bytes 1179680 | tf_op jit(solution)/shard_map/ppermute | solution.py:538
  784.4 13.9 %collective-permute-done.143 = bf16[4,96,768]{2,1,0:T(8,128)(2,1)S(1)} collective-permute-done((bf16[4,96,768]{2,1,0:T(8,128)(2,1)S(1)}, bf16[4,96,768]{2,1,0:T(8,128)(2,1)S(1)}, u32[]{:S(2)}, u32[]{:S(2)}) %collective-permute-start.143) | collective-permute-done | bytes 589856 | tf_op jit(solution)/shard_map/ppermute | solution.py:538
  800.0 3.3 collective-permute-start.145
  808.2 5.5 collective-permute-done.145
  813.8 3.5 collective-permute-start.134
  818.4 4.9 collective-permute-done.133
  826.8 5.9 collective-permute-start.138
  842.5 4.4 collective-permute-done.127
  (736 shorter events, 314.2 us)
Async XLA Ops:
  6.5 57.6 %collective-permute-start = (f32[8,768]{1,0:T(8,128)}, f32[8,768]{1,0:T(8,128)}, u32[]{:S(2)}, u32[]{:S(2)}) collective-permute-start(f32[8,768]{1,0:T(8,128)} %reshape.949), channel_id=1, source_target_pairs={{1,0},{2,1},{3,2},{0,3},{5,4},{6,5},{7,6},{4,7},{9,8},{10,9},{11,1... | collective-permute-start | bytes 73736 | tf_op jit(solution)/shard_map/ppermute | solution.py:541
  11.5 54.4 %collective-permute-start.1 = (f32[8,768]{1,0:T(8,128)}, f32[8,768]{1,0:T(8,128)}, u32[]{:S(2)}, u32[]{:S(2)}) collective-permute-start(f32[8,768]{1,0:T(8,128)} %reshape.949), channel_id=1, source_target_pairs={{2,0},{3,1},{0,2},{1,3},{6,4},{7,5},{4,6},{5,7},{10,8},{11,9},{8,1... | collective-permute-start | bytes 73736 | tf_op jit(solution)/shard_map/ppermute | solution.py:541
  11.5 56.4 %collective-permute-start.2 = (f32[8,768]{1,0:T(8,128)}, f32[8,768]{1,0:T(8,128)}, u32[]{:S(2)}, u32[]{:S(2)}) collective-permute-start(f32[8,768]{1,0:T(8,128)} %reshape.949), channel_id=1, source_target_pairs={{3,0},{0,1},{1,2},{2,3},{7,4},{4,5},{5,6},{6,7},{11,8},{8,9},{9,10... | collective-permute-start | bytes 73736 | tf_op jit(solution)/shard_map/ppermute | solution.py:541
  17.3 50.7 %collective-permute-start.13 = (bf16[96,384]{1,0:T(8,128)(2,1)}, bf16[96,384]{1,0:T(8,128)(2,1)}, u32[]{:S(2)}, u32[]{:S(2)}) collective-permute-start(bf16[96,384]{1,0:T(8,128)(2,1)} %fusion.141), channel_id=1, source_target_pairs={{1,0},{2,1},{3,2},{0,3},{5,4},{6,5},{7,6},{4,7},{9,8},{10,9},{11,1... | collective-permute-start | bytes 221192 | tf_op jit(solution)/shard_map/ppermute | solution.py:541
  21.4 29.5 %collective-permute-start.72 = (f32[1,1]{1,0:T(1,128)}, f32[1,1]{1,0:T(1,128)}, u32[]{:S(2)}, u32[]{:S(2)}) collective-permute-start(f32[1,1]{1,0:T(1,128)} %bitcast.54), channel_id=1, source_target_pairs={{0,4},{4,0},{8,12},{12,8},{16,20},{20,16},{24,28},{28,24},{1,5},{5... | collective-permute-start | bytes 20 | tf_op jit(solution)/shard_map/ppermute | solution.py:551
  116.4 31.1 %collective-permute-start.56 = (bf16[96,1152]{1,0:T(8,128)(2,1)S(1)}, bf16[96,1152]{1,0:T(8,128)(2,1)S(1)}, u32[]{:S(2)}, u32[]{:S(2)}) collective-permute-start(bf16[96,1152]{1,0:T(8,128)(2,1)S(1)} %copy-done.56), channel_id=1, source_target_pairs={{2,0},{3,1},{0,2},{1,3},{6,4},{7,5},{4,6},{5,7},{10,8},{11,9},{8,1... | collective-permute-start | bytes 663560 | tf_op jit(solution)/shard_map/ppermute | solution.py:541
  117.4 30.0 %collective-permute-start.57 = (bf16[96,1152]{1,0:T(8,128)(2,1)S(1)}, bf16[96,1152]{1,0:T(8,128)(2,1)S(1)}, u32[]{:S(2)}, u32[]{:S(2)}) collective-permute-start(bf16[96,1152]{1,0:T(8,128)(2,1)S(1)} %copy-done.56), channel_id=1, source_target_pairs={{3,0},{0,1},{1,2},{2,3},{7,4},{4,5},{5,6},{6,7},{11,8},{8,9},{9,10... | collective-permute-start | bytes 663560 | tf_op jit(solution)/shard_map/ppermute | solution.py:541
  117.7 33.7 %collective-permute-start.46 = (bf16[96,1152]{1,0:T(8,128)(2,1)S(1)}, bf16[96,1152]{1,0:T(8,128)(2,1)S(1)}, u32[]{:S(2)}, u32[]{:S(2)}) collective-permute-start(bf16[96,1152]{1,0:T(8,128)(2,1)S(1)} %copy-done.59), channel_id=1, source_target_pairs={{2,0},{3,1},{0,2},{1,3},{6,4},{7,5},{4,6},{5,7},{10,8},{11,9},{8,1... | collective-permute-start | bytes 663560 | tf_op jit(solution)/shard_map/ppermute | solution.py:541
  119.4 32.0 %collective-permute-start.47 = (bf16[96,1152]{1,0:T(8,128)(2,1)S(1)}, bf16[96,1152]{1,0:T(8,128)(2,1)S(1)}, u32[]{:S(2)}, u32[]{:S(2)}) collective-permute-start(bf16[96,1152]{1,0:T(8,128)(2,1)S(1)} %copy-done.59), channel_id=1, source_target_pairs={{3,0},{0,1},{1,2},{2,3},{7,4},{4,5},{5,6},{6,7},{11,8},{8,9},{9,10... | collective-permute-start | bytes 663560 | tf_op jit(solution)/shard_map/ppermute | solution.py:541
  122.3 37.5 %collective-permute-start.18 = (bf16[3,96,384]{2,1,0:T(8,128)(2,1)}, bf16[3,96,384]{2,1,0:T(8,128)(2,1)}, u32[]{:S(2)}, u32[]{:S(2)}) collective-permute-start(bf16[3,96,384]{2,1,0:T(8,128)(2,1)} %collective-permute-done.17.refs_15_.refs_21_), channel_id=1, source_target_pairs={{8,0},{12,4},{0,8},{4,12},{24,16},{28,20},{16,24},{20,28},{9,1},{1... | collective-permute-start | bytes 663560 | tf_op jit(solution)/shard_map/ppermute | solution.py:535
  154.1 32.5 %collective-permute-start.26 = (bf16[3,96,768]{2,1,0:T(8,128)(2,1)}, bf16[3,96,768]{2,1,0:T(8,128)(2,1)}, u32[]{:S(2)}, u32[]{:S(2)}) collective-permute-start(bf16[3,96,768]{2,1,0:T(8,128)(2,1)} %pad_maximum_fusion.7.refs_5_.refs_10_), channel_id=1, source_target_pairs={{8,0},{12,4},{0,8},{4,12},{24,16},{28,20},{16,24},{20,28},{9,1},{1... | collective-permute-start | bytes 1327112 | tf_op jit(solution)/shard_map/ppermute | solution.py:535
  190.6 33.5 %collective-permute-start.70 = (bf16[2,384,192]{2,1,0:T(8,128)(2,1)}, bf16[2,384,192]{2,1,0:T(8,128)(2,1)S(1)}, u32[]{:S(2)}, u32[]{:S(2)}) collective-permute-start(bf16[2,384,192]{2,1,0:T(8,128)(2,1)} %get-tuple-element.116), channel_id=1, source_target_pairs={{2,0},{3,1},{0,2},{1,3},{6,4},{7,5},{4,6},{5,7},{10,8},{11,9},{8,1... | collective-permute-start | bytes 884744 | tf_op jit(solution)/shard_map/ppermute | solution.py:541
  197.6 28.4 %collective-permute-start.71 = (bf16[2,384,192]{2,1,0:T(8,128)(2,1)}, bf16[2,384,192]{2,1,0:T(8,128)(2,1)S(1)}, u32[]{:S(2)}, u32[]{:S(2)}) collective-permute-start(bf16[2,384,192]{2,1,0:T(8,128)(2,1)} %get-tuple-element.117), channel_id=1, source_target_pairs={{3,0},{0,1},{1,2},{2,3},{7,4},{4,5},{5,6},{6,7},{11,8},{8,9},{9,10... | collective-permute-start | bytes 884744 | tf_op jit(solution)/shard_map/ppermute | solution.py:541
  198.2 27.8 %collective-permute-start.28 = (bf16[3,96,768]{2,1,0:T(8,128)(2,1)}, bf16[3,96,768]{2,1,0:T(8,128)(2,1)S(1)}, u32[]{:S(2)}, u32[]{:S(2)}) collective-permute-start(bf16[3,96,768]{2,1,0:T(8,128)(2,1)} %collective-permute-done.26.refs_6_.refs_11_), channel_id=1, source_target_pairs={{16,0},{20,4},{24,8},{28,12},{0,16},{4,20},{8,24},{12,28},{17,1},{... | collective-permute-start | bytes 1327112 | tf_op jit(solution)/shard_map/ppermute | solution.py:535
  199.5 27.2 %collective-permute-start.30 = (bf16[3,96,768]{2,1,0:T(8,128)(2,1)}, bf16[3,96,768]{2,1,0:T(8,128)(2,1)S(1)}, u32[]{:S(2)}, u32[]{:S(2)}) collective-permute-start(bf16[3,96,768]{2,1,0:T(8,128)(2,1)} %collective-permute-done.26.refs_6_.refs_11_), channel_id=1, source_target_pairs={{4,0},{0,4},{12,8},{8,12},{20,16},{16,20},{28,24},{24,28},{5,1},{1... | collective-permute-start | bytes 1327112 | tf_op jit(solution)/shard_map/ppermute | solution.py:535
  231.8 48.9 %collective-permute-start.58 = (bf16[3,96,1152]{2,1,0:T(8,128)(2,1)S(1)}, bf16[3,96,1152]{2,1,0:T(8,128)(2,1)}, u32[]{:S(2)}, u32[]{:S(2)}) collective-permute-start(bf16[3,96,1152]{2,1,0:T(8,128)(2,1)S(1)} %pad_maximum_fusion.3.refs_14_.refs_18_.refs_20_), channel_id=1, source_target_pairs={{8,0},{12,4},{0,8},{4,12},{24,16},{28,20},{16,24},{20,28},{9,1},{1... | collective-permute-start | bytes 1990664 | tf_op jit(solution)/shard_map/ppermute | solution.py:535
  232.7 49.2 %collective-permute-start.61 = (bf16[3,96,1152]{2,1,0:T(8,128)(2,1)S(1)}, bf16[3,96,1152]{2,1,0:T(8,128)(2,1)S(1)}, u32[]{:S(2)}, u32[]{:S(2)}) collective-permute-start(bf16[3,96,1152]{2,1,0:T(8,128)(2,1)S(1)} %pad_maximum_fusion.3.refs_14_.refs_18_.refs_20_), channel_id=1, source_target_pairs={{4,0},{0,4},{12,8},{8,12},{20,16},{16,20},{28,24},{24,28},{5,1},{1... | collective-permute-start | bytes 1990664 | tf_op jit(solution)/shard_map/ppermute | solution.py:535
  232.7 48.9 %collective-permute-start.48 = (bf16[3,96,1152]{2,1,0:T(8,128)(2,1)S(1)}, bf16[3,96,1152]{2,1,0:T(8,128)(2,1)}, u32[]{:S(2)}, u32[]{:S(2)}) collective-permute-start(bf16[3,96,1152]{2,1,0:T(8,128)(2,1)S(1)} %pad_maximum_fusion.2.refs_5_.refs_9_.refs_11_), channel_id=1, source_target_pairs={{8,0},{12,4},{0,8},{4,12},{24,16},{28,20},{16,24},{20,28},{9,1},{1... | collective-permute-start | bytes 1990664 | tf_op jit(solution)/shard_map/ppermute | solution.py:535
  240.3 43.0 %collective-permute-start.49 = (bf16[3,96,1152]{2,1,0:T(8,128)(2,1)S(1)}, bf16[3,96,1152]{2,1,0:T(8,128)(2,1)S(1)}, u32[]{:S(2)}, u32[]{:S(2)}) collective-permute-start(bf16[3,96,1152]{2,1,0:T(8,128)(2,1)S(1)} %pad_maximum_fusion.2.refs_5_.refs_9_.refs_11_), channel_id=1, source_target_pairs={{16,0},{20,4},{24,8},{28,12},{0,16},{4,20},{8,24},{12,28},{17,1},{... | collective-permute-start | bytes 1990664 | tf_op jit(solution)/shard_map/ppermute | solution.py:535
  303.3 40.4 %collective-permute-start.80 = (bf16[3,96,192]{2,1,0:T(8,128)(2,1)}, bf16[3,96,192]{2,1,0:T(8,128)(2,1)S(1)}, u32[]{:S(2)}, u32[]{:S(2)}) collective-permute-start(bf16[3,96,192]{2,1,0:T(8,128)(2,1)} %pad_maximum_fusion.15.refs_6_), channel_id=1, source_target_pairs={{4,0},{0,4},{12,8},{8,12},{20,16},{16,20},{28,24},{24,28},{5,1},{1... | collective-permute-start | bytes 331784 | tf_op jit(solution)/shard_map/ppermute | solution.py:535
  303.8 40.7 %collective-permute-start.81 = (bf16[3,96,192]{2,1,0:T(8,128)(2,1)}, bf16[3,96,192]{2,1,0:T(8,128)(2,1)S(1)}, u32[]{:S(2)}, u32[]{:S(2)}) collective-permute-start(bf16[3,96,192]{2,1,0:T(8,128)(2,1)} %collective-permute-done.77.refs_7_), channel_id=1, source_target_pairs={{4,0},{0,4},{12,8},{8,12},{20,16},{16,20},{28,24},{24,28},{5,1},{1... | collective-permute-start | bytes 331784 | tf_op jit(solution)/shard_map/ppermute | solution.py:535
  303.9 40.7 %collective-permute-start.82 = (bf16[3,96,192]{2,1,0:T(8,128)(2,1)S(1)}, bf16[3,96,192]{2,1,0:T(8,128)(2,1)S(1)}, u32[]{:S(2)}, u32[]{:S(2)}) collective-permute-start(bf16[3,96,192]{2,1,0:T(8,128)(2,1)S(1)} %copy-done.124), channel_id=1, source_target_pairs={{4,0},{0,4},{12,8},{8,12},{20,16},{16,20},{28,24},{24,28},{5,1},{1... | collective-permute-start | bytes 331784 | tf_op jit(solution)/shard_map/ppermute | solution.py:535
  304.6 40.0 %collective-permute-start.83 = (bf16[3,96,192]{2,1,0:T(8,128)(2,1)S(1)}, bf16[3,96,192]{2,1,0:T(8,128)(2,1)S(1)}, u32[]{:S(2)}, u32[]{:S(2)}) collective-permute-start(bf16[3,96,192]{2,1,0:T(8,128)(2,1)S(1)} %copy-done.126), channel_id=1, source_target_pairs={{4,0},{0,4},{12,8},{8,12},{20,16},{16,20},{28,24},{24,28},{5,1},{1... | collective-permute-start | bytes 331784 | tf_op jit(solution)/shard_map/ppermute | solution.py:535
  343.3 194.1 %collective-permute-start.65 = (bf16[384,768]{1,0:T(8,128)(2,1)}, bf16[384,768]{1,0:T(8,128)(2,1)}, u32[]{:S(2)}, u32[]{:S(2)}) collective-permute-start(bf16[384,768]{1,0:T(8,128)(2,1)} %get-tuple-element.107.refs_0_.refs_1_), channel_id=1, source_target_pairs={{1,0},{2,1},{3,2},{0,3},{5,4},{6,5},{7,6},{4,7},{9,8},{10,9},{11,1... | collective-permute-start | bytes 1769480 | tf_op jit(solution)/shard_map/ppermute | solution.py:541
  343.8 194.7 %collective-permute-start.66 = (bf16[384,768]{1,0:T(8,128)(2,1)}, bf16[384,768]{1,0:T(8,128)(2,1)}, u32[]{:S(2)}, u32[]{:S(2)}) collective-permute-start(bf16[384,768]{1,0:T(8,128)(2,1)} %get-tuple-element.107.refs_0_.refs_1_), channel_id=1, source_target_pairs={{2,0},{3,1},{0,2},{1,3},{6,4},{7,5},{4,6},{5,7},{10,8},{11,9},{8,1... | collective-permute-start | bytes 1769480 | tf_op jit(solution)/shard_map/ppermute | solution.py:541
  357.9 75.0 %collective-permute-start.147 = (bf16[4,384,192]{1,2,0:T(8,128)(2,1)S(1)}, bf16[4,384,192]{1,2,0:T(8,128)(2,1)S(1)}, u32[]{:S(2)}, u32[]{:S(2)}) collective-permute-start(bf16[4,384,192]{1,2,0:T(8,128)(2,1)S(1)} %copy.303), channel_id=1, source_target_pairs={{4,0},{0,4},{12,8},{8,12},{20,16},{16,20},{28,24},{24,28},{5,1},{1... | collective-permute-start | bytes 1769480 | tf_op jit(solution)/shard_map/ppermute | solution.py:535
  462.8 45.4 %collective-permute-start.91 = (f32[13,768]{1,0:T(8,128)S(1)}, f32[13,768]{1,0:T(8,128)S(1)}, u32[]{:S(2)}, u32[]{:S(2)}) collective-permute-start(f32[13,768]{1,0:T(8,128)S(1)} %select_maximum_fusion), channel_id=1, source_target_pairs={{0,1},{1,0},{2,3},{3,2},{4,5},{5,4},{6,7},{7,6},{8,9},{9,8},{10,11... | collective-permute-start | bytes 119816 | tf_op jit(solution)/shard_map/ppermute | solution.py:558
  512.3 86.9 %collective-permute-start.105 = (bf16[4,384,384]{2,1,0:T(8,128)(2,1)}, bf16[4,384,384]{2,1,0:T(8,128)(2,1)}, u32[]{:S(2)}, u32[]{:S(2)}) collective-permute-start(bf16[4,384,384]{2,1,0:T(8,128)(2,1)} %get-tuple-element.149), channel_id=1, source_target_pairs={{4,0},{0,4},{12,8},{8,12},{20,16},{16,20},{28,24},{24,28},{5,1},{1... | collective-permute-start | bytes 3538952 | tf_op jit(solution)/shard_map/ppermute | solution.py:535
  536.7 66.4 %collective-permute-start.117 = (bf16[4,384,384]{2,1,0:T(8,128)(2,1)}, bf16[4,384,384]{2,1,0:T(8,128)(2,1)}, u32[]{:S(2)}, u32[]{:S(2)}) collective-permute-start(bf16[4,384,384]{2,1,0:T(8,128)(2,1)} %get-tuple-element.153), channel_id=1, source_target_pairs={{4,0},{0,4},{12,8},{8,12},{20,16},{16,20},{28,24},{24,28},{5,1},{1... | collective-permute-start | bytes 3538952 | tf_op jit(solution)/shard_map/ppermute | solution.py:535
  538.4 37.6 %collective-permute-start.86 = (bf16[384,768]{1,0:T(8,128)(2,1)}, bf16[384,768]{1,0:T(8,128)(2,1)}, u32[]{:S(2)}, u32[]{:S(2)}) collective-permute-start(bf16[384,768]{1,0:T(8,128)(2,1)} %get-tuple-element.137), channel_id=1, source_target_pairs={{0,1},{1,0},{2,3},{3,2},{4,5},{5,4},{6,7},{7,6},{8,9},{9,8},{10,11... | collective-permute-start | bytes 1769480 | tf_op jit(solution)/shard_map/ppermute | solution.py:874
  570.8 95.7 %collective-permute-start.99 = (bf16[4,384,384]{2,1,0:T(8,128)(2,1)}, bf16[4,384,384]{2,1,0:T(8,128)(2,1)}, u32[]{:S(2)}, u32[]{:S(2)}) collective-permute-start(bf16[4,384,384]{2,1,0:T(8,128)(2,1)} %get-tuple-element.147), channel_id=1, source_target_pairs={{4,0},{0,4},{12,8},{8,12},{20,16},{16,20},{28,24},{24,28},{5,1},{1... | collective-permute-start | bytes 3538952 | tf_op jit(solution)/shard_map/ppermute | solution.py:535
  577.8 32.4 %collective-permute-start.88 = (bf16[384,768]{1,0:T(8,128)(2,1)S(1)}, bf16[384,768]{1,0:T(8,128)(2,1)S(1)}, u32[]{:S(2)}, u32[]{:S(2)}) collective-permute-start(bf16[384,768]{1,0:T(8,128)(2,1)S(1)} %convert_element_type.1177.refs_0_), channel_id=1, source_target_pairs={{1,0},{2,1},{3,2},{0,3},{5,4},{6,5},{7,6},{4,7},{9,8},{10,9},{11,1... | collective-permute-start | bytes 1769480 | tf_op jit(solution)/shard_map/ppermute | solution.py:541
  579.6 70.3 %collective-permute-start.89 = (bf16[384,768]{1,0:T(8,128)(2,1)S(1)}, bf16[384,768]{1,0:T(8,128)(2,1)S(1)}, u32[]{:S(2)}, u32[]{:S(2)}) collective-permute-start(bf16[384,768]{1,0:T(8,128)(2,1)S(1)} %convert_element_type.1177.refs_0_), channel_id=1, source_target_pairs={{2,0},{3,1},{0,2},{1,3},{6,4},{7,5},{4,6},{5,7},{10,8},{11,9},{8,1... | collective-permute-start | bytes 1769480 | tf_op jit(solution)/shard_map/ppermute | solution.py:541
  599.2 53.0 %collective-permute-start.90 = (bf16[384,768]{1,0:T(8,128)(2,1)S(1)}, bf16[384,768]{1,0:T(8,128)(2,1)S(1)}, u32[]{:S(2)}, u32[]{:S(2)}) collective-permute-start(bf16[384,768]{1,0:T(8,128)(2,1)S(1)} %convert_element_type.1177.refs_0_), channel_id=1, source_target_pairs={{3,0},{0,1},{1,2},{2,3},{7,4},{4,5},{5,6},{6,7},{11,8},{8,9},{9,10... | collective-permute-start | bytes 1769480 | tf_op jit(solution)/shard_map/ppermute | solution.py:541
  603.2 56.0 %collective-permute-start.106 = (bf16[4,2,96,384]{3,2,1,0:T(8,128)(2,1)}, bf16[4,2,96,384]{3,2,1,0:T(8,128)(2,1)}, u32[]{:S(2)}, u32[]{:S(2)}) collective-permute-start(bf16[4,2,96,384]{3,2,1,0:T(8,128)(2,1)} %fusion.54), channel_id=1, source_target_pairs={{0,16},{4,20},{8,24},{12,28},{16,0},{20,4},{24,8},{28,12},{1,17},{... | collective-permute-start | bytes 1769480 | tf_op jit(solution)/shard_map/ppermute | solution.py:538
  610.2 58.7 %collective-permute-start.111 = (bf16[4,384,384]{2,1,0:T(8,128)(2,1)}, bf16[4,384,384]{2,1,0:T(8,128)(2,1)}, u32[]{:S(2)}, u32[]{:S(2)}) collective-permute-start(bf16[4,384,384]{2,1,0:T(8,128)(2,1)} %get-tuple-element.151), channel_id=1, source_target_pairs={{4,0},{0,4},{12,8},{8,12},{20,16},{16,20},{28,24},{24,28},{5,1},{1... | collective-permute-start | bytes 3538952 | tf_op jit(solution)/shard_map/ppermute | solution.py:535
  653.1 41.2 %collective-permute-start.141 = (bf16[4,384,768]{2,1,0:T(8,128)(2,1)}, bf16[4,384,768]{2,1,0:T(8,128)(2,1)S(1)}, u32[]{:S(2)}, u32[]{:S(2)}) collective-permute-start(bf16[4,384,768]{2,1,0:T(8,128)(2,1)} %get-tuple-element.161), channel_id=1, source_target_pairs={{4,0},{0,4},{12,8},{8,12},{20,16},{16,20},{28,24},{24,28},{5,1},{1... | collective-permute-start | bytes 7077896 | tf_op jit(solution)/shard_map/ppermute | solution.py:535
  659.2 38.7 %collective-permute-start.129 = (bf16[4,384,768]{2,1,0:T(8,128)(2,1)}, bf16[4,384,768]{2,1,0:T(8,128)(2,1)S(1)}, u32[]{:S(2)}, u32[]{:S(2)}) collective-permute-start(bf16[4,384,768]{2,1,0:T(8,128)(2,1)} %get-tuple-element.157), channel_id=1, source_target_pairs={{4,0},{0,4},{12,8},{8,12},{20,16},{16,20},{28,24},{24,28},{5,1},{1... | collective-permute-start | bytes 7077896 | tf_op jit(solution)/shard_map/ppermute | solution.py:535
  687.9 47.5 %collective-permute-start.135 = (bf16[4,384,768]{2,1,0:T(8,128)(2,1)}, bf16[4,384,768]{2,1,0:T(8,128)(2,1)}, u32[]{:S(2)}, u32[]{:S(2)}) collective-permute-start(bf16[4,384,768]{2,1,0:T(8,128)(2,1)} %get-tuple-element.159), channel_id=1, source_target_pairs={{4,0},{0,4},{12,8},{8,12},{20,16},{16,20},{28,24},{24,28},{5,1},{1... | collective-permute-start | bytes 7077896 | tf_op jit(solution)/shard_map/ppermute | solution.py:535
  691.5 47.1 %collective-permute-start.123 = (bf16[4,384,768]{2,1,0:T(8,128)(2,1)}, bf16[4,384,768]{2,1,0:T(8,128)(2,1)}, u32[]{:S(2)}, u32[]{:S(2)}) collective-permute-start(bf16[4,384,768]{2,1,0:T(8,128)(2,1)} %get-tuple-element.155), channel_id=1, source_target_pairs={{4,0},{0,4},{12,8},{8,12},{20,16},{16,20},{28,24},{24,28},{5,1},{1... | collective-permute-start | bytes 7077896 | tf_op jit(solution)/shard_map/ppermute | solution.py:535
  728.6 29.2 %collective-permute-start.142 = (bf16[4,2,96,768]{3,2,1,0:T(8,128)(2,1)}, bf16[4,2,96,768]{3,2,1,0:T(8,128)(2,1)}, u32[]{:S(2)}, u32[]{:S(2)}) collective-permute-start(bf16[4,2,96,768]{3,2,1,0:T(8,128)(2,1)} %fusion.31), channel_id=1, source_target_pairs={{0,16},{4,20},{8,24},{12,28},{16,0},{20,4},{24,8},{28,12},{1,17},{... | collective-permute-start | bytes 3538952 | tf_op jit(solution)/shard_map/ppermute | solution.py:538
  731.3 30.4 %collective-permute-start.130 = (bf16[4,2,96,768]{3,2,1,0:T(8,128)(2,1)}, bf16[4,2,96,768]{3,2,1,0:T(8,128)(2,1)}, u32[]{:S(2)}, u32[]{:S(2)}) collective-permute-start(bf16[4,2,96,768]{3,2,1,0:T(8,128)(2,1)} %fusion.29), channel_id=1, source_target_pairs={{0,8},{4,12},{8,0},{12,4},{16,24},{20,28},{24,16},{28,20},{1,9},{5... | collective-permute-start | bytes 3538952 | tf_op jit(solution)/shard_map/ppermute | solution.py:538
  737.5 45.5 %collective-permute-start.136 = (bf16[4,2,96,768]{3,2,1,0:T(8,128)(2,1)S(1)}, bf16[4,2,96,768]{3,2,1,0:T(8,128)(2,1)S(1)}, u32[]{:S(2)}, u32[]{:S(2)}) collective-permute-start(bf16[4,2,96,768]{3,2,1,0:T(8,128)(2,1)S(1)} %fusion.30), channel_id=1, source_target_pairs={{0,16},{4,20},{8,24},{12,28},{16,0},{20,4},{24,8},{28,12},{1,17},{... | collective-permute-start | bytes 3538952 | tf_op jit(solution)/shard_map/ppermute | solution.py:538
  740.2 63.1 %collective-permute-start.124 = (bf16[4,2,96,768]{3,2,1,0:T(8,128)(2,1)S(1)}, bf16[4,2,96,768]{3,2,1,0:T(8,128)(2,1)S(1)}, u32[]{:S(2)}, u32[]{:S(2)}) collective-permute-start(bf16[4,2,96,768]{3,2,1,0:T(8,128)(2,1)S(1)} %fusion.28), channel_id=1, source_target_pairs={{0,8},{4,12},{8,0},{12,4},{16,24},{20,28},{24,16},{28,20},{1,9},{5... | collective-permute-start | bytes 3538952 | tf_op jit(solution)/shard_map/ppermute | solution.py:538
  759.1 39.2 %collective-permute-start.143 = (bf16[4,96,768]{2,1,0:T(8,128)(2,1)S(1)}, bf16[4,96,768]{2,1,0:T(8,128)(2,1)S(1)}, u32[]{:S(2)}, u32[]{:S(2)}) collective-permute-start(bf16[4,96,768]{2,1,0:T(8,128)(2,1)S(1)} %fusion.60), channel_id=1, source_target_pairs={{0,8},{4,12},{8,0},{12,4},{16,24},{20,28},{24,16},{28,20},{1,9},{5... | collective-permute-start | bytes 1769480 | tf_op jit(solution)/shard_map/ppermute | solution.py:538
  763.0 40.7 %collective-permute-start.131 = (bf16[4,96,768]{2,1,0:T(8,128)(2,1)S(1)}, bf16[4,96,768]{2,1,0:T(8,128)(2,1)S(1)}, u32[]{:S(2)}, u32[]{:S(2)}) collective-permute-start(bf16[4,96,768]{2,1,0:T(8,128)(2,1)S(1)} %fusion.58), channel_id=1, source_target_pairs={{0,16},{4,20},{8,24},{12,28},{16,0},{20,4},{24,8},{28,12},{1,17},{... | collective-permute-start | bytes 1769480 | tf_op jit(solution)/shard_map/ppermute | solution.py:538
  783.2 43.3 %collective-permute-start.137 = (bf16[4,96,768]{2,1,0:T(8,128)(2,1)S(1)}, bf16[4,96,768]{2,1,0:T(8,128)(2,1)S(1)}, u32[]{:S(2)}, u32[]{:S(2)}) collective-permute-start(bf16[4,96,768]{2,1,0:T(8,128)(2,1)S(1)} %fusion.59), channel_id=1, source_target_pairs={{0,8},{4,12},{8,0},{12,4},{16,24},{20,28},{24,16},{28,20},{1,9},{5... | collective-permute-start | bytes 1769480 | tf_op jit(solution)/shard_map/ppermute | solution.py:538
  803.7 31.4 %collective-permute-start.125 = (bf16[4,96,768]{2,1,0:T(8,128)(2,1)S(1)}, bf16[4,96,768]{2,1,0:T(8,128)(2,1)S(1)}, u32[]{:S(2)}, u32[]{:S(2)}) collective-permute-start(bf16[4,96,768]{2,1,0:T(8,128)(2,1)S(1)} %fusion.57), channel_id=1, source_target_pairs={{0,16},{4,20},{8,24},{12,28},{16,0},{20,4},{24,8},{28,12},{1,17},{... | collective-permute-start | bytes 1769480 | tf_op jit(solution)/shard_map/ppermute | solution.py:538
  (239 other events, 2878.6 us)

commit v2 on v1

v2 whole, which is shorter than its diff:
```python
from functools import partial

import jax
import jax.numpy as jnp
from jax import lax
from jax.experimental import pallas as pl
from jax.experimental.pallas import tpu as pltpu
from jax.sharding import PartitionSpec as P

BETA = 2.0 / 3.0
EPS = 1e-05
LOW = jnp.bfloat16
F32 = jnp.float32
GELU_C = 0.7978845608028654
GELU_K = 0.044715
VMEM_LIMIT = 56 * 1024 * 1024
ATTN_CUTS = (128, 256)
FEED_CUTS = (256, 256, 256)


def gate_open(noise, alpha):
    return jnp.clip(jax.nn.sigmoid((noise + alpha) / BETA) * 1.2 - 0.1, 0.0, 1.0)


def product(left, right, dims):
    return lax.dot_general(left, right, ((dims[:1], dims[1:]), ((), ())), preferred_element_type=F32)


def nn(left, right):
    return product(left, right, (1, 0))


def nt(left, right):
    return product(left, right, (1, 1))


def tn(left, right):
    return product(left, right, (0, 0))


def full(array):
    shape = array.shape
    return pl.BlockSpec(shape, lambda r: (0,) * len(shape))


def by_group(array):
    shape = array.shape
    return pl.BlockSpec((1,) + shape[1:], lambda r: (r,) + (0,) * (len(shape) - 1))


SPECS = {
    "full": full,
    "group": by_group,
    "any": lambda a: pl.BlockSpec(memory_space=pl.ANY),
    "smem": lambda a: pl.BlockSpec(memory_space=pltpu.SMEM),
}


def run(body, groups, inputs, outputs, scratch, flops, name, riders=(), points=1, number=None):
    count = len(inputs)
    sizes = []
    inputs, outputs, scratch = list(inputs), list(outputs), list(scratch)
    n_out, n_scratch = len(outputs), len(scratch)
    for rider in riders:
        sizes.append((len(rider.inputs), len(rider.outputs), len(rider.scratch)))
        inputs += rider.inputs
        outputs += rider.outputs
        scratch += rider.scratch
    out_shape = [jax.ShapeDtypeStruct(shape, dtype) for shape, dtype, _ in outputs]
    moved = sum(a.size * a.dtype.itemsize for a, kind in inputs if kind != "any")

    def whole(*refs):
        refs = list(refs)
        ins, outs, tmps = refs[: len(inputs)], refs[len(inputs) : len(inputs) + len(outputs)], refs[len(inputs) + len(outputs) :]
        at = [count, n_out, n_scratch]
        tasks = []
        for rider, size in zip(riders, sizes):
            tasks.append(rider.tasks(*[part[i : i + n] for part, i, n in zip((ins, outs, tmps), at, size)]))
            at = [i + n for i, n in zip(at, size)]
        merged = []
        longest = max([len(t) for t in tasks], default=0)
        for index in range(longest):
            merged += [t[index] for t in tasks if index < len(t)]
        slots = groups * points
        r = pl.program_id(0)
        chosen = [[] for _ in range(slots)]
        for index, task in enumerate(merged):
            chosen[round(index * (slots - 1) / max(1, len(merged) - 1))].append(task)

        def point(spot):
            for step in range(groups):
                if chosen[step * points + spot]:

                    @pl.when(r == step)
                    def _(step=step):
                        if step == 0 and spot == 0:
                            riders[0].geo.greet()
                        for task in chosen[step * points + spot]:
                            task()

        body(point, *ins[:count], *outs[:n_out], *tmps[:n_scratch])

    params = {"vmem_limit_bytes": VMEM_LIMIT}
    if riders:
        params.update(collective_id=number, has_side_effects=True)
    return pl.pallas_call(
        whole,
        name=name,
        grid=(groups,),
        in_specs=[SPECS[kind](a) for a, kind in inputs],
        out_specs=[SPECS[kind](o) for o, (_, _, kind) in zip(out_shape, outputs)],
        scratch_shapes=scratch,
        out_shape=out_shape,
        compiler_params=pltpu.CompilerParams(**params),
        cost_estimate=pl.CostEstimate(flops=int(flops), bytes_accessed=int(moved), transcendentals=0),
    )(*[a for a, _ in inputs])


class Geometry:
    def __init__(self, ndp, groups):
        self.ndp, self.groups = ndp, groups
        self.size_y, self.size_x = factor_pair(ndp // 2)
        self.chips = self.size_y * self.size_x

    def here(self):
        dp, h = lax.axis_index("dp"), lax.axis_index("head")
        return lax.rem(dp, 2), lax.rem(lax.div(dp, 2), self.size_x), lax.div(dp, 2 * self.size_x), h

    def device(self, c=0, y=0, x=0, z=0):
        core, ix, iy, h = self.here()
        core = 1 - core if c else core
        iy = lax.rem(iy + y + self.size_y, self.size_y) if y else iy
        ix = lax.rem(ix + x + self.size_x, self.size_x) if x else ix
        h = lax.rem(h + z + self.groups, self.groups) if z else h
        return ((iy * self.size_x + ix) * 2 + core, h)

    def peers(self):
        out = [dict(c=1)]
        out += [dict(y=y) for y in range(1, self.size_y)]
        out += [dict(x=x) for x in range(1, self.size_x)]
        return out + [dict(z=z) for z in range(1, self.groups)]

    def greet(self):
        barrier = pltpu.get_barrier_semaphore()
        for peer in self.peers():
            pl.semaphore_signal(barrier, inc=1, device_id=self.device(**peer), device_id_type=pl.DeviceIdType.MESH)
        pl.semaphore_wait(barrier, len(self.peers()))


class Mover:
    def __init__(self, geo, send, recv):
        self.geo, self.send, self.recv, self.ids, self.copies = geo, send, recv, {}, []

    def __call__(self, key, src, dst, **to):
        index = self.ids.setdefault(key, len(self.ids))
        return pltpu.make_async_remote_copy(
            src_ref=src,
            dst_ref=dst,
            send_sem=self.send.at[index],
            recv_sem=self.recv.at[index],
            device_id=self.geo.device(**to),
            device_id_type=pl.DeviceIdType.MESH,
        )


class Gather:
    def __init__(self, geo, owns, chunks):
        self.geo, self.chunks = geo, chunks
        self.inputs = [(own, "any") for own in owns]
        self.outputs = [((geo.groups,) + own.shape, LOW, "any") for own in owns]
        halves = sum(len(chunk) for chunk in chunks)
        each = geo.groups - 1 + 2 * geo.chips
        sems = pltpu.SemaphoreType.DMA((halves * each,))
        self.scratch = [sems, sems, pltpu.SemaphoreType.DMA((len(owns),))]

    def tasks(self, owns, outs, scratch):
        geo, send, recv, local = self.geo, *scratch
        move = Mover(geo, send, recv)
        groups, sx, sy = geo.groups, geo.size_x, geo.size_y
        others = pl.ds(1, groups - 1)

        def spot(y, x, c=0):
            return c * geo.chips + y * sx + x

        def along(chunk, half, r):
            m, col, cols, _ = self.chunks[chunk][half]
            return move(
                ("z", chunk, half, r),
                owns[m].at[0, :, pl.ds(col, cols)],
                outs[m].at[r, 0, :, pl.ds(col, cols)],
                z=-r,
            )

        def plane(chunk, half, at_y, at_x, **to):
            m, col, cols, _ = self.chunks[chunk][half]
            land = spot(at_y + to.get("y", 0), at_x + to.get("x", 0), to.get("c", 0))
            return move(
                ("p", chunk, half, land),
                outs[m].at[others, spot(at_y, at_x), :, pl.ds(col, cols)],
                outs[m].at[others, land, :, pl.ds(col, cols)],
                **{key: -value if key != "c" else value for key, value in to.items()},
            )

        def own_copy(m):
            return pltpu.make_async_copy(owns[m], outs[m].at[0], local.at[m])

        def halves(chunk):
            return range(len(self.chunks[chunk]))

        def firsts(chunk):
            out = []
            for half in halves(chunk):
                out += [plane(chunk, half, 0, 0, x=x) for x in range(1, sx)]
                out += [plane(chunk, half, 0, 0, y=y) for y in range(1, sy)]
            return out

        def seconds(chunk):
            out = []
            for half in halves(chunk):
                if self.chunks[chunk][half][3]:
                    out += [plane(chunk, half, y, 0, x=x) for y in range(1, sy) for x in range(1, sx)]
                else:
                    out += [plane(chunk, half, 0, x, y=y) for x in range(1, sx) for y in range(1, sy)]
            return out

        def cores(chunk, places):
            return [plane(chunk, half, y, x, c=1) for half in halves(chunk) for y, x in places]

        axes = [(0, x) for x in range(1, sx)] + [(y, 0) for y in range(1, sy)]
        corners = [(y, x) for y in range(1, sy) for x in range(1, sx)]

        def alongs(chunk):
            return [along(chunk, half, r) for half in halves(chunk) for r in range(1, groups)]

        def start(copies):
            for copy in copies:
                copy.start()

        def arrive(copies):
            for copy in copies:
                copy.wait_recv()

        count = len(self.chunks)

        def begin():
            start(alongs(0))
            if count > 1:
                start(alongs(1))
            for m in range(len(owns)):
                own_copy(m).start()

        def level_one(chunk):
            arrive(alongs(chunk))
            start(firsts(chunk))
            start(cores(chunk, [(0, 0)]))
            if chunk + 2 < count:
                start(alongs(chunk + 2))

        def level_two(chunk):
            arrive(firsts(chunk))
            start(seconds(chunk))
            start(cores(chunk, axes))

        def level_three(chunk):
            arrive(seconds(chunk))
            start(cores(chunk, corners))

        def end():
            for m in range(len(owns)):
                own_copy(m).wait()
            for chunk in range(count):
                arrive(cores(chunk, [(0, 0)] + axes + corners))
                for copy in alongs(chunk) + firsts(chunk) + seconds(chunk) + cores(chunk, [(0, 0)] + axes + corners):
                    copy.wait_send()

        out = [begin]
        for time in range(count + 2):
            for level, late in ((level_one, 0), (level_two, 1), (level_three, 2)):
                if 0 <= time - late < count:
                    out.append(partial(level, time - late))
        return out + [end]


class Scatter:
    def __init__(self, geo, grads, chunks):
        self.geo, self.chunks = geo, chunks
        self.inputs = [(grad, "any") for grad in grads]
        self.outputs = [(grad.shape[4:], F32, "full") for grad in grads]
        self.feats = grads[0].shape[4]
        halves = [half for chunk in chunks for half in chunk]
        each = 1 + (geo.size_x - 1) + (geo.size_y - 1) + geo.groups - 1
        sems = pltpu.SemaphoreType.DMA((len(halves) * each,))
        self.scratch = [sems, sems, pltpu.SemaphoreType.DMA((len(halves),))]
        for _, _, cols, y_first in halves:
            self.scratch += [pltpu.VMEM(shape, LOW) for shape in self.shapes(cols, y_first)]

    def shapes(self, cols, y_first):
        geo, feats = self.geo, self.feats
        near, far = (geo.size_y, geo.size_x) if y_first else (geo.size_x, geo.size_y)
        return [
            (geo.groups, geo.size_y, geo.size_x, feats, cols),
            (geo.groups, geo.size_y, geo.size_x, feats, cols),
            (near - 1, geo.groups, far, feats, cols),
            (far - 1, geo.groups, feats, cols),
            (geo.groups - 1, feats, cols),
        ]

    def tasks(self, grads, outs, scratch):
        geo, (send, recv, local), buffers = self.geo, scratch[:3], scratch[3:]
        move = Mover(geo, send, recv)
        groups, sx, sy = geo.groups, geo.size_x, geo.size_y
        index = {}
        for chunk, halves in enumerate(self.chunks):
            for half in range(len(halves)):
                index[chunk, half] = len(index)

        def parts(chunk, half):
            number = index[chunk, half]
            return self.chunks[chunk][half], number, buffers[5 * number : 5 * number + 5]

        def load(chunk, half):
            (m, col, cols, _), number, bufs = parts(chunk, half)
            return pltpu.make_async_copy(
                grads[m].at[:, 0, :, :, :, pl.ds(col, cols)], bufs[0], local.at[number]
            )

        def core(chunk, half):
            (m, col, cols, y_first), number, bufs = parts(chunk, half)
            return move(("c", chunk, half), grads[m].at[:, 1, :, :, :, pl.ds(col, cols)], bufs[1], c=1)

        def near(chunk, half):
            (m, col, cols, y_first), number, bufs = parts(chunk, half)
            if y_first:
                return [
                    move(("n", chunk, half, y), bufs[0].at[:, y], bufs[2].at[y - 1], y=y) for y in range(1, sy)
                ]
            return [
                move(("n", chunk, half, x), bufs[0].at[:, :, x], bufs[2].at[x - 1], x=x) for x in range(1, sx)
            ]

        def far(chunk, half):
            (m, col, cols, y_first), number, bufs = parts(chunk, half)
            if y_first:
                return [
                    move(("f", chunk, half, x), bufs[0].at[:, 0, x], bufs[3].at[x - 1], x=x) for x in range(1, sx)
                ]
            return [
                move(("f", chunk, half, y), bufs[0].at[:, y, 0], bufs[3].at[y - 1], y=y) for y in range(1, sy)
            ]

        def along(chunk, half):
            (m, col, cols, y_first), number, bufs = parts(chunk, half)
            return [
                move(("z", chunk, half, r), bufs[0].at[r, 0, 0], bufs[4].at[r - 1], z=r) for r in range(1, groups)
            ]

        def each(chunk):
            return range(len(self.chunks[chunk]))

        def start(copies):
            for copy in copies:
                copy.start()

        def arrive(copies):
            for copy in copies:
                copy.wait_recv()

        def begin_one(chunk):
            for half in each(chunk):
                core(chunk, half).start()
                load(chunk, half).start()

        count = len(self.chunks)

        def begin():
            begin_one(0)
            if count > 1:
                begin_one(1)

        def level_one(chunk):
            for half in each(chunk):
                _, _, bufs = parts(chunk, half)
                load(chunk, half).wait()
                core(chunk, half).wait_recv()
                for r in range(groups):
                    bufs[0][r] = (bufs[0][r].astype(F32) + bufs[1][r].astype(F32)).astype(LOW)
                start(near(chunk, half))
            if chunk + 2 < count:
                begin_one(chunk + 2)

        def level_two(chunk):
            for half in each(chunk):
                (m, col, cols, y_first), _, bufs = parts(chunk, half)
                arrive(near(chunk, half))
                for r in range(groups):
                    keep = (r, 0) if y_first else (r, slice(None), 0)
                    total = bufs[0][keep].astype(F32)
                    for other in range(bufs[2].shape[0]):
                        total = total + bufs[2][other, r].astype(F32)
                    bufs[0][keep] = total.astype(LOW)
                start(far(chunk, half))

        def level_three(chunk):
            for half in each(chunk):
                _, _, bufs = parts(chunk, half)
                arrive(far(chunk, half))
                for r in range(groups):
                    total = bufs[0][r, 0, 0].astype(F32)
                    for other in range(bufs[3].shape[0]):
                        total = total + bufs[3][other, r].astype(F32)
                    bufs[0][r, 0, 0] = total.astype(LOW)
                start(along(chunk, half))

        def level_four(chunk):
            for half in each(chunk):
                (m, col, cols, y_first), _, bufs = parts(chunk, half)
                arrive(along(chunk, half))
                total = bufs[0][0, 0, 0].astype(F32)
                for r in range(1, groups):
                    total = total + bufs[4][r - 1].astype(F32)
                outs[m][:, col : col + cols] = total

        def end():
            for chunk in range(count):
                for half in each(chunk):
                    for copy in [core(chunk, half)] + near(chunk, half) + far(chunk, half) + along(chunk, half):
                        copy.wait_send()

        out = [begin]
        for time in range(count + 3):
            for level, late in ((level_one, 0), (level_two, 1), (level_three, 2), (level_four, 3)):
                if 0 <= time - late < count:
                    out.append(partial(level, time - late))
        return out + [end]


def only_move(point):
    point(0)


def norm_forward(before, gain, shift):
    center = before - jnp.mean(before, -1, keepdims=True)
    spread = jnp.mean(center * center, -1, keepdims=True)
    return center * lax.rsqrt(spread + EPS) * gain + shift


def norm_backward(before, gain, grad):
    center = before - jnp.mean(before, -1, keepdims=True)
    rate = lax.rsqrt(jnp.mean(center * center, -1, keepdims=True) + EPS)
    hat = center * rate
    grad_hat = grad * gain
    mean_one = jnp.mean(grad_hat, -1, keepdims=True)
    mean_two = jnp.mean(grad_hat * hat, -1, keepdims=True)
    grad_before = rate * (grad_hat - mean_one - hat * mean_two)
    return (
        grad_before,
        jnp.sum(grad * hat, 0, keepdims=True),
        jnp.sum(grad, 0, keepdims=True),
        jnp.sum(grad_before, 0, keepdims=True),
    )


BIAS_ONE, BIAS_TWO, GAIN_ONE, GAIN_TWO, SHIFT_ONE, SHIFT_TWO = range(6)


class Window:
    def __init__(self, seqs, seq_len, rows, groups):
        self.seq_len, self.rows, self.groups = seq_len, rows, groups
        self.block = seq_len // groups
        self.seqs = seqs
        h = lax.axis_index("head")
        self.first = lax.div(h * (seqs - 1), groups)
        self.h = h
        self.base = self.first * seq_len
        self.own = h * rows - self.base
        self.pair = (h + 1 - 2 * lax.rem(h, 2)) * rows - self.base
        self.mid = lax.rem(h, 2) * (2 * rows)
        self.mid_row = lax.rem(h, 2) * self.block

    def at(self, start, rows):
        return pl.ds(pl.multiple_of(start, self.block), rows)

    def loc(self, piece):
        return lax.div((self.h * (self.rows // self.block) + piece) * self.block, self.seq_len) - self.first

    def keys(self, piece):
        return pl.ds(pl.multiple_of(self.loc(piece) * self.seq_len, self.seq_len), self.seq_len)


def attention_forward(size, layer, first, point, *refs):
    seqs, seq_len, heads, head_size = size
    refs = list(refs)
    xwin, small, vec, lengths, left, right = refs[:6]
    refs = refs[6:]
    resid = None if first else refs.pop(0)
    kv_out, q_out, ctx_out, lse_out, gated_out, before_out, h_out, hb_out, total = refs
    r, groups = pl.program_id(0), pl.num_programs(0)
    width = heads * head_size
    rows = total.shape[0]
    window = Window(seqs, seq_len, rows, total.shape[1] // width)
    block = window.block
    row = small[0, 4 * layer + 2 : 4 * layer + 3, :]
    point(0)
    kv = nn(xwin[...], left[0]) + row[:, 2 * width :]
    kv_out[0] = kv.astype(LOW)
    here = window.at(window.own, rows)
    query = (nn(xwin[here, :], right[0, :, :width]) + row[:, :width]).astype(LOW)
    q_out[0] = query
    scaled = query * jnp.asarray(0.125, LOW)
    for piece in range(rows // block):
        mine = slice(piece * block, (piece + 1) * block)
        keys = window.keys(piece)
        usable = lax.broadcasted_iota(jnp.int32, (block, seq_len), 1) < lengths[window.loc(piece)]
        for head in range(heads):
            lanes = slice(head * head_size, (head + 1) * head_size)
            scores = nt(scaled[mine, lanes], kv_out[0, keys, lanes])
            scores = jnp.where(usable, scores, -1e30)
            largest = jnp.max(scores, -1, keepdims=True)
            powers = jnp.exp(scores - largest)
            sums = jnp.sum(powers, -1, keepdims=True)
            value = kv_out[0, keys, width + head * head_size : width + (head + 1) * head_size]
            context = nn(powers.astype(LOW), value) / sums
            ctx_out[0, mine, lanes] = context
            lse_out[0, mine, head : head + 1] = largest + jnp.log(sums)
            point(1 + piece * heads + head)
    gated = (ctx_out[0] * row[:, width : 2 * width]).astype(LOW)
    gated_out[0] = gated
    part = nt(gated, right[0, :, width:])

    @pl.when(r == 0)
    def _():
        total[...] = part

    @pl.when(r > 0)
    def _():
        total[...] += part

    @pl.when(r == groups - 1)
    def _():
        base = 6 * layer
        if first:
            current = xwin[here, :].astype(F32)
        else:
            current = resid[...]
        before = current + total[...] + vec[base + BIAS_ONE : base + BIAS_ONE + 1, :]
        middle = norm_forward(
            before,
            vec[base + GAIN_ONE : base + GAIN_ONE + 1, :],
            vec[base + SHIFT_ONE : base + SHIFT_ONE + 1, :],
        )
        before_out[...] = before
        h_out[...] = middle
        hb_out[...] = middle.astype(LOW)

    point(1 + rows // block * heads)


def gelu_parts(unit):
    square = unit * unit
    bent = jnp.tanh(GELU_C * unit * (1.0 + GELU_K * square))
    half = 0.5 * (1.0 + bent)
    slope = half + 0.5 * unit * (1.0 - bent * bent) * (GELU_C * (1.0 + 3.0 * GELU_K * square))
    return unit * half, slope


def feed_forward(layer, point, *refs):
    middle, middle_low, small, vec, left, right = refs[:6]
    unit_out, before_out, x_out, xb_out, total = refs[6:]
    r, groups = pl.program_id(0), pl.num_programs(0)
    point(0)
    unit = nn(middle_low[...], left[0]) + small[0, 4 * layer + 1 : 4 * layer + 2, :]
    unit_out[0] = unit.astype(LOW)
    point(1)
    bent = jnp.tanh(GELU_C * unit * (1.0 + GELU_K * (unit * unit)))
    active = (0.5 * unit * (1.0 + bent) * small[0, 4 * layer : 4 * layer + 1, :]).astype(LOW)
    point(2)
    part = nt(active, right[0])

    @pl.when(r == 0)
    def _():
        total[...] = part

    @pl.when(r > 0)
    def _():
        total[...] += part

    @pl.when(r == groups - 1)
    def _():
        base = 6 * layer
        before = middle[...] + total[...] + vec[base + BIAS_TWO : base + BIAS_TWO + 1, :]
        current = norm_forward(
            before,
            vec[base + GAIN_TWO : base + GAIN_TWO + 1, :],
            vec[base + SHIFT_TWO : base + SHIFT_TWO + 1, :],
        )
        before_out[...] = before
        x_out[...] = current
        xb_out[...] = current.astype(LOW)

    point(3)


def match_teacher(layers, point, *refs):
    refs = list(refs)
    states = [refs.pop(0) for _ in range(layers)]
    target, row_ok, factor, weight = refs[:4]
    back_out, loss_out, grad_out = refs[4:]
    r = pl.program_id(0)

    @pl.when(r == 0)
    def _():
        loss_out[...] = jnp.zeros_like(loss_out)
        back_out[...] = jnp.zeros_like(back_out)

    total = None
    for layer in range(layers):
        miss = (nn(states[layer][...], weight[0]) - target[0, layer].astype(F32)) * row_ok[:, :1]
        loss_out[:1, : miss.shape[1]] += jnp.sum(miss * miss, 0, keepdims=True)
        low = (factor[...] * miss).astype(LOW)
        back_out[layer] += nt(low, weight[0])
        grad = tn(states[layer][...], low)
        total = grad if total is None else total + grad
    grad_out[0] = total.astype(LOW)


def feed_backward(size, layer, last, point, *refs):
    seqs, seq_len, heads, head_size = size
    refs = list(refs)
    before_two, before_one, middle_low, unit_in, small, vec, left, right = refs[:8]
    refs = refs[8:]
    if last:
        grad_refs = refs[:2]
        refs = refs[2:]
    else:
        grad_refs = refs[:3]
        refs = refs[3:]
    inner_out, outer_out, attn_out, grad_out, vec_out, unit_vec, total, feed = refs
    r, groups = pl.program_id(0), pl.num_programs(0)
    base = 6 * layer
    point(0)

    @pl.when(r == 0)
    def _():
        if last:
            cotangent, back = grad_refs
            grad = cotangent[...].astype(F32) + back[0]
        else:
            mine, pair, mid = grad_refs
            rows, model = mine.shape
            window = Window(seqs, seq_len, rows, model // (heads * head_size))
            total[...] = mine[...] + pair[...].astype(F32)
            total[window.at(window.mid_row, mid.shape[0]), :] += mid[...].astype(F32)
            grad = total[...]
        grad_before, grad_gain, grad_shift, grad_bias = norm_backward(
            before_two[...], vec[base + GAIN_TWO : base + GAIN_TWO + 1, :], grad
        )
        vec_out[BIAS_TWO : BIAS_TWO + 1, :] = grad_bias
        vec_out[GAIN_TWO : GAIN_TWO + 1, :] = grad_gain
        vec_out[SHIFT_TWO : SHIFT_TWO + 1, :] = grad_shift
        feed[...] = grad_before.astype(LOW)
        total[...] = grad_before

    grad_active = nn(feed[...], right[0])
    point(1)
    value, slope = gelu_parts(unit_in[0].astype(F32))
    opened = small[0, 4 * layer : 4 * layer + 1, :]
    grad_unit = (grad_active * (slope * opened)).astype(LOW)
    unit_vec[0, 0:1, :] = jnp.sum(grad_unit.astype(F32), 0, keepdims=True)
    unit_vec[0, 1:2, :] = jnp.sum(grad_active * value, 0, keepdims=True)
    active = (value * opened).astype(LOW)
    point(2)
    total[...] += nt(grad_unit, left[0])
    point(3)
    inner_out[0] = tn(middle_low[...], grad_unit).astype(LOW)
    point(4)
    outer_out[0] = tn(feed[...], active).astype(LOW)
    point(5)

    @pl.when(r == groups - 1)
    def _():
        grad_before, grad_gain, grad_shift, grad_bias = norm_backward(
            before_one[...], vec[base + GAIN_ONE : base + GAIN_ONE + 1, :], total[...]
        )
        vec_out[BIAS_ONE : BIAS_ONE + 1, :] = grad_bias
        vec_out[GAIN_ONE : GAIN_ONE + 1, :] = grad_gain
        vec_out[SHIFT_ONE : SHIFT_ONE + 1, :] = grad_shift
        grad_out[...] = grad_before
        attn_out[...] = grad_before.astype(LOW)

    point(6)


def attention_backward(size, layer, extra, point, *refs):
    seqs, seq_len, heads, head_size = size
    refs = list(refs)
    attn, grad_before, xwin, query_in, kv, ctx, lse, gated, small, lengths, left, right = refs[:12]
    refs = refs[12:]
    back = refs.pop(0) if extra else None
    left_out, right_out, mine_out, pair_out, mid_out, head_vec = refs[:6]
    grad_kv, grad_q, spread, mine = refs[6:]
    r, groups = pl.program_id(0), pl.num_programs(0)
    width = heads * head_size
    rows = mine.shape[0]
    window = Window(seqs, seq_len, rows, mine.shape[1] // width)
    block = window.block
    row = small[0, 4 * layer + 2 : 4 * layer + 3, :]
    opened = row[:, width : 2 * width]
    point(0)
    grad_gated = nn(attn[...], right[0, :, width:])
    shared = grad_gated * ctx[0]
    grad_ctx = (grad_gated * opened).astype(LOW)
    pulled = shared * opened
    scaled = query_in[0] * jnp.asarray(0.125, LOW)
    grad_kv[...] = jnp.zeros_like(grad_kv)
    for piece in range(rows // block):
        here = slice(piece * block, (piece + 1) * block)
        keys = window.keys(piece)
        usable = lax.broadcasted_iota(jnp.int32, (block, seq_len), 1) < lengths[window.loc(piece)]
        for head in range(heads):
            lanes = slice(head * head_size, (head + 1) * head_size)
            later = slice(width + head * head_size, width + (head + 1) * head_size)
            key = kv[0, keys, lanes]
            scores = nt(scaled[here, lanes], key)
            chances = jnp.where(usable, jnp.exp(scores - lse[0, here, head : head + 1]), 0.0)
            grad_chances = nt(grad_ctx[here, lanes], kv[0, keys, later])
            delta = jnp.sum(pulled[here, lanes], -1, keepdims=True)
            grad_scores = (chances * (grad_chances - delta)).astype(LOW)
            grad_q[here, lanes] = nn(grad_scores, key) * 0.125
            grad_kv[keys, lanes] += tn(grad_scores, scaled[here, lanes])
            grad_kv[keys, later] += tn(chances.astype(LOW), grad_ctx[here, lanes])
            point(1 + piece * heads + head)
    spot = 1 + rows // block * heads
    query_low = grad_q[...].astype(LOW)
    kv_low = grad_kv[...].astype(LOW)
    head_vec[0, 0:1, :width] = jnp.sum(query_low.astype(F32), 0, keepdims=True)
    head_vec[0, 0:1, 2 * width :] = jnp.sum(kv_low.astype(F32), 0, keepdims=True)
    head_vec[0, 1:2, :width] = jnp.sum(shared, 0, keepdims=True)

    @pl.when(r == 0)
    def _():
        spread[...] = jnp.zeros_like(spread)
        if extra:
            mine[...] = grad_before[...] + back[0]
        else:
            mine[...] = grad_before[...]

    spread[...] += nt(kv_low, left[0])
    mine[...] += nt(query_low, right[0, :, :width])
    point(spot)
    left_out[0] = tn(xwin[...], kv_low).astype(LOW)
    point(spot + 1)
    here = window.at(window.own, rows)
    right_out[0, :, :width] = tn(xwin[here, :], query_low).astype(LOW)
    right_out[0, :, width:] = tn(attn[...], gated[0]).astype(LOW)

    @pl.when(r == groups - 1)
    def _():
        mine_out[...] = mine[...] + spread[here, :]
        pair_out[...] = spread[window.at(window.pair, rows), :].astype(LOW)
        mid_out[...] = spread[window.at(window.mid, mid_out.shape[0]), :].astype(LOW)

    point(spot + 2)


def place_rows(groups, info, *refs):
    pieces, matrix, out = refs[:groups], refs[groups], refs[groups + 1]
    r = pl.program_id(0)
    for group in range(groups):

        @pl.when(r == group)
        def _(group=group):
            out[...] = nn(pieces[group][...], matrix[...]).astype(out.dtype)


def factor_pair(count):
    side = 1
    for trial in range(1, count + 1):
        if count % trial == 0 and trial * trial <= count:
            side = trial
    return side, count // side


def after(value, *others):
    return lax.optimization_barrier((value,) + others)[0]


def on_device(
    ndp,
    groups,
    hidden_in,
    seq_lengths,
    layer_map,
    teacher_states,
    out_cotangent,
    query_weight,
    key_weight,
    value_weight,
    query_value_bias,
    output_weight,
    branch_bias,
    norm_gain,
    norm_shift,
    inner_weight,
    inner_bias,
    outer_weight,
    head_alpha,
    head_noise,
    unit_alpha,
    unit_noise,
    map_weight,
):
    tokens_dev, model = hidden_in.shape
    seqs_dev = seq_lengths.shape[0]
    seq_len = tokens_dev // seqs_dev
    width = query_weight.shape[2]
    units = inner_weight.shape[2]
    layers, heads = head_alpha.shape
    head_size = width // heads
    rows = tokens_dev // groups
    feats = model // ndp
    geo = Geometry(ndp, groups)
    size_y, size_x, chips = geo.size_y, geo.size_x, geo.chips
    size = (seqs_dev, seq_len, heads, head_size)
    dp = lax.axis_index("dp")
    h = lax.axis_index("head")
    my_c, my_x, my_y, _ = geo.here()

    def pull_group(value, r):
        return lax.ppermute(value, "head", [((i + r) % groups, i) for i in range(groups)])

    def push_group(value, r):
        return lax.ppermute(value, "head", [(i, (i + r) % groups) for i in range(groups)])

    def sum_plane(value):
        for axis, count in (("c", 2), ("y", size_y), ("x", size_x)):
            step = 1
            while step < count:
                stride = {"c": 1, "x": 2, "y": 2 * size_x}[axis] * step
                value = value + lax.ppermute(value, "dp", [(i, i ^ stride) for i in range(ndp)])
                step *= 2
        return value

    def sum_groups(value):
        step = 1
        while step < groups:
            value = value + lax.ppermute(value, "head", [(i, i ^ step) for i in range(groups)])
            step *= 2
        return value

    position = jnp.arange(ndp)
    pos_c, pos_y, pos_x = position // chips, (position // size_x) % size_y, position % size_x
    order = (((my_y + pos_y) % size_y) * size_x + (my_x + pos_x) % size_x) * 2 + (my_c ^ pos_c)
    place = (my_c ^ (position % 2)) * chips
    place = place + ((position // (2 * size_x) - my_y) % size_y) * size_x
    place = place + ((position // 2) % size_x - my_x) % size_x
    source = (order[:, None] * feats + jnp.arange(feats)[None, :]).reshape(model)
    matrix = (source[:, None] == jnp.arange(model)[None, :]).astype(LOW)

    def reorder(value):
        return product(matrix, value, (1, 0)).astype(LOW)

    def reorder_turned(value):
        return product(matrix, value, (1, 1)).astype(LOW)

    kinds = []
    for layer in range(layers):
        kinds.append(reorder(jnp.concatenate([key_weight[layer], value_weight[layer]], 1)))
        kinds.append(
            jnp.concatenate([reorder(query_weight[layer]), reorder_turned(output_weight[layer])], 1)
        )
        kinds.append(reorder(inner_weight[layer]))
        kinds.append(reorder_turned(outer_weight[layer]))
    kinds.append(reorder(map_weight))
    kinds = [kind.reshape(ndp, feats, kind.shape[1]) for kind in kinds]

    def cuts(cols, steps):
        out, start = [], 0
        for step in steps:
            out.append((start, step))
            start += step
        return out if start == cols else [(0, cols)]

    def pairs(cols, steps):
        return [[(0, col, count, False), (1, col, count, True)] for col, count in cuts(cols, steps)]

    attn_pairs, feed_pairs = pairs(2 * width, ATTN_CUTS), pairs(units, FEED_CUTS)

    def attn_gather(layer):
        return Gather(geo, kinds[4 * layer : 4 * layer + 2], attn_pairs)

    def feed_gather(layer):
        return Gather(geo, kinds[4 * layer + 2 : 4 * layer + 4], feed_pairs)

    def matrices(arrays):
        return [(array.reshape(groups, model, array.shape[-1]), "group") for array in arrays]

    def parts(grad):
        return grad.reshape(groups, 2, size_y, size_x, feats, grad.shape[-1])

    open_unit, unit_back = jax.vjp(partial(gate_open, unit_noise), unit_alpha)
    open_head, head_back = jax.vjp(partial(gate_open, head_noise), head_alpha)
    (unit_slope,) = unit_back(jnp.ones_like(open_unit))
    (head_slope,) = head_back(jnp.ones_like(open_head))
    mixed = jnp.concatenate(
        [
            query_value_bias[:, 0],
            jnp.repeat(open_head, head_size, axis=1),
            jnp.zeros((layers, width), F32),
            query_value_bias[:, 1],
        ],
        1,
    )
    empty = jnp.zeros((layers, units), F32)
    small_own = jnp.stack([open_unit, inner_bias, mixed, empty], 1).reshape(4 * layers, units)
    small = jnp.stack([small_own] + [pull_group(small_own, r) for r in range(1, groups)])
    vec = jnp.concatenate([branch_bias, norm_gain, norm_shift], 1).reshape(6 * layers, ndp, feats)
    vec = jnp.take(vec, order, axis=1).reshape(6 * layers, model)
    vec = jnp.concatenate([vec, jnp.zeros((16 - 6 * layers, model), F32)])

    window = Window(seqs_dev, seq_len, rows, groups)
    block, mid_rows = window.block, 2 * window.block
    blocks = rows // block
    win, base, mid_row = window.first, window.base, window.mid_row
    locs = jnp.stack([window.loc(piece) for piece in range(blocks)])
    lengths = lax.dynamic_slice(seq_lengths, (win,), (2,))
    spot = (h * rows + jnp.arange(rows)) % seq_len
    own_lengths = jnp.repeat(jnp.take(lengths, locs), block, total_repeat_length=rows)
    row_ok = jnp.broadcast_to((spot < own_lengths).astype(F32)[:, None], (rows, 128))
    count_all = sum_plane(jnp.sum(seq_lengths).astype(F32).reshape(1, 1))
    factor = (tokens_dev * ndp) / count_all

    hidden = product(lax.dynamic_slice(hidden_in, (base, 0), (2 * seq_len, model)), matrix, (1, 1)).astype(LOW)
    cotangent = product(
        lax.dynamic_slice(out_cotangent, (h * rows, 0), (rows, model)), matrix, (1, 1)
    ).astype(LOW)
    chosen = jnp.take(teacher_states, layer_map, axis=0)

    def teacher_rows(r):
        return lax.dynamic_slice(
            chosen, (0, ((h - r) % groups) * rows, 0), (layers, rows, width)
        )

    target = jnp.stack(
        [teacher_rows(0)] + [pull_group(teacher_rows(r), r) for r in range(1, groups)]
    )

    weights = matrices(run(only_move, 1, [], [], [], 0, "gather_first", [attn_gather(0)], 1, 1))
    xwin, resid = hidden, None
    records = []
    lows = []
    for layer in range(layers):
        inputs = [(xwin, "full"), (small, "group"), (vec, "full"), (lengths, "smem")] + weights
        if layer:
            inputs.append((resid, "full"))
        attn_weights = weights
        kv, query, ctx, lse, gated, before_one, middle, middle_low, *got = run(
            partial(attention_forward, size, layer, layer == 0),
            groups,
            inputs,
            [
                ((groups, 2 * seq_len, 2 * width), LOW, "group"),
                ((groups, rows, width), LOW, "group"),
                ((groups, rows, width), F32, "group"),
                ((groups, rows, 128), F32, "group"),
                ((groups, rows, width), LOW, "group"),
                ((rows, model), F32, "full"),
                ((rows, model), F32, "full"),
                ((rows, model), LOW, "full"),
            ],
            [pltpu.VMEM((rows, model), F32)],
            8e9,
            "attention_forward",
            [feed_gather(layer)],
            2 + blocks * heads,
            2 + 2 * layer,
        )
        feed_weights = matrices(got)
        ahead = attn_gather(layer + 1) if layer + 1 < layers else Gather(geo, kinds[-1:], [[(0, 0, width, False)]])
        unit_in, before_two, resid, low, *got = run(
            partial(feed_forward, layer),
            groups,
            [(middle, "full"), (middle_low, "full"), (small, "group"), (vec, "full")] + feed_weights,
            [
                ((groups, rows, units), LOW, "group"),
                ((rows, model), F32, "full"),
                ((rows, model), F32, "full"),
                ((rows, model), LOW, "full"),
            ],
            [pltpu.VMEM((rows, model), F32)],
            5e9,
            "feed_forward",
            [ahead],
            4,
            3 + 2 * layer,
        )
        weights = matrices(got)
        records.append(
            (xwin, kv, query, ctx, lse, gated, before_one, middle_low, unit_in, before_two, attn_weights, feed_weights)
        )
        lows.append(low)
        if layer + 1 < layers:
            pair = lax.ppermute(low, "head", [(i, i ^ 1) for i in range(groups)])
            mid = lax.ppermute(
                lax.dynamic_slice(low, (mid_row, 0), (mid_rows, model)), "head", [(1, 2), (2, 1)]
            )
            odd = h % 2 == 1
            ahead = jnp.where(odd, pair, low)
            behind = jnp.where(odd, low, pair)
            xwin = jnp.where(
                h < 2, jnp.concatenate([ahead, behind, mid]), jnp.concatenate([mid, ahead, behind])
            )
    back, loss, grad_map = run(
        partial(match_teacher, layers),
        groups,
        [(low, "full") for low in lows] + [(target, "group"), (row_ok, "full"), (factor, "full")] + weights,
        [
            ((layers, rows, model), F32, "full"),
            ((8, 256), F32, "full"),
            ((groups, model, width), LOW, "group"),
        ],
        [],
        4e9,
        "match_teacher",
    )
    info_place = jnp.stack([h]).astype(jnp.int32)

    def place_all(value, dtype):
        pieces = [value] + [pull_group(value, r) for r in range(1, groups)]
        return pl.pallas_call(
            partial(place_rows, groups),
            name="place_rows",
            grid_spec=pltpu.PrefetchScalarGridSpec(
                num_scalar_prefetch=1,
                grid=(groups,),
                in_specs=[pl.BlockSpec(a.shape, lambda r, info: (0, 0)) for a in pieces + [matrix]],
                out_specs=pl.BlockSpec((rows, model), lambda r, info: (lax.rem(info[0] + r, groups), 0)),
            ),
            out_shape=jax.ShapeDtypeStruct((tokens_dev, model), dtype),
            compiler_params=pltpu.CompilerParams(vmem_limit_bytes=VMEM_LIMIT),
            cost_estimate=pl.CostEstimate(
                flops=2 * tokens_dev * model * model, bytes_accessed=8 * tokens_dev * model, transcendentals=0
            ),
        )(info_place, *pieces, matrix)

    block_out = place_all(lows[-1], LOW)

    grads = [(cotangent, "full"), (back[layers - 1 :], "full")]
    results = [None] * layers
    riders, waiting = [], []
    number = 2 + 2 * layers

    def settle(got):
        for (layer, name), value in zip(waiting, got):
            results[layer][name] = value

    map_rider = Scatter(geo, [parts(grad_map)], [[(0, 0, width, False)]])
    for layer in reversed(range(layers)):
        results[layer] = {}
        xwin, kv, query, ctx, lse, gated, before_one, middle_low, unit_in, before_two, attn_weights, feed_weights = records[layer]
        inner, outer, attn, grad_before, vec_out, unit_vec, *got = run(
            partial(feed_backward, size, layer, layer == layers - 1),
            groups,
            [
                (before_two, "full"),
                (before_one, "full"),
                (middle_low, "full"),
                (unit_in, "group"),
                (small, "group"),
                (vec, "full"),
            ]
            + feed_weights
            + grads,
            [((groups, model, units), LOW, "group")] * 2
            + [
                ((rows, model), LOW, "full"),
                ((rows, model), F32, "full"),
                ((8, model), F32, "full"),
                ((groups, 8, units), F32, "group"),
            ],
            [pltpu.VMEM((rows, model), F32), pltpu.VMEM((rows, model), LOW)],
            10e9,
            "feed_backward",
            riders,
            7,
            number,
        )
        number += 1
        settle(got)
        riders = [Scatter(geo, [parts(inner), parts(outer)], feed_pairs)]
        waiting = [(layer, "inner"), (layer, "outer")]
        if layer == layers - 1:
            riders.append(map_rider)
            waiting.append((layer, "map"))
        extra = [(back[layer - 1 : layer], "full")] if layer else []
        left, right, mine, to_pair, to_mid, head_vec, *got = run(
            partial(attention_backward, size, layer, bool(layer)),
            groups,
            [
                (attn, "full"),
                (grad_before, "full"),
                (xwin, "full"),
                (query, "group"),
                (kv, "group"),
                (ctx, "group"),
                (lse, "group"),
                (gated, "group"),
                (small, "group"),
                (lengths, "smem"),
            ]
            + attn_weights
            + extra,
            [((groups, model, 2 * width), LOW, "group")] * 2
            + [
                ((rows, model), F32, "full"),
                ((rows, model), LOW, "full"),
                ((mid_rows, model), LOW, "full"),
                ((groups, 8, units), F32, "group"),
            ],
            [
                pltpu.VMEM((2 * seq_len, 2 * width), F32),
                pltpu.VMEM((rows, width), F32),
                pltpu.VMEM((2 * seq_len, model), F32),
                pltpu.VMEM((rows, model), F32),
            ],
            12e9,
            "attention_backward",
            riders,
            4 + blocks * heads,
            number,
        )
        number += 1
        settle(got)
        riders = [Scatter(geo, [parts(left), parts(right)], attn_pairs)]
        waiting = [(layer, "kv"), (layer, "qo")]
        from_pair = lax.ppermute(to_pair, "head", [(i, i ^ 1) for i in range(groups)])
        from_mid = lax.ppermute(to_mid, "head", [(1, 2), (2, 1)])
        grads = [(mine, "full"), (from_pair, "full"), (from_mid, "full")]
        results[layer].update(vec=vec_out, unit=unit_vec, head=head_vec)
    settle(run(only_move, 1, [], [], [], 0, "scatter_last", riders, 1, number))
    grad_map = results[layers - 1]["map"]
    grad_in = mine + from_pair.astype(F32)
    patch = lax.dynamic_slice(grad_in, (mid_row, 0), (mid_rows, model)) + from_mid.astype(F32)
    grad_in = lax.dynamic_update_slice(grad_in, patch, (mid_row, 0)).astype(LOW)
    grad_hidden = place_all(grad_in, F32)

    by_feature = jnp.concatenate([results[layer]["vec"][:6] for layer in range(layers)])
    by_feature = jnp.take(by_feature.reshape(6 * layers, ndp, feats), place, axis=1)
    by_feature = by_feature.reshape(6 * layers, model)
    loss_row = jnp.concatenate([loss[:1], jnp.zeros((1, model - loss.shape[1]), F32)], 1)
    by_feature = sum_groups(jnp.concatenate([by_feature, loss_row]))
    by_unit = jnp.concatenate(
        [jnp.concatenate([results[layer]["unit"][:, :2], results[layer]["head"][:, :2]], 1) for layer in range(layers)], 1
    )
    summed = by_unit[0]
    for r in range(1, groups):
        summed = summed + push_group(by_unit[r], r)
    everything = sum_plane(jnp.concatenate([by_feature, summed]))
    distill_loss = jnp.sum(everything[6 * layers]) / (count_all[0, 0] * model * layers)
    by_unit = everything[6 * layers + 1 :].reshape(layers, 4, units)
    mine_feats = lax.dynamic_slice(
        everything[: 6 * layers].reshape(layers, 3, 2, model), (0, 0, 0, dp * feats), (layers, 3, 2, feats)
    )
    unit_count = units // ndp
    mine_units = lax.dynamic_slice(by_unit[:, :2], (0, 0, dp * unit_count), (layers, 2, unit_count))
    own_slope = lax.dynamic_slice(unit_slope, (0, dp * unit_count), (layers, unit_count))
    qv_cols = width // ndp
    both = jnp.stack([by_unit[:, 2, :width], by_unit[:, 2, 3 * width : 4 * width]], 1)
    grad_qv_bias = lax.dynamic_slice(both, (0, 0, dp * qv_cols), (layers, 2, qv_cols))
    head_sums = jnp.sum(by_unit[:, 3, :width].reshape(layers, heads, head_size), -1)

    def stacked(member, cols, turned=False):
        arrays = [results[layer][member][:, cols] for layer in range(layers)]
        return jnp.stack([array.T if turned else array for array in arrays])

    front, rear, whole = slice(0, width), slice(width, 2 * width), slice(None)
    return (
        block_out,
        grad_hidden,
        distill_loss,
        stacked("qo", front),
        stacked("kv", front),
        stacked("kv", rear),
        grad_qv_bias,
        stacked("qo", rear, True),
        mine_feats[:, 0],
        mine_feats[:, 1],
        mine_feats[:, 2],
        stacked("inner", whole),
        mine_units[:, 0],
        stacked("outer", whole, True),
        head_sums * head_slope,
        mine_units[:, 1] * own_slope,
        grad_map,
    )


def solution(mesh):
    in_specs = (
        P("dp", None),
        P("dp"),
        P(),
        P(None, "dp", "head"),
        P("dp", None),
        P(None, None, "head"),
        P(None, None, "head"),
        P(None, None, "head"),
        P(None, None, "head"),
        P(None, "head", None),
        P(),
        P(),
        P(),
        P(None, None, "head"),
        P(None, "head"),
        P(None, "head", None),
        P(None, "head"),
        P(None, "head"),
        P(None, "head"),
        P(None, "head"),
        P(None, "head"),
    )
    out_specs = (
        P("dp", None),
        P("dp", None),
        P(),
        P(None, "dp", "head"),
        P(None, "dp", "head"),
        P(None, "dp", "head"),
        P(None, None, ("head", "dp")),
        P(None, "head", "dp"),
        P(None, None, "dp"),
        P(None, None, "dp"),
        P(None, None, "dp"),
        P(None, "dp", "head"),
        P(None, ("head", "dp")),
        P(None, "head", "dp"),
        P(None, "head"),
        P(None, ("head", "dp")),
        P("dp", "head"),
    )
    return jax.shard_map(
        partial(on_device, mesh.shape["dp"], mesh.shape["head"]),
        mesh=mesh,
        in_specs=in_specs,
        out_specs=out_specs,
        check_vma=False,
    )
```

time: 862 us -> 797 us (0.925)
  Pallas kernels: 217 us -> 562 us
  waiting for transfers between devices: 283 us -> 76.7 us
  starting transfers between devices: 169 us -> 58.2 us
  other arithmetic: 73.5 us -> 28.1 us
  local copies, waits for them, and re-layouts: 75.1 us -> 32.5 us
    pallas_call x9 -> x11, Pallas kernels: 205 us -> 550 us  [run(): pl.pallas_call(whole, name=name, grid=(groups,), in_specs=[SPECS[kind](a)...]
    ppermute x76 -> x0, waiting for transfers between devices: 108 us -> none  [the longest x18 67.1 us: push(): lax.ppermute(value, 'dp', [(i, relative(i, c, y, x)) for i in range(ndp)])]
    ppermute x33 -> x12, waiting for transfers between devices: 107 us -> 44.1 us  [pull_group(): lax.ppermute(value, 'head', [((i + r) % groups, i) for i in range(groups)])]
    ppermute x76 -> x0, starting transfers between devices: 48.5 us -> none  [the longest x58 27.3 us: pull(): lax.ppermute(value, 'dp', [(relative(i, c, y, x), i) for i in range(ndp)])]
    ppermute x30 -> x3, waiting for transfers between devices: 43.7 us -> 0.48 us  [push_group(): lax.ppermute(value, 'head', [(i, (i + r) % groups) for i in range(groups)])]
    ppermute x33 -> x12, starting transfers between devices: 61.4 us -> 25 us  [pull_group(): lax.ppermute(value, 'head', [((i + r) % groups, i) for i in range(groups)])]
    ppermute x30 -> x3, starting transfers between devices: 40.2 us -> 5.56 us  [push_group(): lax.ppermute(value, 'head', [(i, (i + r) % groups) for i in range(groups)])]
    convert_element_type x27 -> x0, other arithmetic: 28 us -> none  [the longest x18 21 us: scatter(): total(part(i)).astype(LOW)]
  transfers between devices with their start and end apart: 153 -> 29, of which waited for: 51 -> 9; matrix products, arithmetic and copies ran while one was open for 19% -> 9% of each run, Pallas kernels for 26% -> 44%
where the time goes in v2:
time: 797 us; the launch traced here: 789 us
  Pallas kernels  562 us (71%)
  waiting for transfers between devices  76.7 us (10%)
  starting transfers between devices  58.2 us (7%)
  local copies, waits for them, and re-layouts  32.5 us (4%)
  other arithmetic  28.1 us (4%)
  matrix products  25.8 us (3%)
    pallas_call x11, Pallas kernels, run(): pl.pallas_call(whole, name=name, grid=(groups,), in_specs=[SPECS[kind](a)...  550 us
    ppermute x12, waiting for transfers between devices, pull_group(): lax.ppermute(value, 'head', [((i + r) % groups, i) for i in range(groups)])  44.1 us
    dot_general x13, matrix products, product(): lax.dot_general(left, right, ((dims[:1], dims[1:]), ((), ())), preferred_...  25.8 us
    ppermute x12, starting transfers between devices, pull_group(): lax.ppermute(value, 'head', [((i + r) % groups, i) for i in range(groups)])  25 us
    ppermute x2, waiting for transfers between devices, sum_groups(): lax.ppermute(value, 'head', [(i, i ^ step) for i in range(groups)])  21.3 us
  transfers between devices with their start and end apart: 29, of which 9 were waited for; matrix products, arithmetic and copies ran while one was open for 9% of the time, Pallas kernels for 44%

profile of v2, /device:TPU:0, one launch (start us, length us, event | category | flops | bytes accessed | tf_op | source)
XLA Modules:
  0.0 789.3 jit_solution(13410977425983234033)
XLA Ops:
  5.9 5.0 collective-permute-start
  14.4 2.4 gather_fusion
  16.8 1.5 copy.68
  18.3 1.6 broadcast_select_fusion
  21.1 2.8 collective-permute-start.8
  29.4 1.4 fusion.26
  30.9 2.2 fusion.16
  33.1 2.2 fusion.18
  35.3 2.2 fusion.17
  37.5 2.3 fusion.19
  44.0 2.1 slice_bitcast_fusion
  46.1 1.6 fusion.20
  47.8 2.7 fusion.14.refs_0_.refs_2_
  52.2 2.7 fusion.21
  54.9 2.7 fusion.22.refs_8_
  63.0 39.6 %gather_first.1 = (bf16[4,8,96,384]{3,2,1,0:T(8,128)(2,1)}, bf16[4,8,96,384]{3,2,1,0:T(8,128)(2,1)}) custom-call(bf16[8,96,384]{2,1,0:T(8,128)(2,1)} %bitcast.175, bf16[8,96,384]{2,1,0:T(8,128)(2,1)} %bitcast.174), custom_call_target="tpu_custom_call" | custom-call | tf_op jit(solution)/shard_map/gather_first/pallas_call | solution.py:106
  105.7 81.4 %attention_forward.2 = (bf16[4,1024,384]{2,1,0:T(8,128)(2,1)}, bf16[4,384,192]{2,1,0:T(8,128)(2,1)}, f32[4,384,192]{2,1,0:T(8,128)}, f32[4,384,128]{2,1,0:T(8,12...) custom-call(bf16[1024,768]{1,0:T(8,128)(2,1)} %fusion.14.refs_0_.ref, ...), custom_call_target="tpu_custom_call" | custom-call | flops 8000000000 | bytes 6438920 | tf_op jit(solution)/shard_map/attention_forward/pallas_call | solution.py:106
  187.0 43.7 %feed_forward.2 = (bf16[4,384,768]{2,1,0:T(8,128)(2,1)}, f32[384,768]{1,0:T(8,128)}, f32[384,768]{1,0:T(8,128)}, bf16[384,768]{1,0:T(8,128)(2,1)}, bf16[4,8,96,3...) custom-call(f32[384,768]{1,0:T(8,128)} %get-tuple-element.100.refs_0_, ...), custom_call_target="tpu_custom_call" | custom-call | flops 5000000000 | bytes 11354112 | tf_op jit(solution)/shard_map/feed_forward/pallas_call | solution.py:106
  231.3 2.0 fusion.82
  234.0 2.9 collective-permute-start.12
  238.3 2.9 collective-permute-start.13
  243.7 11.2 %collective-permute-start.4 = (bf16[256,768]{1,0:T(8,128)(2,1)S(1)}, bf16[256,768]{1,0:T(8,128)(2,1)S(1)}, u32[]{:S(2)}, u32[]{:S(2)}) collective-permute-start(bf16[256,768]{1,0:T(8,128)(2,1)S(1)} %constant_dynamic-slice_fusion.15), channel_id=1, source_target_pairs={{1,2},{2,1},{5,6},{6,5},{9,10},{10,9},{13,14},{14,13},{17,18},{18,... | collective-permute-start | bytes 1179656 | tf_op jit(solution)/shard_map/ppermute | solution.py:1003
  255.0 2.7 pad_maximum_fusion.refs_2_
  257.8 1.8 maximum_select_fusion.refs_0_.refs_2_
  259.6 82.6 %attention_forward.3 = (bf16[4,1024,384]{2,1,0:T(8,128)(2,1)}, bf16[4,384,192]{2,1,0:T(8,128)(2,1)}, f32[4,384,192]{2,1,0:T(8,128)}, f32[4,384,128]{2,1,0:T(8,12...) custom-call(bf16[1024,768]{1,0:T(8,128)(2,1)} %maximum_select_fusion, ...), custom_call_target="tpu_custom_call" | custom-call | flops 8000000000 | bytes 7618568 | tf_op jit(solution)/shard_map/attention_forward/pallas_call | solution.py:106
  342.2 24.2 %feed_forward.3 = (bf16[4,384,768]{2,1,0:T(8,128)(2,1)}, f32[384,768]{1,0:T(8,128)}, f32[384,768]{1,0:T(8,128)}, bf16[384,768]{1,0:T(8,128)(2,1)}, bf16[4,8,96,192]{3,2,1,0:T(8,128)(2,1)}) custom-call(f32[384,768]{1,0:T(8,128)} %get-tuple-element.108.refs_0_, bf16[384,768]{1,0:T(8,128)(2,1)} %get-tuple-element.109.refs_1_.refs_2_, ...), custom_call_target="tpu_custom_call" | custom-call | flops 5000000000 | bytes 11354112 | tf_op jit(solution)/shard_map/feed_forward/pallas_call | solution.py:106
  367.2 8.9 %match_teacher.1 = (f32[2,384,768]{2,1,0:T(8,128)}, f32[8,256]{1,0:T(8,128)}, bf16[4,768,192]{2,1,0:T(8,128)(2,1)}) custom-call(bf16[384,768]{1,0:T(8,128)(2,1)} %get-tuple-element.104.refs_0_, bf16[384,768]{1,0:T(8,128)(2,1)} %get-tuple-element.112.refs_0_.refs_1_, bf16[4,2,384,192]{3,2,1,0:T(8,128)(2,1)} %pad_maximum_fusion.refs_2_, ...), custom_call_target="tpu_custom_call" | custom-call | flops 4000000000 | bytes 3735556 | tf_op jit(solution)/shard_map/match_teacher/pallas_call | solution.py:106
  376.2 3.2 fusion.108
  379.4 19.0 %feed_backward.2 = (bf16[4,768,768]{2,1,0:T(8,128)(2,1)}, bf16[4,768,768]{2,1,0:T(8,128)(2,1)}, bf16[384,768]{1,0:T(8,128)(2,1)}, f32[384,768]{1,0:T(8,128)}, f32[8,768]{1,0:T(8,128)}, /*index=5*/f32[4,8,768]{2,1,0:T(8,128)}) custom-call(f32[384,768]{1,0:T(8,128)} %get-tuple-element.116.refs_0_, f32[384,768]{1,0:T(8,128)} %get-tuple-element.117.refs_1_, ...), custom_call_target="tpu_custom_call" | custom-call | flops 10000000000 | bytes 16662528 | tf_op jit(solution)/shard_map/feed_backward/pallas_call | solution.py:106
  398.3 75.1 %attention_backward.2 = (bf16[4,768,384]{2,1,0:T(8,128)(2,1)}, bf16[4,768,384]{2,1,0:T(8,128)(2,1)}, f32[384,768]{1,0:T(8,128)}, bf16[384,768]{1,0:T(8,128)(2,1)...) custom-call(bf16[384,768]{1,0:T(8,128)(2,1)} %get-tuple-element.121., ...), custom_call_target="tpu_custom_call" | custom-call | flops 12000000000 | bytes 15630344 | tf_op jit(solution)/shard_map/attention_backward/pallas_call | solution.py:106
  478.5 3.8 collective-permute-start.6
  484.8 5.1 collective-permute-done.14.refs_9_
  490.7 69.2 %feed_backward.3 = (bf16[4,768,768]{2,1,0:T(8,128)(2,1)}, bf16[4,768,768]{2,1,0:T(8,128)(2,1)}, bf16[384,768]{1,0:T(8,128)(2,1)}, f32[384,768]{1,0:T(8,128)}, f3...) custom-call(f32[384,768]{1,0:T(8,128)} %get-tuple-element.113.refs_0_, ...), custom_call_target="tpu_custom_call" | custom-call | flops 10000000000 | bytes 17055744 | tf_op jit(solution)/shard_map/feed_backward/pallas_call | solution.py:106
  559.9 69.1 %attention_backward.3 = (bf16[4,768,384]{2,1,0:T(8,128)(2,1)}, bf16[4,768,384]{2,1,0:T(8,128)(2,1)}, f32[384,768]{1,0:T(8,128)}, bf16[384,768]{1,0:T(8,128)(2,1)...) custom-call(bf16[384,768]{1,0:T(8,128)(2,1)} %get-tuple-element.136.refs_0_, ...), custom_call_target="tpu_custom_call" | custom-call | flops 12000000000 | bytes 14450696 | tf_op jit(solution)/shard_map/attention_backward/pallas_call | solution.py:106
  629.1 37.5 %scatter_last.1 = (f32[96,384]{1,0:T(8,128)}, f32[96,384]{1,0:T(8,128)}) custom-call(bf16[4,2,2,2,96,384]{5,4,3,2,1,0:T(8,128)(2,1)} %bitcast.172, bf16[4,2,2,2,96,384]{5,4,3,2,1,0:T(8,128)(2,1)} %bitcast.173), custom_call_target="tpu_custom_call" | custom-call | tf_op jit(solution)/shard_map/scatter_last/pallas_call | solution.py:106
  669.5 1.6 collective-permute-start.21
  673.8 2.0 collective-permute-start.24
  678.4 2.8 collective-permute-start.25
  682.9 2.8 collective-permute-start.22
  685.7 21.3 %collective-permute-done.22 = f32[13,768]{1,0:T(8,128)S(1)} collective-permute-done((f32[13,768]{1,0:T(8,128)S(1)}, f32[13,768]{1,0:T(8,128)S(1)}, u32[]{:S(2)}, u32[]{:S(2)}) %collective-permute-start.22) | collective-permute-done | bytes 39968 | tf_op jit(solution)/shard_map/ppermute | solution.py:846
  710.6 5.7 place_rows.2
  717.3 3.4 collective-permute-done.28
  723.0 3.4 collective-permute-start.18
  726.4 3.8 collective-permute-start.19
  730.2 1.9 collective-permute-start.20
  736.2 5.3 collective-permute-done.18.refs_1_
  741.6 38.7 %collective-permute-done.19.refs_2_ = bf16[384,768]{1,0:T(8,128)(2,1)S(1)} collective-permute-done((bf16[384,768]{1,0:T(8,128)(2,1)S(1)}, bf16[384,768]{1,0:T(8,128)(2,1)S(1)}, u32[]{:S(2)}, u32[]{:S(2)}) %collective-permute-start.19) | collective-permute-done | bytes 589856 | tf_op jit(solution)/shard_map/ppermute | solution.py:829
  781.1 6.2 place_rows.3
  (226 shorter events, 62.9 us)
Async XLA Ops:
  0.7 47.1 %copy-start = (bf16[1536,768]{1,0:T(8,128)(2,1)S(1)}, bf16[1536,768]{1,0:T(8,128)(2,1)}, u32[]{:S(2)}) copy-start(bf16[1536,768]{1,0:T(8,128)(2,1)} %param.25) | copy-start | bytes 7077892
  5.2 8.5 %copy-start.18 = (f32[2,4,768]{2,1,0:T(4,128)}, f32[2,4,768]{2,1,0:T(4,128)S(1)}, u32[]{:S(2)}) copy-start(f32[2,4,768]{2,1,0:T(4,128)S(1)} %copy.61) | copy-start | bytes 73732
  5.9 96.8 %collective-permute-start = (f32[8,768]{1,0:T(8,128)}, f32[8,768]{1,0:T(8,128)}, u32[]{:S(2)}, u32[]{:S(2)}) collective-permute-start(f32[8,768]{1,0:T(8,128)} %reshape.485), channel_id=1, source_target_pairs={{1,0},{2,1},{3,2},{0,3},{5,4},{6,5},{7,6},{4,7},{9,8},{10,9},{11,1... | collective-permute-start | bytes 73736 | tf_op jit(solution)/shard_map/ppermute | solution.py:829
  10.9 92.4 %collective-permute-start.1 = (f32[8,768]{1,0:T(8,128)}, f32[8,768]{1,0:T(8,128)}, u32[]{:S(2)}, u32[]{:S(2)}) collective-permute-start(f32[8,768]{1,0:T(8,128)} %reshape.485), channel_id=1, source_target_pairs={{2,0},{3,1},{0,2},{1,3},{6,4},{7,5},{4,6},{5,7},{10,8},{11,9},{8,1... | collective-permute-start | bytes 73736 | tf_op jit(solution)/shard_map/ppermute | solution.py:829
  10.9 93.3 %collective-permute-start.2 = (f32[8,768]{1,0:T(8,128)}, f32[8,768]{1,0:T(8,128)}, u32[]{:S(2)}, u32[]{:S(2)}) collective-permute-start(f32[8,768]{1,0:T(8,128)} %reshape.485), channel_id=1, source_target_pairs={{3,0},{0,1},{1,2},{2,3},{7,4},{4,5},{5,6},{6,7},{11,8},{8,9},{9,10... | collective-permute-start | bytes 73736 | tf_op jit(solution)/shard_map/ppermute | solution.py:829
  21.1 233.9 %collective-permute-start.8 = (bf16[2,384,192]{2,1,0:T(8,128)(2,1)}, bf16[2,384,192]{2,1,0:T(8,128)(2,1)}, u32[]{:S(2)}, u32[]{:S(2)}) collective-permute-start(bf16[2,384,192]{2,1,0:T(8,128)(2,1)} %get-tuple-element.230), channel_id=1, source_target_pairs={{1,0},{2,1},{3,2},{0,3},{5,4},{6,5},{7,6},{4,7},{9,8},{10,9},{11,1... | collective-permute-start | bytes 884744 | tf_op jit(solution)/shard_map/ppermute | solution.py:829
  23.9 231.1 %collective-permute-start.9 = (bf16[2,384,192]{2,1,0:T(8,128)(2,1)}, bf16[2,384,192]{2,1,0:T(8,128)(2,1)}, u32[]{:S(2)}, u32[]{:S(2)}) collective-permute-start(bf16[2,384,192]{2,1,0:T(8,128)(2,1)} %get-tuple-element.229), channel_id=1, source_target_pairs={{2,0},{3,1},{0,2},{1,3},{6,4},{7,5},{4,6},{5,7},{10,8},{11,9},{8,1... | collective-permute-start | bytes 884744 | tf_op jit(solution)/shard_map/ppermute | solution.py:829
  59.5 43.2 %copy-start.8 = (bf16[2,384,192]{2,1,0:T(8,128)(2,1)S(1)}, bf16[2,384,192]{2,1,0:T(8,128)(2,1)}, u32[]{:S(2)}) copy-start(bf16[2,384,192]{2,1,0:T(8,128)(2,1)} %get-tuple-element.228) | copy-start | bytes 884740
  102.7 152.3 %collective-permute-start.10 = (bf16[2,384,192]{2,1,0:T(8,128)(2,1)S(1)}, bf16[2,384,192]{2,1,0:T(8,128)(2,1)S(1)}, u32[]{:S(2)}, u32[]{:S(2)}) collective-permute-start(bf16[2,384,192]{2,1,0:T(8,128)(2,1)S(1)} %copy-done.8), channel_id=1, source_target_pairs={{3,0},{0,1},{1,2},{2,3},{7,4},{4,5},{5,6},{6,7},{11,8},{8,9},{9,10... | collective-permute-start | bytes 884744 | tf_op jit(solution)/shard_map/ppermute | solution.py:829
  103.3 130.0 %collective-permute-start.11 = (f32[1,1]{1,0:T(1,128)}, f32[1,1]{1,0:T(1,128)}, u32[]{:S(2)}, u32[]{:S(2)}) collective-permute-start(f32[1,1]{1,0:T(1,128)} %bitcast.55), channel_id=1, source_target_pairs={{0,4},{4,0},{8,12},{12,8},{16,20},{20,16},{24,28},{28,24},{1,5},{5... | collective-permute-start | bytes 20 | tf_op jit(solution)/shard_map/ppermute | solution.py:839
  230.7 27.0 %collective-permute-start.3 = (bf16[384,768]{1,0:T(8,128)(2,1)}, bf16[384,768]{1,0:T(8,128)(2,1)S(1)}, u32[]{:S(2)}, u32[]{:S(2)}) collective-permute-start(bf16[384,768]{1,0:T(8,128)(2,1)} %get-tuple-element.104.refs_0_), channel_id=1, source_target_pairs={{0,1},{1,0},{2,3},{3,2},{4,5},{5,4},{6,7},{7,6},{8,9},{9,8},{10,11... | collective-permute-start | bytes 1769480 | tf_op jit(solution)/shard_map/ppermute | solution.py:1002
  234.0 3.7 collective-permute-start.12
  238.3 3.7 collective-permute-start.13
  243.7 14.1 %collective-permute-start.4 = (bf16[256,768]{1,0:T(8,128)(2,1)S(1)}, bf16[256,768]{1,0:T(8,128)(2,1)S(1)}, u32[]{:S(2)}, u32[]{:S(2)}) collective-permute-start(bf16[256,768]{1,0:T(8,128)(2,1)S(1)} %constant_dynamic-slice_fusion.15), channel_id=1, source_target_pairs={{1,2},{2,1},{5,6},{6,5},{9,10},{10,9},{13,14},{14,13},{17,18},{18,... | collective-permute-start | bytes 1179656 | tf_op jit(solution)/shard_map/ppermute | solution.py:1003
  473.4 16.5 %collective-permute-start.14 = (bf16[384,768]{1,0:T(8,128)(2,1)}, bf16[384,768]{1,0:T(8,128)(2,1)S(1)}, u32[]{:S(2)}, u32[]{:S(2)}) collective-permute-start(bf16[384,768]{1,0:T(8,128)(2,1)} %get-tuple-element.132), channel_id=1, source_target_pairs={{0,1},{1,0},{2,3},{3,2},{4,5},{5,4},{6,7},{7,6},{8,9},{9,8},{10,11... | collective-permute-start | bytes 1769480 | tf_op jit(solution)/shard_map/ppermute | solution.py:1135
  474.5 10.2 %collective-permute-start.15 = (bf16[256,768]{1,0:T(8,128)(2,1)}, bf16[256,768]{1,0:T(8,128)(2,1)S(1)}, u32[]{:S(2)}, u32[]{:S(2)}) collective-permute-start(bf16[256,768]{1,0:T(8,128)(2,1)} %get-tuple-element.133), channel_id=1, source_target_pairs={{1,2},{2,1},{5,6},{6,5},{9,10},{10,9},{13,14},{14,13},{17,18},{18,... | collective-permute-start | bytes 1179656 | tf_op jit(solution)/shard_map/ppermute | solution.py:1136
  477.1 231.9 %collective-permute-start.5 = (bf16[384,768]{1,0:T(8,128)(2,1)}, bf16[384,768]{1,0:T(8,128)(2,1)}, u32[]{:S(2)}, u32[]{:S(2)}) collective-permute-start(bf16[384,768]{1,0:T(8,128)(2,1)} %get-tuple-element.112.refs_0_.refs_1_), channel_id=1, source_target_pairs={{1,0},{2,1},{3,2},{0,3},{5,4},{6,5},{7,6},{4,7},{9,8},{10,9},{11,1... | collective-permute-start | bytes 1769480 | tf_op jit(solution)/shard_map/ppermute | solution.py:829
  478.5 231.2 %collective-permute-start.6 = (bf16[384,768]{1,0:T(8,128)(2,1)}, bf16[384,768]{1,0:T(8,128)(2,1)}, u32[]{:S(2)}, u32[]{:S(2)}) collective-permute-start(bf16[384,768]{1,0:T(8,128)(2,1)} %get-tuple-element.112.refs_0_.refs_1_), channel_id=1, source_target_pairs={{2,0},{3,1},{0,2},{1,3},{6,4},{7,5},{4,6},{5,7},{10,8},{11,9},{8,1... | collective-permute-start | bytes 1769480 | tf_op jit(solution)/shard_map/ppermute | solution.py:829
  629.1 38.6 %copy-start.17 = (f32[96,384]{1,0:T(8,128)S(1)}, f32[96,384]{1,0:T(8,128)}, u32[]{:S(2)}) copy-start(f32[96,384]{1,0:T(8,128)} %get-tuple-element.158) | copy-start | bytes 442372
  666.6 9.2 %copy-start.16 = (f32[96,384]{1,0:T(8,128)S(1)}, f32[96,384]{1,0:T(8,128)}, u32[]{:S(2)}) copy-start(f32[96,384]{1,0:T(8,128)} %get-tuple-element.159) | copy-start | bytes 442372
  666.6 9.2 %copy-start.15 = (f32[96,384]{1,0:T(8,128)S(1)}, f32[96,384]{1,0:T(8,128)}, u32[]{:S(2)}) copy-start(f32[96,384]{1,0:T(8,128)} %get-tuple-element.160) | copy-start | bytes 442372
  667.7 8.2 %copy-start.11 = (f32[96,768]{1,0:T(8,128)S(1)}, f32[96,768]{1,0:T(8,128)}, u32[]{:S(2)}) copy-start(f32[96,768]{1,0:T(8,128)} %get-tuple-element.164) | copy-start | bytes 884740
  667.7 8.2 %copy-start.14 = (f32[96,768]{1,0:T(8,128)S(1)}, f32[96,768]{1,0:T(8,128)}, u32[]{:S(2)}) copy-start(f32[96,768]{1,0:T(8,128)} %get-tuple-element.163) | copy-start | bytes 884740
  668.7 8.1 %copy-start.10 = (f32[96,768]{1,0:T(8,128)S(1)}, f32[96,768]{1,0:T(8,128)}, u32[]{:S(2)}) copy-start(f32[96,768]{1,0:T(8,128)} %get-tuple-element.162) | copy-start | bytes 884740
  668.7 8.1 %copy-start.13 = (f32[96,768]{1,0:T(8,128)S(1)}, f32[96,768]{1,0:T(8,128)}, u32[]{:S(2)}) copy-start(f32[96,768]{1,0:T(8,128)} %get-tuple-element.161) | copy-start | bytes 884740
  669.5 8.8 %collective-permute-start.21 = (f32[13,768]{1,0:T(8,128)S(1)}, f32[13,768]{1,0:T(8,128)S(1)}, u32[]{:S(2)}, u32[]{:S(2)}) collective-permute-start(f32[13,768]{1,0:T(8,128)S(1)} %select_maximum_fusion), channel_id=1, source_target_pairs={{0,1},{1,0},{2,3},{3,2},{4,5},{5,4},{6,7},{7,6},{8,9},{9,8},{10,11... | collective-permute-start | bytes 119816 | tf_op jit(solution)/shard_map/ppermute | solution.py:846
  673.0 8.2 %collective-permute-start.23 = (f32[8,768]{1,0:T(8,128)S(1)}, f32[8,768]{1,0:T(8,128)S(1)}, u32[]{:S(2)}, u32[]{:S(2)}) collective-permute-start(f32[8,768]{1,0:T(8,128)S(1)} %get-tuple-element.245), channel_id=1, source_target_pairs={{0,1},{1,2},{2,3},{3,0},{4,5},{5,6},{6,7},{7,4},{8,9},{9,10},{10,1... | collective-permute-start | bytes 73736 | tf_op jit(solution)/shard_map/ppermute | solution.py:832
  673.8 7.5 collective-permute-start.24
  678.4 4.5 collective-permute-start.25
  681.2 28.5 %collective-permute-start.7 = (bf16[384,768]{1,0:T(8,128)(2,1)}, bf16[384,768]{1,0:T(8,128)(2,1)S(1)}, u32[]{:S(2)}, u32[]{:S(2)}) collective-permute-start(bf16[384,768]{1,0:T(8,128)(2,1)} %get-tuple-element.112.refs_0_.refs_1_), channel_id=1, source_target_pairs={{3,0},{0,1},{1,2},{2,3},{7,4},{4,5},{5,6},{6,7},{11,8},{8,9},{9,10... | collective-permute-start | bytes 1769480 | tf_op jit(solution)/shard_map/ppermute | solution.py:829
  681.3 41.3 %collective-permute-start.16 = (bf16[384,768]{1,0:T(8,128)(2,1)}, bf16[384,768]{1,0:T(8,128)(2,1)S(1)}, u32[]{:S(2)}, u32[]{:S(2)}) collective-permute-start(bf16[384,768]{1,0:T(8,128)(2,1)} %get-tuple-element.146), channel_id=1, source_target_pairs={{0,1},{1,0},{2,3},{3,2},{4,5},{5,4},{6,7},{7,6},{8,9},{9,8},{10,11... | collective-permute-start | bytes 1769480 | tf_op jit(solution)/shard_map/ppermute | solution.py:1135
  682.9 24.1 %collective-permute-start.22 = (f32[13,768]{1,0:T(8,128)S(1)}, f32[13,768]{1,0:T(8,128)S(1)}, u32[]{:S(2)}, u32[]{:S(2)}) collective-permute-start(f32[13,768]{1,0:T(8,128)S(1)} %fusion.112), channel_id=1, source_target_pairs={{0,2},{1,3},{2,0},{3,1},{4,6},{5,7},{6,4},{7,5},{8,10},{9,11},{10,... | collective-permute-start | bytes 119816 | tf_op jit(solution)/shard_map/ppermute | solution.py:846
  707.0 1.3 collective-permute-start.26
  708.3 14.5 %collective-permute-start.17 = (bf16[256,768]{1,0:T(8,128)(2,1)}, bf16[256,768]{1,0:T(8,128)(2,1)S(1)}, u32[]{:S(2)}, u32[]{:S(2)}) collective-permute-start(bf16[256,768]{1,0:T(8,128)(2,1)} %get-tuple-element.147), channel_id=1, source_target_pairs={{1,2},{2,1},{5,6},{6,5},{9,10},{10,9},{13,14},{14,13},{17,18},{18,... | collective-permute-start | bytes 1179656 | tf_op jit(solution)/shard_map/ppermute | solution.py:1136
  709.0 7.2 collective-permute-start.27
  710.6 12.1 %copy-start.5 = (f32[384,768]{1,0:T(8,128)S(1)}, f32[384,768]{1,0:T(8,128)}, u32[]{:S(2)}) copy-start(f32[384,768]{1,0:T(8,128)} %get-tuple-element.145) | copy-start | bytes 3538948
  716.3 4.4 collective-permute-start.28
  722.7 9.4 %slice-start.1 = ((f32[2,4,768]{2,1,0:T(4,128)}), f32[2,2,768]{2,1,0:T(2,128)S(1)}, s32[]{:S(2)}) async-start(f32[2,4,768]{2,1,0:T(4,128)} %copy-done.21), calls=%async_computation.1 | async-start | bytes 24576 | tf_op jit(solution)/shard_map/slice | solution.py:1164
  722.8 10.0 %slice-start = ((f32[21,768]{1,0:T(8,128)}), f32[12,768]{1,0:T(8,128)S(1)}, s32[]{:S(2)}) async-start(f32[21,768]{1,0:T(8,128)} %copy-done.9), calls=%async_computation | async-start | bytes 98304 | tf_op jit(solution)/shard_map/slice | solution.py:1161
  722.8 10.1 %copy-start.27 = (f32[2,192]{1,0:T(2,128)S(1)}, f32[2,192]{1,0:T(2,128)}, u32[]{:S(2)}) copy-start(f32[2,192]{1,0:T(2,128)} %get-tuple-element.251) | copy-start | bytes 4612
  722.8 12.9 %copy-start.28 = (f32[2,3]{1,0:T(2,128)S(1)}, f32[2,3]{1,0:T(2,128)}, u32[]{:S(2)}) copy-start(f32[2,3]{1,0:T(2,128)} %get-tuple-element.224) | copy-start | bytes 76
  723.0 58.1 %copy-start.3 = (bf16[384,768]{1,0:T(8,128)(2,1)}, bf16[384,768]{1,0:T(8,128)(2,1)S(1)}, u32[]{:S(2)}) copy-start(bf16[384,768]{1,0:T(8,128)(2,1)S(1)} %convert_element_type.79.refs_0_) | copy-start | bytes 1769476
  723.0 18.6 %collective-permute-start.18 = (bf16[384,768]{1,0:T(8,128)(2,1)S(1)}, bf16[384,768]{1,0:T(8,128)(2,1)S(1)}, u32[]{:S(2)}, u32[]{:S(2)}) collective-permute-start(bf16[384,768]{1,0:T(8,128)(2,1)S(1)} %convert_element_type.79.refs_0_), channel_id=1, source_target_pairs={{1,0},{2,1},{3,2},{0,3},{5,4},{6,5},{7,6},{4,7},{9,8},{10,9},{11,1... | collective-permute-start | bytes 1769480 | tf_op jit(solution)/shard_map/ppermute | solution.py:829
  726.4 53.9 %collective-permute-start.19 = (bf16[384,768]{1,0:T(8,128)(2,1)S(1)}, bf16[384,768]{1,0:T(8,128)(2,1)S(1)}, u32[]{:S(2)}, u32[]{:S(2)}) collective-permute-start(bf16[384,768]{1,0:T(8,128)(2,1)S(1)} %convert_element_type.79.refs_0_), channel_id=1, source_target_pairs={{2,0},{3,1},{0,2},{1,3},{6,4},{7,5},{4,6},{5,7},{10,8},{11,9},{8,1... | collective-permute-start | bytes 1769480 | tf_op jit(solution)/shard_map/ppermute | solution.py:829
  730.2 50.9 %collective-permute-start.20 = (bf16[384,768]{1,0:T(8,128)(2,1)S(1)}, bf16[384,768]{1,0:T(8,128)(2,1)}, u32[]{:S(2)}, u32[]{:S(2)}) collective-permute-start(bf16[384,768]{1,0:T(8,128)(2,1)S(1)} %convert_element_type.79.refs_0_), channel_id=1, source_target_pairs={{3,0},{0,1},{1,2},{2,3},{7,4},{4,5},{5,6},{6,7},{11,8},{8,9},{9,10... | collective-permute-start | bytes 1769480 | tf_op jit(solution)/shard_map/ppermute | solution.py:829
  736.2 51.1 %copy-start.20 = (f32[96,192]{1,0:T(8,128)S(1)}, f32[96,192]{1,0:T(8,128)}, u32[]{:S(2)}) copy-start(f32[96,192]{1,0:T(8,128)} %get-tuple-element.306) | copy-start | bytes 221188
  741.6 39.5 %copy-start.6 = (bf16[384,768]{1,0:T(8,128)(2,1)}, bf16[384,768]{1,0:T(8,128)(2,1)S(1)}, u32[]{:S(2)}) copy-start(bf16[384,768]{1,0:T(8,128)(2,1)S(1)} %collective-permute-done.18.refs_1_) | copy-start | bytes 1769476
  781.1 6.8 copy-start.1
  (21 other events, 53.6 us)

commit v3 on v2

v3 whole, which is shorter than its diff:
```python
from functools import partial

import jax
import jax.numpy as jnp
from jax import lax
from jax.experimental import pallas as pl
from jax.experimental.pallas import tpu as pltpu
from jax.sharding import PartitionSpec as P

BETA = 2.0 / 3.0
EPS = 1e-05
LOW = jnp.bfloat16
F32 = jnp.float32
GELU_C = 0.7978845608028654
GELU_K = 0.044715
VMEM_LIMIT = 56 * 1024 * 1024
ATTN_CUTS = (128, 256)
FEED_CUTS = (128, 128, 256, 256)
BACK_CUTS = (128,) * 6
LAST_CUTS = (128, 128, 128)
MESH = pl.DeviceIdType.MESH


def gate_open(noise, alpha):
    return jnp.clip(jax.nn.sigmoid((noise + alpha) / BETA) * 1.2 - 0.1, 0.0, 1.0)


def product(left, right, dims):
    return lax.dot_general(left, right, ((dims[:1], dims[1:]), ((), ())), preferred_element_type=F32)


def nn(left, right):
    return product(left, right, (1, 0))


def nt(left, right):
    return product(left, right, (1, 1))


def tn(left, right):
    return product(left, right, (0, 0))


def factor_pair(count):
    side = 1
    for trial in range(1, count + 1):
        if count % trial == 0 and trial * trial <= count:
            side = trial
    return side, count // side


def block_of(shape, place):
    if place == "full":
        return pl.BlockSpec(shape, lambda r: (0,) * len(shape))
    return pl.BlockSpec((1,) + tuple(shape[1:]), lambda r: (place(r),) + (0,) * (len(shape) - 1))


def spec_of(array, kind):
    if kind == "any":
        return pl.BlockSpec(memory_space=pl.ANY)
    if kind == "smem":
        return pl.BlockSpec(memory_space=pltpu.SMEM)
    if kind == "group":
        return block_of(array.shape, lambda r: r)
    return block_of(array.shape, kind)


def run(body, steps, inputs, outputs, scratch, flops, name, riders=(), points=1, number=None):
    inputs, outputs, scratch = list(inputs), list(outputs), list(scratch)
    at = [len(inputs), len(outputs), len(scratch)]
    starts, sizes = [], []
    for rider in riders:
        starts.append((len(inputs), len(outputs), len(scratch)))
        inputs += rider.inputs
        outputs += rider.outputs
        scratch += rider.scratch
        sizes.append((len(rider.inputs), len(rider.outputs), len(rider.scratch)))
    out_shape = [jax.ShapeDtypeStruct(shape, dtype) for shape, dtype, _ in outputs]
    moved = sum(a.size * a.dtype.itemsize for a, kind in inputs if kind != "any")
    n_in, n_out = len(inputs), len(outputs)
    peers = []
    for rider in riders:
        peers += [peer for peer in rider.peers if peer not in peers]

    def whole(*refs):
        kinds = refs[:n_in], refs[n_in : n_in + n_out], refs[n_in + n_out :]
        slots = steps * points
        listed = []
        for number, (rider, start, size) in enumerate(zip(riders, starts, sizes)):
            tasks = rider.tasks(*[part[i : i + n] for part, i, n in zip(kinds, start, size)])
            for index, task in enumerate(tasks):
                listed.append((index / max(1, len(tasks) - 1), number, index, task))
        chosen = [[] for _ in range(slots)]
        for share, _, _, task in sorted(listed, key=lambda item: item[:3]):
            chosen[round(share * (slots - 1))].append(task)
        r = pl.program_id(0)

        def point(spot, span=range(steps)):
            for step in span:
                if chosen[step * points + spot]:

                    @pl.when(r == step)
                    def _(step=step):
                        if step == 0 and spot == 0:
                            riders[0].geo.greet(peers)
                        for task in chosen[step * points + spot]:
                            task()

        body(point, *[ref for part, n in zip(kinds, at) for ref in part[:n]])

    params = {"vmem_limit_bytes": VMEM_LIMIT}
    if riders:
        params.update(collective_id=number, has_side_effects=True)
    return pl.pallas_call(
        whole,
        name=name,
        grid=(steps,),
        in_specs=[spec_of(a, kind) for a, kind in inputs],
        out_specs=[spec_of(o, kind) for o, (_, _, kind) in zip(out_shape, outputs)],
        scratch_shapes=scratch,
        out_shape=out_shape,
        compiler_params=pltpu.CompilerParams(**params),
        cost_estimate=pl.CostEstimate(flops=int(flops), bytes_accessed=int(moved), transcendentals=0),
    )(*[a for a, _ in inputs])


def only_move(point):
    point(0)


class Geometry:
    def __init__(self, ndp, groups):
        self.ndp, self.groups = ndp, groups
        self.size_y, self.size_x = factor_pair(ndp // 2)

    def here(self):
        dp, h = lax.axis_index("dp"), lax.axis_index("head")
        return lax.rem(dp, 2), lax.rem(lax.div(dp, 2), self.size_x), lax.div(dp, 2 * self.size_x), h

    def place(self, c=0, y=0, x=0, z=0):
        core, ix, iy, h = self.here()
        core = 1 - core if c else core
        iy = lax.rem(iy + (y + self.size_y), self.size_y) if y else iy
        ix = lax.rem(ix + (x + self.size_x), self.size_x) if x else ix
        h = lax.rem(h + (z + self.groups), self.groups) if z else h
        return iy, ix, core, h

    def device(self, **to):
        iy, ix, core, h = self.place(**to)
        return ((iy * self.size_x + ix) * 2 + core, h)

    def axes(self):
        out = [dict(c=1)]
        out += [dict(y=y) for y in range(1, self.size_y)]
        out += [dict(x=x) for x in range(1, self.size_x)]
        return out + self.column()

    def column(self):
        return [dict(z=z) for z in range(1, self.groups)]

    def plane(self):
        out = []
        for c in range(2):
            for y in range(self.size_y):
                for x in range(self.size_x):
                    to = {key: value for key, value in (("c", c), ("y", y), ("x", x)) if value}
                    if to:
                        out.append(to)
        return out

    def greet(self, peers):
        barrier = pltpu.get_barrier_semaphore()
        for peer in peers:
            pl.semaphore_signal(barrier, inc=1, device_id=self.device(**peer), device_id_type=MESH)
        pl.semaphore_wait(barrier, len(peers))


class Mover:
    def __init__(self, geo, send, recv):
        self.geo, self.send, self.recv, self.ids = geo, send, recv, {}

    def __call__(self, key, src, dst, **to):
        index = self.ids.setdefault(key, len(self.ids))
        return pltpu.make_async_remote_copy(
            src_ref=src,
            dst_ref=dst,
            send_sem=self.send.at[index],
            recv_sem=self.recv.at[index],
            device_id=self.geo.device(**to),
            device_id_type=MESH,
        )


def back(to):
    return {key: value if key == "c" else -value for key, value in to.items()}


def start(copies):
    for copy in copies:
        copy.start()


def arrive(copies):
    for copy in copies:
        copy.wait_recv()


def leave(copies):
    for copy in copies:
        copy.wait_send()


class Gather:
    def __init__(self, geo, owns, chunks):
        self.geo, self.chunks, self.peers = geo, chunks, geo.axes()
        self.layers = [layer for _, layer in owns]
        self.inputs = [(own, "any") for own, _ in owns]
        self.outputs = [((geo.groups,) + own.shape[1:], LOW, "any") for own, _ in owns]
        halves = sum(len(chunk) for chunk in chunks)
        each = geo.groups - 1 + 2 * geo.size_x * geo.size_y
        sems = pltpu.SemaphoreType.DMA((halves * each,))
        self.scratch = [sems, sems, pltpu.SemaphoreType.DMA((2, len(owns)))]
        self.scratch += [pltpu.VMEM(own.shape[1:], LOW) for own, _ in owns]

    def tasks(self, owns, outs, scratch):
        geo, (send, recv, local), stages = self.geo, scratch[:3], scratch[3:]
        move = Mover(geo, send, recv)
        groups, sx, sy = geo.groups, geo.size_x, geo.size_y
        others = pl.ds(1, groups - 1)
        owns = [own.at[layer] for own, layer in zip(owns, self.layers)]

        def columns(chunk, half):
            m, col, cols, _ = self.chunks[chunk][half]
            return m, pl.ds(col, cols)

        def along(chunk, half, r):
            m, cols = columns(chunk, half)
            iy, ix, core, _ = geo.place()
            return move(
                ("z", chunk, half, r), owns[m].at[iy, ix, core, :, cols], outs[m].at[r, iy, ix, core, :, cols], z=-r
            )

        def hop(chunk, half, block, to):
            m, cols = columns(chunk, half)
            iy, ix, core, _ = geo.place(**block)
            part = outs[m].at[others, iy, ix, core, :, cols]
            return move(("p", chunk, half, str(block), str(to)), part, part, **back(to))

        def into(m):
            return pltpu.make_async_copy(owns[m], stages[m], local.at[0, m])

        def out_of(m):
            return pltpu.make_async_copy(stages[m], outs[m].at[0], local.at[1, m])

        ways_x = [dict(x=x) for x in range(1, sx)]
        ways_y = [dict(y=y) for y in range(1, sy)]
        corners = [dict(x=x, y=y) for x in range(1, sx) for y in range(1, sy)]

        def halves(chunk):
            return range(len(self.chunks[chunk]))

        def alongs(chunk):
            return [along(chunk, half, r) for half in halves(chunk) for r in range(1, groups)]

        def firsts(chunk):
            return [hop(chunk, half, {}, to) for half in halves(chunk) for to in ways_x + ways_y]

        def seconds(chunk):
            out = []
            for half in halves(chunk):
                near, far = (ways_y, ways_x) if self.chunks[chunk][half][3] else (ways_x, ways_y)
                out += [hop(chunk, half, block, to) for block in near for to in far]
            return out

        def cores(chunk, blocks):
            return [hop(chunk, half, block, dict(c=1)) for half in halves(chunk) for block in blocks]

        count = len(self.chunks)

        def begin():
            start(alongs(0))
            if count > 1:
                start(alongs(1))
            for m in range(len(owns)):
                into(m).start()

        def level_one(chunk):
            arrive(alongs(chunk))
            start(firsts(chunk))
            start(cores(chunk, [{}]))
            if chunk + 2 < count:
                start(alongs(chunk + 2))

        def level_two(chunk):
            arrive(firsts(chunk))
            start(seconds(chunk))
            start(cores(chunk, ways_x + ways_y))
            if chunk == 0:
                for m in range(len(owns)):
                    into(m).wait()
                    out_of(m).start()

        def level_three(chunk):
            arrive(seconds(chunk))
            start(cores(chunk, corners))

        def end():
            for m in range(len(owns)):
                out_of(m).wait()
            for chunk in range(count):
                last = cores(chunk, [{}] + ways_x + ways_y + corners)
                arrive(last)
                leave(alongs(chunk) + firsts(chunk) + seconds(chunk) + last)

        out = [begin]
        for time in range(count + 2):
            for level, late in ((level_one, 0), (level_two, 1), (level_three, 2)):
                if 0 <= time - late < count:
                    out.append(partial(level, time - late))
        return out + [end]


class Scatter:
    def __init__(self, geo, grads, chunks):
        self.geo, self.chunks, self.peers = geo, chunks, geo.axes()
        self.inputs = [(grad, "any") for grad in grads]
        self.outputs = [(grad.shape[4:], F32, "full") for grad in grads]
        feats = grads[0].shape[4]
        halves = [half for chunk in chunks for half in chunk]
        each = 1 + (geo.size_x - 1) + (geo.size_y - 1) + geo.groups - 1
        sems = pltpu.SemaphoreType.DMA((len(halves) * each,))
        self.scratch = [sems, sems, pltpu.SemaphoreType.DMA((len(halves),))]
        for _, _, cols, y_first in halves:
            near, far = (geo.size_y, geo.size_x) if y_first else (geo.size_x, geo.size_y)
            self.scratch += [
                pltpu.VMEM(shape, LOW)
                for shape in (
                    (geo.groups, geo.size_y, geo.size_x, feats, cols),
                    (geo.groups, geo.size_y, geo.size_x, feats, cols),
                    (near - 1, geo.groups, far, feats, cols),
                    (far - 1, geo.groups, feats, cols),
                    (geo.groups - 1, feats, cols),
                )
            ]

    def tasks(self, grads, outs, scratch):
        geo, (send, recv, local), buffers = self.geo, scratch[:3], scratch[3:]
        move = Mover(geo, send, recv)
        groups, sx, sy = geo.groups, geo.size_x, geo.size_y
        index = {}
        for chunk, halves in enumerate(self.chunks):
            for half in range(len(halves)):
                index[chunk, half] = len(index)

        def parts(chunk, half):
            m, col, cols, y_first = self.chunks[chunk][half]
            number = index[chunk, half]
            return grads[m], pl.ds(col, cols), y_first, buffers[5 * number : 5 * number + 5]

        def load(chunk, half):
            grad, cols, _, bufs = parts(chunk, half)
            _, _, core, _ = geo.place()
            return pltpu.make_async_copy(
                grad.at[:, :, :, core, :, cols], bufs[0], local.at[index[chunk, half]]
            )

        def cross(chunk, half):
            grad, cols, _, bufs = parts(chunk, half)
            _, _, core, _ = geo.place(c=1)
            return move(("c", chunk, half), grad.at[:, :, :, core, :, cols], bufs[1], c=1)

        def near(chunk, half):
            _, _, y_first, bufs = parts(chunk, half)
            out = []
            for step in range(1, sy if y_first else sx):
                to = dict(y=step) if y_first else dict(x=step)
                iy, ix, _, _ = geo.place(**to)
                part = bufs[0].at[:, iy] if y_first else bufs[0].at[:, :, ix]
                out.append(move(("n", chunk, half, step), part, bufs[2].at[step - 1], **to))
            return out

        def far(chunk, half):
            _, _, y_first, bufs = parts(chunk, half)
            out = []
            for step in range(1, sx if y_first else sy):
                to = dict(x=step) if y_first else dict(y=step)
                iy, ix, _, _ = geo.place(**to)
                out.append(move(("f", chunk, half, step), bufs[0].at[:, iy, ix], bufs[3].at[step - 1], **to))
            return out

        def along(chunk, half):
            _, _, _, bufs = parts(chunk, half)
            iy, ix, _, _ = geo.place()
            return [
                move(("z", chunk, half, r), bufs[0].at[r, iy, ix], bufs[4].at[r - 1], z=r) for r in range(1, groups)
            ]

        def each(chunk):
            return range(len(self.chunks[chunk]))

        def begin_one(chunk):
            for half in each(chunk):
                cross(chunk, half).start()
                load(chunk, half).start()

        count = len(self.chunks)

        def begin():
            for chunk in range(min(2, count)):
                begin_one(chunk)

        def level_one(chunk):
            for half in each(chunk):
                _, _, _, bufs = parts(chunk, half)
                load(chunk, half).wait()
                cross(chunk, half).wait_recv()
                for r in range(groups):
                    bufs[0][r] = (bufs[0][r].astype(F32) + bufs[1][r].astype(F32)).astype(LOW)
                start(near(chunk, half))
            if chunk + 2 < count:
                begin_one(chunk + 2)

        def level_two(chunk):
            iy, ix, _, _ = geo.place()
            for half in each(chunk):
                _, _, y_first, bufs = parts(chunk, half)
                arrive(near(chunk, half))
                for r in range(groups):
                    total = (bufs[0][r, iy] if y_first else bufs[0][r, :, ix]).astype(F32)
                    for other in range(bufs[2].shape[0]):
                        total = total + bufs[2][other, r].astype(F32)
                    if y_first:
                        bufs[0][r, iy] = total.astype(LOW)
                    else:
                        bufs[0][r, :, ix] = total.astype(LOW)
                start(far(chunk, half))

        def level_three(chunk):
            iy, ix, _, _ = geo.place()
            for half in each(chunk):
                _, _, _, bufs = parts(chunk, half)
                arrive(far(chunk, half))
                for r in range(groups):
                    total = bufs[0][r, iy, ix].astype(F32)
                    for other in range(bufs[3].shape[0]):
                        total = total + bufs[3][other, r].astype(F32)
                    bufs[0][r, iy, ix] = total.astype(LOW)
                start(along(chunk, half))

        def level_four(chunk):
            iy, ix, _, _ = geo.place()
            for half in each(chunk):
                m, col, cols, _ = self.chunks[chunk][half]
                _, _, _, bufs = parts(chunk, half)
                arrive(along(chunk, half))
                total = bufs[0][0, iy, ix].astype(F32)
                for r in range(1, groups):
                    total = total + bufs[4][r - 1].astype(F32)
                outs[m][:, col : col + cols] = total

        def end():
            for chunk in range(count):
                for half in each(chunk):
                    leave([cross(chunk, half)] + near(chunk, half) + far(chunk, half) + along(chunk, half))

        out = [begin]
        for time in range(count + 3):
            for level, late in ((level_one, 0), (level_two, 1), (level_three, 2), (level_four, 3)):
                if 0 <= time - late < count:
                    out.append(partial(level, time - late))
        return out + [end]


class Spread:
    def __init__(self, geo, value, plane=False, absolute=True):
        self.geo, self.plane, self.absolute = geo, plane, absolute
        self.peers = geo.plane() if plane else geo.column()
        self.inputs = [(value, "full")]
        self.outputs = [((len(self.peers) + 1,) + value.shape, value.dtype, "any")]
        sems = pltpu.SemaphoreType.DMA((len(self.peers),))
        self.scratch = [sems, sems, pltpu.SemaphoreType.DMA]

    def tasks(self, values, outs, scratch):
        geo, (value,), (out,), (send, recv, local) = self.geo, values, outs, scratch
        move = Mover(geo, send, recv)
        own = 0
        if self.absolute:
            own = geo.device()[0] if self.plane else geo.device()[1]
        copies = []
        for to in self.peers:
            slot = own if self.absolute else to["z"]
            copies.append(move(str(to), value, out.at[slot], **back(to)))
        mine = pltpu.make_async_copy(value, out.at[own], local)

        def begin():
            start(copies)
            mine.start()

        def end():
            mine.wait()
            arrive(copies)
            leave(copies)

        return [begin, end]


class Deal:
    def __init__(self, geo, value):
        self.geo, self.peers = geo, geo.column()
        self.rows = value.shape[1] // geo.groups
        self.inputs = [(value, "any")]
        shape = (geo.groups - 1, value.shape[0], self.rows, value.shape[2])
        self.outputs = [(shape, value.dtype, "any")]
        sems = pltpu.SemaphoreType.DMA((geo.groups - 1,))
        self.scratch = [sems, sems]

    def tasks(self, values, outs, scratch):
        geo = self.geo
        move = Mover(geo, *scratch)
        copies = []
        for r in range(1, geo.groups):
            first = pl.multiple_of(geo.place(z=-r)[3] * self.rows, self.rows)
            copies.append(move(r, values[0].at[:, pl.ds(first, self.rows), :], outs[0].at[r - 1], z=-r))

        def end():
            arrive(copies)
            leave(copies)

        return [lambda: start(copies), end]


class Fold:
    def __init__(self, geo, items):
        self.geo, self.peers = geo, geo.plane() + geo.column()
        self.inputs = [(item[0], "full") for item in items]
        self.picks = [item[1:] for item in items]
        rows = sum(stop - first for _, (first, stop), _ in self.picks)
        self.rows = -(-rows // 8) * 8
        self.outputs = [((self.rows, 128), F32, "full")]
        near, far = pltpu.SemaphoreType.DMA((geo.ndp - 1,)), pltpu.SemaphoreType.DMA((geo.groups - 1,))
        wide = pltpu.VMEM((geo.ndp, geo.groups, self.rows, 128), F32)
        slim = pltpu.VMEM((geo.groups, self.rows, 128), F32)
        self.scratch = [near, near, far, far, wide, wide, slim, slim]

    def tasks(self, values, outs, scratch):
        geo = self.geo
        near_send, near_recv, far_send, far_recv, packed, landed, middle, last = scratch
        groups, ndp = geo.groups, geo.ndp
        to_plane, to_column = Mover(geo, near_send, near_recv), Mover(geo, far_send, far_recv)
        dp, h = geo.device()
        near, far = [], []
        for to in geo.plane():
            there, _ = geo.device(**to)
            near.append(to_plane(str(to), packed.at[there], landed.at[dp], **to))
        for r in range(1, groups):
            far.append(to_column(r, middle.at[r], last.at[h], z=r))

        def begin():
            packed[...] = jnp.zeros_like(packed)
            row = 0
            for value, (grouped, (low, high), (first, stride, cols)) in zip(values, self.picks):
                for r in range(groups):
                    for d in range(ndp):
                        lanes = slice(first + d * stride, first + d * stride + cols)
                        part = value[r, low:high, lanes] if grouped else value[low:high, lanes]
                        packed[d, r, row : row + high - low, :cols] = part
                row += high - low
            start(near)

        def fold():
            landed[dp] = packed[dp]
            arrive(near)
            total = landed[0]
            for d in range(1, ndp):
                total = total + landed[d]
            middle[...] = total
            start(far)

        def end():
            last[h] = middle[0]
            arrive(far)
            total = last[0]
            for z in range(1, groups):
                total = total + last[z]
            outs[0][...] = total
            leave(near)
            leave(far)

        return [begin, fold, end]


def norm_forward(before, gain, shift):
    center = before - jnp.mean(before, -1, keepdims=True)
    spread = jnp.mean(center * center, -1, keepdims=True)
    return center * lax.rsqrt(spread + EPS) * gain + shift


def norm_backward(before, gain, grad):
    center = before - jnp.mean(before, -1, keepdims=True)
    rate = lax.rsqrt(jnp.mean(center * center, -1, keepdims=True) + EPS)
    hat = center * rate
    grad_hat = grad * gain
    mean_one = jnp.mean(grad_hat, -1, keepdims=True)
    mean_two = jnp.mean(grad_hat * hat, -1, keepdims=True)
    grad_before = rate * (grad_hat - mean_one - hat * mean_two)
    return (
        grad_before,
        jnp.sum(grad * hat, 0, keepdims=True),
        jnp.sum(grad, 0, keepdims=True),
        jnp.sum(grad_before, 0, keepdims=True),
    )


BIAS_ONE, BIAS_TWO, GAIN_ONE, GAIN_TWO, SHIFT_ONE, SHIFT_TWO = range(6)


class Window:
    def __init__(self, size, rows, groups):
        self.seqs, self.seq_len, self.heads, self.head_size = size
        self.rows, self.groups = rows, groups
        self.block = self.seq_len // groups
        self.mid_rows = 2 * self.block
        h = lax.axis_index("head")
        self.h = h
        self.first = lax.div(h * (self.seqs - 1), groups)
        self.base = self.first * self.seq_len
        self.own = h * rows - self.base
        pair = h + 1 - 2 * lax.rem(h, 2)
        self.pair = pair * rows - self.base
        self.mid = lax.rem(h, 2) * (2 * rows)
        self.mid_row = lax.rem(h, 2) * self.block
        self.middle = (h > 0) & (h < groups - 1)
        dp = lax.axis_index("dp")
        self.to_pair = (dp, pair)
        self.to_mid = (dp, groups - 1 - h)

    def at(self, begin, rows):
        return pl.ds(pl.multiple_of(begin, self.block), rows)

    def loc(self, piece):
        return lax.div((self.h * (self.rows // self.block) + piece) * self.block, self.seq_len) - self.first

    def keys(self, piece):
        return pl.ds(pl.multiple_of(self.loc(piece) * self.seq_len, self.seq_len), self.seq_len)


def remote(src, dst, sems, to):
    return pltpu.make_async_remote_copy(
        src_ref=src, dst_ref=dst, send_sem=sems.at[0], recv_sem=sems.at[1], device_id=to, device_id_type=MESH
    )


def add_up(r, total, part):
    @pl.when(r == 0)
    def _():
        total[...] = part

    @pl.when(r > 0)
    def _():
        total[...] += part


def attention_forward(size, layer, first, point, *refs):
    seqs, seq_len, heads, head_size = size
    refs = list(refs)
    xwin, small, vec, lengths, left, right = refs[:6]
    refs = refs[6:]
    resid = None if first else refs.pop(0)
    kv_out, q_out, ctx_out, lse_out, gated_out, before_out, h_out, hb_out, total = refs
    r, groups = pl.program_id(0), pl.num_programs(0)
    width = heads * head_size
    rows = total.shape[0]
    window = Window(size, rows, total.shape[1] // width)
    block = window.block
    offset = window.base if first else 0
    row = small[0, 4 * layer + 2 : 4 * layer + 3, :]
    point(0)
    kv = nn(xwin[window.at(offset, 2 * seq_len), :], left[0]) + row[:, 2 * width :]
    kv_out[0] = kv.astype(LOW)
    here = window.at(offset + window.own, rows)
    query = (nn(xwin[here, :], right[0, :, :width]) + row[:, :width]).astype(LOW)
    q_out[0] = query
    scaled = query * jnp.asarray(0.125, LOW)
    for piece in range(rows // block):
        mine = slice(piece * block, (piece + 1) * block)
        keys = window.keys(piece)
        usable = lax.broadcasted_iota(jnp.int32, (block, seq_len), 1) < lengths[window.loc(piece)]
        for head in range(heads):
            lanes = slice(head * head_size, (head + 1) * head_size)
            scores = nt(scaled[mine, lanes], kv_out[0, keys, lanes])
            scores = jnp.where(usable, scores, -1e30)
            largest = jnp.max(scores, -1, keepdims=True)
            powers = jnp.exp(scores - largest)
            sums = jnp.sum(powers, -1, keepdims=True)
            value = kv_out[0, keys, width + head * head_size : width + (head + 1) * head_size]
            context = nn(powers.astype(LOW), value) / sums
            ctx_out[0, mine, lanes] = context
            lse_out[0, mine, head : head + 1] = largest + jnp.log(sums)
            point(1 + piece * heads + head)
    gated = (ctx_out[0] * row[:, width : 2 * width]).astype(LOW)
    gated_out[0] = gated
    add_up(r, total, nt(gated, right[0, :, width:]))

    @pl.when(r == groups - 1)
    def _():
        base = 6 * layer
        if first:
            current = xwin[here, :].astype(F32)
        else:
            current = resid[...]
        before = current + total[...] + vec[base + BIAS_ONE : base + BIAS_ONE + 1, :]
        middle = norm_forward(
            before,
            vec[base + GAIN_ONE : base + GAIN_ONE + 1, :],
            vec[base + SHIFT_ONE : base + SHIFT_ONE + 1, :],
        )
        before_out[...] = before
        h_out[...] = middle
        hb_out[...] = middle.astype(LOW)

    point(1 + rows // block * heads)


def gelu_parts(unit):
    square = unit * unit
    bent = jnp.tanh(GELU_C * unit * (1.0 + GELU_K * square))
    half = 0.5 * (1.0 + bent)
    slope = half + 0.5 * unit * (1.0 - bent * bent) * (GELU_C * (1.0 + 3.0 * GELU_K * square))
    return unit * half, slope


def feed_forward(size, layer, halo, point, *refs):
    refs = list(refs)
    middle, middle_low, small, vec, left, right = refs[:6]
    refs = refs[6:]
    unit_out, before_out, x_out, xb_out = refs[:4]
    refs = refs[4:]
    win_out = refs.pop(0) if halo else None
    total = refs.pop(0)
    r, groups = pl.program_id(0), pl.num_programs(0)
    point(0)
    unit = nn(middle_low[...], left[0]) + small[0, 4 * layer + 1 : 4 * layer + 2, :]
    unit_out[0] = unit.astype(LOW)
    point(1)
    bent = jnp.tanh(GELU_C * unit * (1.0 + GELU_K * (unit * unit)))
    active = (0.5 * unit * (1.0 + bent) * small[0, 4 * layer : 4 * layer + 1, :]).astype(LOW)
    point(2)
    add_up(r, total, nn(active, right[0]))
    if halo:
        low, zero, pair_sems, mid_sems, local = refs
        rows = total.shape[0]
        window = Window(size, rows, win_out.shape[1] // (size[2] * size[3]))
        groups_all, mid_rows = window.groups, window.mid_rows
        own = win_out.at[window.at(window.own, rows)]
        to_pair = remote(low, own, pair_sems, window.to_pair)
        to_mid = remote(
            low.at[window.at(window.mid_row, mid_rows)],
            win_out.at[window.at((1 - lax.rem(window.h, 2)) * 2 * rows, mid_rows)],
            mid_sems,
            window.to_mid,
        )
        mine = pltpu.make_async_copy(low, own, local.at[0])
        empty = pltpu.make_async_copy(
            zero, win_out.at[window.at(lax.rem(window.h + 1, 2) * 2 * rows, mid_rows)], local.at[1]
        )

    @pl.when(r == groups - 1)
    def _():
        base = 6 * layer
        before = middle[...] + total[...] + vec[base + BIAS_TWO : base + BIAS_TWO + 1, :]
        current = norm_forward(
            before,
            vec[base + GAIN_TWO : base + GAIN_TWO + 1, :],
            vec[base + SHIFT_TWO : base + SHIFT_TWO + 1, :],
        )
        before_out[...] = before
        x_out[...] = current
        xb_out[...] = current.astype(LOW)
        if halo:
            low[...] = current.astype(LOW)
            to_pair.start()

            @pl.when(window.middle)
            def _():
                to_mid.start()

            mine.start()

            @pl.when(jnp.logical_not(window.middle))
            def _():
                zero[...] = jnp.zeros_like(zero)
                empty.start()

    point(3)
    if halo:

        @pl.when(r == groups - 1)
        def _():
            mine.wait()
            to_pair.wait()

            @pl.when(window.middle)
            def _():
                to_mid.wait()

            @pl.when(jnp.logical_not(window.middle))
            def _():
                empty.wait()


def match_teacher(layers, tokens, point, *refs):
    refs = list(refs)
    states = [refs.pop(0) for _ in range(layers)]
    target, chosen, row_ok, counts, weight = refs[:5]
    back_out, loss_out, grad_out = refs[5:]
    r = pl.program_id(0)
    rows = states[0].shape[0]

    @pl.when(r == 0)
    def _():
        loss_out[...] = jnp.zeros_like(loss_out)
        back_out[...] = jnp.zeros_like(back_out)

    count = jnp.sum(counts[...][:, 0:1, 0:1], 0)
    factor = tokens / count
    mine = pl.ds(pl.multiple_of(lax.axis_index("head") * rows, rows), rows)
    total = None
    for layer in range(layers):
        goal = jnp.where(r == 0, chosen[layer, mine, :], target[0, layer]).astype(F32)
        miss = (nn(states[layer][...], weight[0]) - goal) * row_ok[:, :1]
        loss_out[:1, :1] += jnp.sum(jnp.sum(miss * miss, 0, keepdims=True), 1, keepdims=True)
        low = (factor * miss).astype(LOW)
        back_out[layer] += nt(low, weight[0])
        grad = tn(states[layer][...], low)
        total = grad if total is None else total + grad
    grad_out[0] = total.astype(LOW)


def feed_backward(layer, last, point, *refs):
    refs = list(refs)
    before_two, before_one, middle_low, unit_in, small, vec, left, right = refs[:8]
    refs = refs[8:]
    grad_refs = [refs.pop(0) for _ in range(2 if last else 1)]
    inner_out, outer_out, attn_out, grad_out, vec_out, unit_vec, total, feed = refs
    r, groups = pl.program_id(0), pl.num_programs(0)
    base = 6 * layer
    point(0)

    @pl.when(r == 0)
    def _():
        if last:
            cotangent, spread = grad_refs
            rows = total.shape[0]
            mine = pl.ds(pl.multiple_of(lax.axis_index("head") * rows, rows), rows)
            grad = cotangent[mine, :].astype(F32) + spread[0]
        else:
            grad = grad_refs[0][...]
        grad_before, grad_gain, grad_shift, grad_bias = norm_backward(
            before_two[...], vec[base + GAIN_TWO : base + GAIN_TWO + 1, :], grad
        )
        vec_out[BIAS_TWO : BIAS_TWO + 1, :] = grad_bias
        vec_out[GAIN_TWO : GAIN_TWO + 1, :] = grad_gain
        vec_out[SHIFT_TWO : SHIFT_TWO + 1, :] = grad_shift
        feed[...] = grad_before.astype(LOW)
        total[...] = grad_before

    grad_active = nt(feed[...], right[0])
    point(1)
    value, slope = gelu_parts(unit_in[0].astype(F32))
    opened = small[0, 4 * layer : 4 * layer + 1, :]
    grad_unit = (grad_active * (slope * opened)).astype(LOW)
    unit_vec[0, 0:1, :] = jnp.sum(grad_unit.astype(F32), 0, keepdims=True)
    unit_vec[0, 1:2, :] = jnp.sum(grad_active * value, 0, keepdims=True)
    active = (value * opened).astype(LOW)
    point(2)
    total[...] += nt(grad_unit, left[0])
    point(3)
    inner_out[0] = tn(middle_low[...], grad_unit).astype(LOW)
    point(4)
    outer_out[0] = tn(feed[...], active).astype(LOW)
    point(5)

    @pl.when(r == groups - 1)
    def _():
        grad_before, grad_gain, grad_shift, grad_bias = norm_backward(
            before_one[...], vec[base + GAIN_ONE : base + GAIN_ONE + 1, :], total[...]
        )
        vec_out[BIAS_ONE : BIAS_ONE + 1, :] = grad_bias
        vec_out[GAIN_ONE : GAIN_ONE + 1, :] = grad_gain
        vec_out[SHIFT_ONE : SHIFT_ONE + 1, :] = grad_shift
        grad_out[...] = grad_before
        attn_out[...] = grad_before.astype(LOW)

    point(6)


def attention_backward(size, layer, first, point, *refs):
    seqs, seq_len, heads, head_size = size
    refs = list(refs)
    attn, grad_before, xwin, query_in, kv, ctx, lse, gated, small, lengths, left, right = refs[:12]
    refs = refs[12:]
    extra = None if first else refs.pop(0)
    left_out, right_out, grad_out, head_vec = refs[:4]
    (grad_kv, grad_q, kv_all, q_all, spread, mine, pair_low, pair_got, mid_low, mid_got, pair_sems, mid_sems) = refs[4:]
    step, groups = pl.program_id(0), pl.num_programs(0) // 2
    width = heads * head_size
    rows = mine.shape[0]
    group_count = mine.shape[1] // width
    window = Window(size, rows, group_count)
    block, mid_rows = window.block, window.mid_rows
    blocks = rows // block
    offset = window.base if first else 0
    here = window.at(offset + window.own, rows)
    row = small[0, 4 * layer + 2 : 4 * layer + 3, :]
    to_pair = remote(pair_low, pair_got, pair_sems, window.to_pair)
    to_mid = remote(mid_low, mid_got, mid_sems, window.to_mid)
    ahead, behind = range(group_count), range(group_count, 2 * group_count)

    @pl.when(step < groups)
    def _():
        point(0, ahead)
        opened = row[:, width : 2 * width]
        grad_gated = nn(attn[...], right[0, :, width:])
        shared = grad_gated * ctx[0]
        grad_ctx = (grad_gated * opened).astype(LOW)
        pulled = shared * opened
        scaled = query_in[0] * jnp.asarray(0.125, LOW)
        grad_kv[...] = jnp.zeros_like(grad_kv)
        for piece in range(blocks):
            part = slice(piece * block, (piece + 1) * block)
            keys = window.keys(piece)
            usable = lax.broadcasted_iota(jnp.int32, (block, seq_len), 1) < lengths[window.loc(piece)]
            for head in range(heads):
                lanes = slice(head * head_size, (head + 1) * head_size)
                later = slice(width + head * head_size, width + (head + 1) * head_size)
                key = kv[0, keys, lanes]
                scores = nt(scaled[part, lanes], key)
                chances = jnp.where(usable, jnp.exp(scores - lse[0, part, head : head + 1]), 0.0)
                grad_chances = nt(grad_ctx[part, lanes], kv[0, keys, later])
                delta = jnp.sum(pulled[part, lanes], -1, keepdims=True)
                grad_scores = (chances * (grad_chances - delta)).astype(LOW)
                grad_q[part, lanes] = nn(grad_scores, key) * 0.125
                grad_kv[keys, lanes] += tn(grad_scores, scaled[part, lanes])
                grad_kv[keys, later] += tn(chances.astype(LOW), grad_ctx[part, lanes])
                point(1 + piece * heads + head, ahead)
        query_low = grad_q[...].astype(LOW)
        kv_low = grad_kv[...].astype(LOW)
        q_all[step] = query_low
        kv_all[step] = kv_low
        head_vec[0, 0:1, :width] = jnp.sum(query_low.astype(F32), 0, keepdims=True)
        head_vec[0, 0:1, 2 * width :] = jnp.sum(kv_low.astype(F32), 0, keepdims=True)
        shared_sum = jnp.sum(shared, 0, keepdims=True)
        lane = lax.broadcasted_iota(jnp.int32, (1, 128), 1)
        by_head = jnp.zeros((1, 128), F32)
        for head in range(heads):
            one = jnp.sum(shared_sum[:, head * head_size : (head + 1) * head_size], 1, keepdims=True)
            by_head = jnp.where(lane == head, one, by_head)
        head_vec[0, 1:2, :128] = by_head

        @pl.when(step == 0)
        def _():
            spread[...] = jnp.zeros_like(spread)
            mine[...] = grad_before[...] if first else grad_before[...] + extra[0]

        spread[...] += nt(kv_low, left[0])
        mine[...] += nt(query_low, right[0, :, :width])
        point(1 + blocks * heads, ahead)

        @pl.when(step == groups - 1)
        def _():
            pair_low[...] = spread[window.at(window.pair, rows), :].astype(LOW)
            to_pair.start()

            @pl.when(window.middle)
            def _():
                mid_low[...] = spread[window.at(window.mid, mid_rows), :].astype(LOW)
                to_mid.start()

    @pl.when(step >= groups)
    def _():
        for spot in range(1 + blocks * heads):
            if spot % 3 == 0:
                point(spot, behind)
        r = step - groups
        left_out[0] = tn(xwin[window.at(offset, 2 * seq_len), :], kv_all[r]).astype(LOW)
        for spot in range(1 + blocks * heads):
            if spot % 3 == 1:
                point(spot, behind)
        right_out[0, :, :width] = tn(xwin[here, :], q_all[r]).astype(LOW)
        for spot in range(1 + blocks * heads):
            if spot % 3 == 2:
                point(spot, behind)
        right_out[0, :, width:] = tn(attn[...], gated[0]).astype(LOW)

        @pl.when(step == 2 * groups - 1)
        def _():
            to_pair.wait()
            mine[...] += spread[window.at(window.own, rows), :] + pair_got[...].astype(F32)

            @pl.when(window.middle)
            def _():
                to_mid.wait()
                mine[window.at(window.mid_row, mid_rows), :] += mid_got[...].astype(F32)

            grad_out[...] = mine[...].astype(grad_out.dtype)

        point(1 + blocks * heads, behind)


def on_device(
    ndp,
    groups,
    hidden_in,
    seq_lengths,
    layer_map,
    teacher_states,
    out_cotangent,
    query_weight,
    key_weight,
    value_weight,
    query_value_bias,
    output_weight,
    branch_bias,
    norm_gain,
    norm_shift,
    inner_weight,
    inner_bias,
    outer_weight,
    head_alpha,
    head_noise,
    unit_alpha,
    unit_noise,
    map_weight,
):
    tokens_dev, model = hidden_in.shape
    seqs_dev = seq_lengths.shape[0]
    seq_len = tokens_dev // seqs_dev
    width = query_weight.shape[2]
    units = inner_weight.shape[2]
    layers, heads = head_alpha.shape
    head_size = width // heads
    rows = tokens_dev // groups
    feats = model // ndp
    geo = Geometry(ndp, groups)
    size = (seqs_dev, seq_len, heads, head_size)
    window = Window(size, rows, groups)
    blocks = rows // window.block
    dp = lax.axis_index("dp")

    def slices(array):
        return array.reshape(array.shape[0], geo.size_y, geo.size_x, 2, feats, array.shape[-1])

    def matrices(arrays):
        return [(array.reshape(groups, model, array.shape[-1]), "group") for array in arrays]

    def pairs(cols, steps):
        out, begin = [], 0
        for step in steps:
            out.append([(0, begin, step, False), (1, begin, step, True)])
            begin += step
        return out if begin == cols else [[(0, 0, cols, False), (1, 0, cols, True)]]

    key_value = slices(jnp.concatenate([key_weight, value_weight], 2))
    query_output = slices(jnp.concatenate([query_weight, jnp.swapaxes(output_weight, 1, 2)], 2))
    inner, outer = slices(inner_weight), slices(outer_weight)

    def attn_gather(layer):
        return Gather(geo, [(key_value, layer), (query_output, layer)], pairs(2 * width, ATTN_CUTS))

    def feed_gather(layer):
        return Gather(geo, [(inner, layer), (outer, layer)], pairs(units, FEED_CUTS))

    open_unit, unit_back = jax.vjp(partial(gate_open, unit_noise), unit_alpha)
    open_head, head_back = jax.vjp(partial(gate_open, head_noise), head_alpha)
    (unit_slope,) = unit_back(jnp.ones_like(open_unit))
    (head_slope,) = head_back(jnp.ones_like(open_head))
    mixed = jnp.concatenate(
        [
            query_value_bias[:, 0],
            jnp.repeat(open_head, head_size, axis=1),
            jnp.zeros((layers, width), F32),
            query_value_bias[:, 1],
        ],
        1,
    )
    small = jnp.stack([open_unit, inner_bias, mixed, mixed], 1).reshape(4 * layers, units)
    vec = jnp.concatenate([branch_bias, norm_gain, norm_shift], 1).reshape(6 * layers, model)
    lengths = lax.dynamic_slice(seq_lengths, (window.first,), (2,))
    spot = jnp.arange(tokens_dev)
    row_ok = (spot % seq_len < jnp.repeat(seq_lengths, seq_len, total_repeat_length=tokens_dev)).astype(F32)
    row_ok = lax.dynamic_slice(row_ok, (window.h * rows,), (rows,))
    row_ok = jnp.broadcast_to(row_ok[:, None], (rows, 128))
    count = jnp.broadcast_to(jnp.sum(seq_lengths).astype(F32), (8, 128))
    chosen = jnp.take(teacher_states, layer_map, axis=0)

    *weights, small, counts = run(
        only_move,
        1,
        [],
        [],
        [],
        0,
        "gather_first",
        [attn_gather(0), Spread(geo, small, absolute=False), Spread(geo, count, plane=True)],
        1,
        1,
    )
    weights = matrices(weights)
    xwin, resid = hidden_in, None
    records, lows = [], []
    row_block = pltpu.VMEM((rows, model), F32)
    low_block = pltpu.VMEM((rows, model), LOW)
    mid_block = pltpu.VMEM((window.mid_rows, model), LOW)
    two = pltpu.SemaphoreType.DMA((2,))
    for layer in range(layers):
        ending = layer == layers - 1
        inputs = [(xwin, "full"), (small, "group"), (vec, "full"), (lengths, "smem")] + weights
        if layer:
            inputs.append((resid, "full"))
        attn_weights = weights
        kv, query, ctx, lse, gated, before_one, middle, middle_low, *got = run(
            partial(attention_forward, size, layer, layer == 0),
            groups,
            inputs,
            [
                ((groups, 2 * seq_len, 2 * width), LOW, "group"),
                ((groups, rows, width), LOW, "group"),
                ((groups, rows, width), F32, "group"),
                ((groups, rows, 128), F32, "group"),
                ((groups, rows, width), LOW, "group"),
                ((rows, model), F32, "full"),
                ((rows, model), F32, "full"),
                ((rows, model), LOW, "full"),
            ],
            [row_block],
            8e9,
            "attention_forward",
            [feed_gather(layer)],
            2 + blocks * heads,
            2 + 2 * layer,
        )
        feed_weights = matrices(got)
        outputs = [
            ((groups, rows, units), LOW, "group"),
            ((rows, model), F32, "full"),
            ((rows, model), F32, "full"),
            ((rows, model), LOW, "full"),
        ]
        scratch = [row_block]
        if ending:
            riders = [Gather(geo, [(slices(map_weight[None]), 0)], [[(0, 0, width, False)]]), Deal(geo, chosen)]
        else:
            riders = [attn_gather(layer + 1)]
            outputs.append(((2 * seq_len, model), LOW, "any"))
            scratch += [low_block, mid_block, two, two, two]
        unit_in, before_two, resid, low, *got = run(
            partial(feed_forward, size, layer, not ending),
            groups,
            [(middle, "full"), (middle_low, "full"), (small, "group"), (vec, "full")] + feed_weights,
            outputs,
            scratch,
            5e9,
            "feed_forward",
            riders,
            4,
            3 + 2 * layer,
        )
        records.append(
            (xwin, kv, query, ctx, lse, gated, before_one, middle_low, unit_in, before_two, attn_weights, feed_weights)
        )
        lows.append(low)
        if not ending:
            xwin, *got = got
            weights = matrices(got)
    weights, target = matrices(got[:1]), got[1]
    spread, loss, grad_map = run(
        partial(match_teacher, layers, float(tokens_dev * ndp)),
        groups,
        [(low, "full") for low in lows]
        + [(target, lambda r: jnp.maximum(r - 1, 0)), (chosen, "full"), (row_ok, "full"), (counts, "full")]
        + weights,
        [
            ((layers, rows, model), F32, "full"),
            ((8, 128), F32, "full"),
            ((groups, model, width), LOW, "group"),
        ],
        [],
        4e9,
        "match_teacher",
    )

    def parts(grad):
        return slices(grad)

    grads = [(out_cotangent, "full"), (spread[layers - 1 :], "full")]
    results = [{} for _ in range(layers)]
    riders, waiting = [Spread(geo, lows[-1])], [(0, "block_out")]
    number = 2 + 2 * layers

    def settle(got):
        for (layer, name), value in zip(waiting, got):
            results[layer][name] = value

    early, late = (lambda s: jnp.minimum(s, groups - 1)), (lambda s: jnp.maximum(s - groups, 0))
    for layer in reversed(range(layers)):
        xwin, kv, query, ctx, lse, gated, before_one, middle_low, unit_in, before_two, attn_weights, feed_weights = records[layer]
        inner_grad, outer_grad, attn, grad_before, vec_out, unit_vec, *got = run(
            partial(feed_backward, layer, layer == layers - 1),
            groups,
            [
                (before_two, "full"),
                (before_one, "full"),
                (middle_low, "full"),
                (unit_in, "group"),
                (small, "group"),
                (vec, "full"),
            ]
            + feed_weights
            + grads,
            [((groups, model, units), LOW, "group")] * 2
            + [
                ((rows, model), LOW, "full"),
                ((rows, model), F32, "full"),
                ((8, model), F32, "full"),
                ((groups, 8, units), F32, "group"),
            ],
            [row_block, low_block],
            10e9,
            "feed_backward",
            riders,
            7,
            number,
        )
        number += 1
        settle(got)
        riders = [Scatter(geo, [parts(inner_grad), parts(outer_grad)], pairs(units, BACK_CUTS))]
        waiting = [(layer, "inner"), (layer, "outer")]
        if layer == layers - 1:
            riders.append(Scatter(geo, [parts(grad_map)], [[(0, 0, width, False)]]))
            waiting.append((0, "map"))
        left, right, grad, head_vec, *got = run(
            partial(attention_backward, size, layer, layer == 0),
            2 * groups,
            [
                (attn, "full"),
                (grad_before, "full"),
                (xwin, "full"),
                (query, early),
                (kv, early),
                (ctx, early),
                (lse, early),
                (gated, late),
                (small, early),
                (lengths, "smem"),
            ]
            + [(array, early) for array, _ in attn_weights]
            + ([(spread[layer - 1 : layer], "full")] if layer else []),
            [((groups, model, 2 * width), LOW, late)] * 2
            + [
                ((rows, model), F32 if layer else LOW, "full"),
                ((groups, 8, units), F32, early),
            ],
            [
                pltpu.VMEM((2 * seq_len, 2 * width), F32),
                pltpu.VMEM((rows, width), F32),
                pltpu.VMEM((groups, 2 * seq_len, 2 * width), LOW),
                pltpu.VMEM((groups, rows, width), LOW),
                pltpu.VMEM((2 * seq_len, model), F32),
                row_block,
                low_block,
                low_block,
                mid_block,
                mid_block,
                two,
                two,
            ],
            12e9,
            "attention_backward",
            riders,
            2 + blocks * heads,
            number,
        )
        number += 1
        settle(got)
        riders = [Scatter(geo, [parts(left), parts(right)], pairs(2 * width, LAST_CUTS if layer == 0 else ATTN_CUTS))]
        waiting = [(layer, "kv"), (layer, "qo")]
        grads = [(grad, "full")]
        results[layer].update(vec=vec_out, unit=unit_vec, head=head_vec)

    everywhere = (0, feats, feats)
    unit_count, qv_cols = units // ndp, width // ndp
    items = [(results[layer]["vec"], False, (0, 6), everywhere) for layer in range(layers)]
    items += [(results[layer]["unit"], True, (0, 2), (0, unit_count, unit_count)) for layer in range(layers)]
    for layer in range(layers):
        items += [(results[layer]["head"], True, (0, 1), (0, qv_cols, qv_cols))]
        items += [(results[layer]["head"], True, (0, 1), (3 * width, qv_cols, qv_cols))]
    items += [(results[layer]["head"], True, (1, 2), (0, 0, 128)) for layer in range(layers)]
    items += [(loss, False, (0, 1), (0, 0, 128))]
    riders += [Fold(geo, items), Spread(geo, grad)]
    waiting += [(0, "sums"), (0, "grad_hidden")]
    settle(run(only_move, 1, [], [], [], 0, "scatter_last", riders, 1, number))
    sums = results[0]["sums"]
    by_feature = sums[: 6 * layers, :feats].reshape(layers, 3, 2, feats)
    by_unit = sums[6 * layers : 8 * layers, :unit_count].reshape(layers, 2, unit_count)
    by_column = sums[8 * layers : 10 * layers, :qv_cols].reshape(layers, 2, qv_cols)
    by_head = sums[10 * layers : 11 * layers, :heads]
    distill_loss = sums[11 * layers, 0] / (jnp.sum(counts[:, 0, 0]) * model * layers)
    own_slope = lax.dynamic_slice(unit_slope, (0, dp * unit_count), (layers, unit_count))

    def stacked(member, cols, turned=False):
        arrays = [results[layer][member][:, cols] for layer in range(layers)]
        return jnp.stack([array.T if turned else array for array in arrays])

    front, rear, whole = slice(0, width), slice(width, 2 * width), slice(None)
    return (
        results[0]["block_out"].reshape(tokens_dev, model),
        results[0]["grad_hidden"].reshape(tokens_dev, model).astype(F32),
        distill_loss,
        stacked("qo", front),
        stacked("kv", front),
        stacked("kv", rear),
        by_column,
        stacked("qo", rear, True),
        by_feature[:, 0],
        by_feature[:, 1],
        by_feature[:, 2],
        stacked("inner", whole),
        by_unit[:, 0],
        stacked("outer", whole, True),
        by_head * head_slope,
        by_unit[:, 1] * own_slope,
        results[0]["map"],
    )


def solution(mesh):
    in_specs = (
        P("dp", None),
        P("dp"),
        P(),
        P(None, "dp", "head"),
        P("dp", None),
        P(None, None, "head"),
        P(None, None, "head"),
        P(None, None, "head"),
        P(None, None, "head"),
        P(None, "head", None),
        P(),
        P(),
        P(),
        P(None, None, "head"),
        P(None, "head"),
        P(None, "head", None),
        P(None, "head"),
        P(None, "head"),
        P(None, "head"),
        P(None, "head"),
        P(None, "head"),
    )
    out_specs = (
        P("dp", None),
        P("dp", None),
        P(),
        P(None, "dp", "head"),
        P(None, "dp", "head"),
        P(None, "dp", "head"),
        P(None, None, ("head", "dp")),
        P(None, "head", "dp"),
        P(None, None, "dp"),
        P(None, None, "dp"),
        P(None, None, "dp"),
        P(None, "dp", "head"),
        P(None, ("head", "dp")),
        P(None, "head", "dp"),
        P(None, "head"),
        P(None, ("head", "dp")),
        P("dp", "head"),
    )
    return jax.shard_map(
        partial(on_device, mesh.shape["dp"], mesh.shape["head"]),
        mesh=mesh,
        in_specs=in_specs,
        out_specs=out_specs,
        check_vma=False,
    )
```

time: 797 us -> 642 us (0.81)
  waiting for transfers between devices: 76.7 us -> 0 us
  starting transfers between devices: 58.2 us -> 0 us
  matrix products: 25.8 us -> 0 us
  Pallas kernels: 562 us -> 577 us
    ppermute x29 -> x0, waiting for transfers between devices: 76.7 us -> none  [the longest x12 44.1 us: pull_group(): lax.ppermute(value, 'head', [((i + r) % groups, i) for i in range(groups)])]
    ppermute x29 -> x0, starting transfers between devices: 58.2 us -> none  [the longest x12 25 us: pull_group(): lax.ppermute(value, 'head', [((i + r) % groups, i) for i in range(groups)])]
    dot_general x13 -> x0, matrix products: 25.8 us -> none  [product(): lax.dot_general(left, right, ((dims[:1], dims[1:]), ((), ())), preferred_...]
    pallas_call x13 -> x11, Pallas kernels: 562 us -> 577 us  [run(): pl.pallas_call(whole, name=name, grid=(steps,), in_specs=[spec_of(a, kind...]
  transfers between devices with their start and end apart: 29 -> 0, of which waited for: 9 -> 0; matrix products, arithmetic and copies ran while one was open for 9% -> 0% of each run, Pallas kernels for 44% -> 0%
where the time goes in v3:
time: 642 us; the launch traced here: 633 us
  Pallas kernels  577 us (90%)
  local copies, waits for them, and re-layouts  25.8 us (4%)
  other arithmetic  25.6 us (4%)
    pallas_call x11, Pallas kernels, run(): pl.pallas_call(whole, name=name, grid=(steps,), in_specs=[spec_of(a, kind...  577 us

profile of v3, /device:TPU:0, one launch (start us, length us, event | category | flops | bytes accessed | tf_op | source)
XLA Modules:
  0.0 632.8 jit_solution(7159510221426332658)
XLA Ops:
  0.7 1.4 reduce_sum.18
  2.8 1.2 dynamic_slice.9.refs_3_.refs_9_
  4.0 1.2 compare_and_fusion
  5.2 0.7 compare_select_fusion
  5.9 1.4 fusion.19
  7.2 2.7 fusion.4
  9.9 1.3 fusion.15
  12.6 0.8 fusion.17
  13.4 1.3 broadcast_compare_fusion.1
  15.9 0.7 pad_maximum_fusion.9
  17.3 0.8 pad_maximum_fusion.8
  18.7 0.8 broadcast_in_dim.39.refs_4_
  19.5 1.9 copy.55
  21.3 0.7 gather_fusion
  22.1 0.7 copy.56
  22.8 1.4 broadcast_select_fusion.refs_7_.refs_3_
  24.3 1.4 copy.51
  25.8 1.4 copy.50
  27.2 39.0 %gather_first.1 = (bf16[4,2,2,2,96,384]{5,4,3,2,1,0:T(8,128)(2,1)}, bf16[4,2,2,2,96,384]{5,4,3,2,1,0:T(8,128)(2,1)}, f32[4,8,768]{2,1,0:T(8,128)}, f32[8,8,128]{2,1,0:T(8,128)}) custom-call(bf16[2,2,2,2,96,384]{5,4,3,2,1,0:T(8,128)(2,1)} %bitcast.91, bf16[2,2,2,2,96,384]{5,4,3,2,1,0:T(8,128)(2,1)} %bitcast.89, f32[8,768]{1,0:T(8,128)} %reshape.205.refs_2_, ...), custom_call_target="tpu_custom_call" | custom-call | bytes 28672 | tf_op jit(solution)/shard_map/gather_first/pallas_call | solution.py:114
  66.2 1.4 slice_reduce_fusion
  68.2 55.6 %attention_forward.2 = (bf16[4,1024,384]{2,1,0:T(8,128)(2,1)}, bf16[4,384,192]{2,1,0:T(8,128)(2,1)}, f32[4,384,192]{2,1,0:T(8,128)}, f32[4,384,128]{2,1,0:T(8,12...) custom-call(bf16[1536,768]{1,0:T(8,128)(2,1)} %refs_2_.1, ...), custom_call_target="tpu_custom_call" | custom-call | flops 8000000000 | bytes 7213064 | tf_op jit(solution)/shard_map/attention_forward/pallas_call | solution.py:114
  123.9 47.6 %feed_forward.2 = (bf16[4,384,768]{2,1,0:T(8,128)(2,1)}, f32[384,768]{1,0:T(8,128)}, f32[384,768]{1,0:T(8,128)}, bf16[384,768]{1,0:T(8,128)(2,1)}, bf16[1024,768...) custom-call(f32[384,768]{1,0:T(8,128)} %get-tuple-element.103.refs_0_, ...), custom_call_target="tpu_custom_call" | custom-call | flops 5000000000 | bytes 11341824 | tf_op jit(solution)/shard_map/feed_forward/pallas_call | solution.py:114
  171.5 54.7 %attention_forward.3 = (bf16[4,1024,384]{2,1,0:T(8,128)(2,1)}, bf16[4,384,192]{2,1,0:T(8,128)(2,1)}, f32[4,384,192]{2,1,0:T(8,128)}, f32[4,384,128]{2,1,0:T(8,12...) custom-call(bf16[1024,768]{1,0:T(8,128)(2,1)} %get-tuple-element.107, ...), custom_call_target="tpu_custom_call" | custom-call | flops 8000000000 | bytes 7606280 | tf_op jit(solution)/shard_map/attention_forward/pallas_call | solution.py:114
  226.2 47.2 %feed_forward.3 = (bf16[4,384,768]{2,1,0:T(8,128)(2,1)}, f32[384,768]{1,0:T(8,128)}, f32[384,768]{1,0:T(8,128)}, bf16[384,768]{1,0:T(8,128)(2,1)}, bf16[4,2,2,2,...) custom-call(f32[384,768]{1,0:T(8,128)} %get-tuple-element.111.refs_0_, ...), custom_call_target="tpu_custom_call" | custom-call | flops 5000000000 | bytes 11341824 | tf_op jit(solution)/shard_map/feed_forward/pallas_call | solution.py:114
  273.4 9.6 %match_teacher.1 = (f32[2,384,768]{2,1,0:T(8,128)}, f32[8,128]{1,0:T(8,128)}, bf16[4,768,192]{2,1,0:T(8,128)(2,1)}) custom-call(bf16[384,768]{1,0:T(8,128)(2,1)} %get-tuple-element.118.refs_0_, bf16[384,768]{1,0:T(8,128)(2,1)} %get-tuple-element.119.refs_1_.refs_10_, bf16[3,2,384,192]{3,2,1,0:T(8,128)(2,1)} %get-tuple-element.120.refs_2_, ...), custom_call_target="tpu_custom_call" | custom-call | flops 4000000000 | bytes 4653056 | tf_op jit(solution)/shard_map/match_teacher/pallas_call | solution.py:114
  282.9 3.2 fusion.16
  286.2 59.2 %feed_backward.2 = (bf16[4,768,768]{2,1,0:T(8,128)(2,1)}, bf16[4,768,768]{2,1,0:T(8,128)(2,1)}, bf16[384,768]{1,0:T(8,128)(2,1)}, f32[384,768]{1,0:T(8,128)}, f3...) custom-call(f32[384,768]{1,0:T(8,128)} %get-tuple-element.115.refs_0_, ...), custom_call_target="tpu_custom_call" | custom-call | flops 10000000000 | bytes 19009536 | tf_op jit(solution)/shard_map/feed_backward/pallas_call | solution.py:114
  345.4 77.1 %attention_backward.2 = (bf16[4,768,384]{2,1,0:T(8,128)(2,1)}, bf16[4,768,384]{2,1,0:T(8,128)(2,1)}, f32[384,768]{1,0:T(8,128)}, f32[4,8,768]{2,1,0:T(8,128)}, f...) custom-call(bf16[384,768]{1,0:T(8,128)(2,1)} %get-tuple-element.128.refs_0_, ...), custom_call_target="tpu_custom_call" | custom-call | flops 12000000000 | bytes 15630344 | tf_op jit(solution)/shard_map/attention_backward/pallas_call | solution.py:114
  422.5 44.8 %feed_backward.3 = (bf16[4,768,768]{2,1,0:T(8,128)(2,1)}, bf16[4,768,768]{2,1,0:T(8,128)(2,1)}, bf16[384,768]{1,0:T(8,128)(2,1)}, f32[384,768]{1,0:T(8,128)}, f3...) custom-call(f32[384,768]{1,0:T(8,128)} %get-tuple-element.125.refs_0_, ...), custom_call_target="tpu_custom_call" | custom-call | flops 10000000000 | bytes 16060416 | tf_op jit(solution)/shard_map/feed_backward/pallas_call | solution.py:114
  467.3 71.2 %attention_backward.3 = (bf16[4,768,384]{2,1,0:T(8,128)(2,1)}, bf16[4,768,384]{2,1,0:T(8,128)(2,1)}, bf16[384,768]{1,0:T(8,128)(2,1)}, f32[4,8,768]{2,1,0:T(8,12...) custom-call(bf16[384,768]{1,0:T(8,128)(2,1)} %get-tuple-element.141.refs_0_, f32[384,768]{1,0:T(8,128)} %get-tuple-element.142.refs_1_, ...), custom_call_target="tpu_custom_call" | custom-call | flops 12000000000 | bytes 15237128 | tf_op jit(solution)/shard_map/attention_backward/pallas_call | solution.py:114
  538.5 70.9 %scatter_last.1 = (f32[96,384]{1,0:T(8,128)}, f32[96,384]{1,0:T(8,128)}, f32[24,128]{1,0:T(8,128)}, bf16[4,384,768]{2,1,0:T(8,128)(2,1)}) custom-call(bf16[4,2,2,2,96,384]{5,4,3,2,1,0:T(8,128)(2,1)} %bitcast.94, bf16[4,2,2,2,96,384]{5,4,3,2,1,0:T(8,128)(2,1)} %bitcast.95, f32[8,768]{1,0:T(8,128)} %get-tuple-element.152.refs_2_, ...), custom_call_target="tpu_custom_call" | custom-call | bytes 1429504 | tf_op jit(solution)/shard_map/scatter_last/pallas_call | solution.py:114
  609.4 1.3 slice.89
  611.4 1.3 fusion.7
  612.6 0.7 slice.104
  613.9 1.3 fusion.10
  615.2 1.3 slice.97
  616.5 0.7 slice.100
  617.8 1.1 slice_bitcast_fusion.1
  618.9 1.1 slice_bitcast_fusion.3
  620.1 0.8 copy.62
  620.9 0.7 pad_maximum_fusion.4
  621.7 0.7 pad_maximum_fusion.6
  622.3 0.7 pad_maximum_fusion.5
  623.0 0.9 pad_maximum_fusion.2
  623.9 0.9 pad_maximum_fusion.3
  624.8 4.4 bitcast_convert_fusion
  629.1 1.4 copy.74
  630.5 0.6 copy.75
  (53 shorter events, 5.5 us)
Async XLA Ops:
  0.7 20.7 %copy-start = (bf16[4,1536,192]{1,2,0:T(8,128)(2,1)S(1)}, bf16[4,1536,192]{1,2,0:T(8,128)(2,1)}, u32[]{:S(2)}) copy-start(bf16[4,1536,192]{1,2,0:T(8,128)(2,1)} %param.26) | copy-start | bytes 7077892
  22.1 0.7 copy-start.15
  22.1 2.1 copy-start.3
  22.8 1.4 copy-start.4
  24.2 1.5 copy-start.5
  24.2 1.5 copy-start.6
  538.5 72.9 %copy-start.14 = (f32[2,3]{1,0:T(2,128)S(1)}, f32[2,3]{1,0:T(2,128)}, u32[]{:S(2)}) copy-start(f32[2,3]{1,0:T(2,128)} %get-tuple-element.208) | copy-start | bytes 76
  538.5 81.4 %copy-start.12 = (f32[96,384]{1,0:T(8,128)S(1)}, f32[96,384]{1,0:T(8,128)}, u32[]{:S(2)}) copy-start(f32[96,384]{1,0:T(8,128)} %get-tuple-element.163) | copy-start | bytes 442372
  609.4 12.1 %copy-start.11 = (f32[96,384]{1,0:T(8,128)S(1)}, f32[96,384]{1,0:T(8,128)}, u32[]{:S(2)}) copy-start(f32[96,384]{1,0:T(8,128)} %get-tuple-element.165) | copy-start | bytes 442372
  609.4 13.6 %copy-start.8 = (f32[96,768]{1,0:T(8,128)S(1)}, f32[96,768]{1,0:T(8,128)}, u32[]{:S(2)}) copy-start(f32[96,768]{1,0:T(8,128)} %get-tuple-element.167) | copy-start | bytes 884740
  609.4 13.6 %copy-start.10 = (f32[96,768]{1,0:T(8,128)S(1)}, f32[96,768]{1,0:T(8,128)}, u32[]{:S(2)}) copy-start(f32[96,768]{1,0:T(8,128)} %get-tuple-element.166) | copy-start | bytes 884740
  617.8 6.1 copy-start.7
  617.8 6.1 copy-start.9
  624.8 4.4 copy-start.2
  624.8 6.4 %copy-start.1 = (bf16[4,1536,192]{1,2,0:T(8,128)(2,1)S(1)}, bf16[4,1536,192]{1,2,0:T(8,128)(2,1)}, u32[]{:S(2)}) copy-start(bf16[4,1536,192]{1,2,0:T(8,128)(2,1)} %param.26) | copy-start | bytes 7077892
  629.1 1.4 copy-start.13
